TPU v7x, 512 devices: a whole 4x8x8 slice. The times are simulated.
512 devices in a mesh: task: 8 (over y_lo, x), ctx: 64 (over y_hi, z, core).
Axes of the slice: x: 4, y: 8 (y_hi: 4, y_lo: 2; y = y_hi * 2 + y_lo), z: 8, core: 2. Of those that a mesh axis runs over, the one named last changes fastest.
Arguments:
- base_queries: bfloat16 [8, 8192, 2048], P('task', 'ctx'), may hold values from -48 to 48
- adapter_input: bfloat16 [8, 8192, 16], P('task', 'ctx'), may hold values from -6 to 6
- adapter_up_weight: bfloat16 [8, 16, 2048], P('task'), may hold values from -1.5 to 1.5
- projected_keys: bfloat16 [8, 8192, 512], P('task', 'ctx'), may hold values from -6 to 6
- projected_values: bfloat16 [8, 8192, 512], P('task', 'ctx'), may hold values from -6 to 6
- output_gradient: bfloat16 [8, 8192, 2048], P('task', 'ctx'), may hold values from -0.52734375 to 0.52734375
- segments: int32 [8, 8192], P('task', 'ctx'), may hold values from 0 to 20, never falling along the last dimension, each value on 1 to 768 neighbouring positions
- solution: float32 [8, 32768], P('task'), may hold values from -1.5 to 1.5
- residual: float32 [8, 32768], P('task'), may hold values from -1.5 to 1.5
- direction: float32 [8, 32768], P('task'), may hold values from -1.5 to 1.5
- damping: float32 [8], P('task'), may hold values from 2 to 8
Outputs:
- new_solution: float32 [8, 32768], P('task', 'ctx')
- new_residual: float32 [8, 32768], P('task', 'ctx')
- new_direction: float32 [8, 32768], P('task', 'ctx')
- meta_gradient: float32 [32768], P('ctx')
Inputs may be any that keep to these rules, and one draw needn't show every extreme that they name: `segments`: segment numbers never fall along a task's tokens; each document holds 1 to 768 tokens, and some document holds exactly 768.
All inputs are finite; a program needn't handle non-finite values.
Results may differ from a plain program's by a relative error of at most 0.0073.
Values may be sent and summed in bfloat16 or wider, within the bound.
No kernel may reach another device: no remote copies, remote signals or barrier semaphores. Data moves between devices by JAX's collectives and lax.ppermute only.
A program may use at most 64 MiB of HBM per device.

v0:
```python
import jax
import jax.numpy as jnp
from jax import lax
from jax.sharding import PartitionSpec as P

HEADS = 16
KV_HEADS = 4
HEAD_DIM = 128
ADAPTER_RANK = 16
SPAN = 6


def passed_along(value, axis, steps):
    count = lax.axis_size(axis)
    leading, last = (max(0, -steps), min(count, count - steps))
    return lax.ppermute(value, axis, [(source, source + steps) for source in range(leading, last)])


def cut_along(shard, dim, size):
    dims = shard.shape
    blocks = shard.reshape(*dims[:dim], size, dims[dim] // size, *dims[dim + 1 :])
    return jnp.moveaxis(blocks, dim, 0)


def summed_on_arrival(shard, axis, dim):
    size = lax.axis_size(axis)
    blocks = lax.all_to_all(cut_along(shard, dim, size), axis, 0, 0, tiled=True)
    return jnp.sum(blocks, axis=0)


def copy_for_each(shard, axis):
    size = lax.axis_size(axis)
    return lax.all_to_all(
        jnp.broadcast_to(shard[None], (size, *shard.shape)), axis, 0, 0, tiled=True
    )


def over_copies(shard, axis):
    return copy_for_each(shard, axis).sum(axis=0)


def packed_total(arrays, axis):
    ends = [0]
    for a in arrays:
        ends.append(ends[-1] + a.size)
    total = over_copies(jnp.concatenate([a.ravel() for a in arrays]), axis)
    return tuple((total[b:e].reshape(a.shape) for a, b, e in zip(arrays, ends, ends[1:])))


def attend(query_matrix, tangent_vectors, grads_in, key_window, value_window, allowed):
    per_group = HEADS // KV_HEADS
    score_scale = HEAD_DIM ** (-0.5)
    row_count = query_matrix.shape[0]
    head_parts = []
    for kv_index in range(KV_HEADS):
        low_col = kv_index * per_group * HEAD_DIM
        high_col = low_col + per_group * HEAD_DIM
        query_head = query_matrix[:, low_col:high_col].reshape(row_count, per_group, HEAD_DIM)
        tangent_head = tangent_vectors[:, low_col:high_col].reshape(row_count, per_group, HEAD_DIM)
        grad_head = grads_in[:, low_col:high_col].reshape(row_count, per_group, HEAD_DIM)
        key_head = key_window[:, kv_index * HEAD_DIM : (kv_index + 1) * HEAD_DIM]
        value_head = value_window[:, kv_index * HEAD_DIM : (kv_index + 1) * HEAD_DIM]
        scores = (
            jnp.einsum("tgd,kd->tgk", query_head, key_head, preferred_element_type=jnp.float32)
            * score_scale
        )
        slopes = (
            jnp.einsum("tgd,kd->tgk", tangent_head, key_head, preferred_element_type=jnp.float32)
            * score_scale
        )
        pulls = jnp.einsum("tgd,kd->tgk", grad_head, value_head, preferred_element_type=jnp.float32)
        key_mask = allowed[:, None, :]
        masked = jnp.where(key_mask, scores, -1e30)
        row_max = jnp.max(masked, axis=2, keepdims=True)
        exp_terms = jnp.exp(masked - row_max)
        probability = exp_terms / jnp.sum(exp_terms, axis=2, keepdims=True)
        mean_slope = jnp.sum(probability * slopes, axis=2, keepdims=True)
        mean_pull = jnp.sum(probability * pulls, axis=2, keepdims=True)
        centred = (slopes - mean_slope) * (pulls - mean_pull)
        covariance = jnp.sum(probability * centred, axis=2, keepdims=True)
        coef_rounded = (probability * (centred - covariance)).astype(jnp.bfloat16)
        head_rows = (
            jnp.einsum("tgk,kd->tgd", coef_rounded, key_head, preferred_element_type=jnp.float32)
            * score_scale
        )
        head_parts.append(head_rows.reshape(row_count, per_group * HEAD_DIM))
    return jnp.concatenate(head_parts, axis=1)


def per_device(
    base_queries,
    adapter_input,
    adapter_up_weight,
    projected_keys,
    projected_values,
    output_gradient,
    segments,
    solution,
    residual,
    direction,
    damping,
):
    tok_count = base_queries.shape[1]
    dev_index = lax.axis_index("ctx")
    adapter_rows = adapter_input[0]
    query_matrix = (
        base_queries[0].astype(jnp.float32)
        + jnp.dot(adapter_rows, adapter_up_weight[0], preferred_element_type=jnp.float32)
    ).astype(jnp.bfloat16)
    shift_matrix_fn = direction[0].reshape(ADAPTER_RANK, HEADS * HEAD_DIM)
    tangent_vectors = jnp.dot(
        adapter_rows.astype(jnp.float32), shift_matrix_fn, precision=lax.Precision.HIGHEST
    ).astype(jnp.bfloat16)
    own_block = (projected_keys[0], projected_values[0], segments[0])
    earlier = []
    for offset in range(1, SPAN + 1):
        earlier.append(passed_along((own_block[0], own_block[1], own_block[2]), "ctx", offset))
    ordered = earlier[::-1] + [own_block]
    key_window = jnp.concatenate([piece[0] for piece in ordered], axis=0)
    value_window = jnp.concatenate([piece[1] for piece in ordered], axis=0)
    seg_window = jnp.concatenate([piece[2] for piece in ordered], axis=0)
    window = (SPAN + 1) * tok_count
    key_place = dev_index * tok_count - SPAN * tok_count + jnp.arange(window, dtype=jnp.int32)
    query_place = dev_index * tok_count + jnp.arange(tok_count, dtype=jnp.int32)
    allowed = (
        (key_place[None, :] <= query_place[:, None])
        & (key_place[None, :] >= 0)
        & (seg_window[None, :] == segments[0][:, None])
    )
    curvature_product_rows = attend(
        query_matrix, tangent_vectors, output_gradient[0], key_window, value_window, allowed
    ).astype(jnp.bfloat16)
    curvature_product_term = jnp.dot(
        adapter_rows.T, curvature_product_rows, preferred_element_type=jnp.float32
    ).reshape(-1)
    damp_val = damping[0]
    dir_full = direction[0]
    res_full = residual[0]
    old_norm = jnp.sum(res_full * res_full)
    part_size = curvature_product_term.shape[0] // lax.axis_size("ctx")
    part_start = dev_index * part_size
    dir_part = lax.dynamic_slice_in_dim(dir_full, part_start, part_size, 0)
    sol_part = lax.dynamic_slice_in_dim(solution[0], part_start, part_size, 0)
    hvp_part = summed_on_arrival(curvature_product_term, "ctx", 0)
    res_part = lax.dynamic_slice_in_dim(res_full, part_start, part_size, 0)
    curved = dir_part + hvp_part / damp_val
    inner_sums = packed_total(
        (jnp.sum(dir_part * curved), jnp.sum(res_part * curved), jnp.sum(curved * curved)), "ctx"
    )
    step_len = old_norm / inner_sums[0]
    new_norm = old_norm - 2.0 * step_len * inner_sums[1] + step_len * step_len * inner_sums[2]
    ratio = new_norm / old_norm
    new_residual = res_part - step_len * curved
    new_direction = new_residual + ratio * dir_part
    new_solution = sol_part + step_len * dir_part
    meta_gradient = over_copies(new_solution, "task") / lax.axis_size("task")
    return (new_solution[None], new_residual[None], new_direction[None], meta_gradient)


def solution(mesh):
    in_specs = (
        P("task", "ctx", None),
        P("task", "ctx", None),
        P("task", None, None),
        P("task", "ctx", None),
        P("task", "ctx", None),
        P("task", "ctx", None),
        P("task", "ctx"),
        P("task", None),
        P("task", None),
        P("task", None),
        P("task"),
    )
    out_specs = (P("task", "ctx"), P("task", "ctx"), P("task", "ctx"), P("ctx"))
    return jax.shard_map(
        per_device, mesh=mesh, in_specs=in_specs, out_specs=out_specs, check_vma=False
    )
```

profile of v0, /device:TPU:1, one launch (start us, length us, event | category | flops | bytes accessed | tf_op | source)
XLA Modules:
  0.0 229.7 jit_solution(9621597738331853668)
XLA Ops:
  0.7 8.6 %collective-permute-start = (s32[128]{0:T(128)}, s32[128]{0:T(128)S(1)}, u32[]{:S(2)}, u32[]{:S(2)}) collective-permute-start(s32[128]{0:T(128)} %bitcast.344), channel_id=1, source_target_pairs={{0,6},{1,7},{2,8},{3,9},{4,10},{5,11},{6,12},{7,13},{8,14},{9,15},... | collective-permute-start | bytes 1544 | tf_op jit(solution)/shard_map/ppermute | solution.py:16
  9.2 7.9 %collective-permute-start.1 = (s32[128]{0:T(128)}, s32[128]{0:T(128)S(1)}, u32[]{:S(2)}, u32[]{:S(2)}) collective-permute-start(s32[128]{0:T(128)} %bitcast.345), channel_id=1, source_target_pairs={{0,5},{1,6},{2,7},{3,8},{4,9},{5,10},{6,11},{7,12},{8,13},{9,14},{... | collective-permute-start | bytes 1544 | tf_op jit(solution)/shard_map/ppermute | solution.py:16
  18.4 4.0 %collective-permute-start.3 = (s32[128]{0:T(128)}, s32[128]{0:T(128)S(1)}, u32[]{:S(2)}, u32[]{:S(2)}) collective-permute-start(s32[128]{0:T(128)} %bitcast.347), channel_id=1, source_target_pairs={{0,3},{1,4},{2,5},{3,6},{4,7},{5,8},{6,9},{7,10},{8,11},{9,12},{10... | collective-permute-start | bytes 1544 | tf_op jit(solution)/shard_map/ppermute | solution.py:16
  29.6 4.4 %collective-permute-start.5 = (s32[128]{0:T(128)S(1)}, s32[128]{0:T(128)S(1)}, u32[]{:S(2)}, u32[]{:S(2)}) collective-permute-start(s32[128]{0:T(128)S(1)} %bitcast.349), channel_id=1, source_target_pairs={{0,1},{1,2},{2,3},{3,4},{4,5},{5,6},{6,7},{7,8},{8,9},{9,10},{10,1... | collective-permute-start | bytes 1544 | tf_op jit(solution)/shard_map/ppermute | solution.py:16
  34.0 7.0 %collective-permute-start.6 = (bf16[128,512]{1,0:T(8,128)(2,1)S(1)}, bf16[128,512]{1,0:T(8,128)(2,1)S(1)}, u32[]{:S(2)}, u32[]{:S(2)}) collective-permute-start(bf16[128,512]{1,0:T(8,128)(2,1)S(1)} %bitcast.328), channel_id=1, source_target_pairs={{0,6},{1,7},{2,8},{3,9},{4,10},{5,11},{6,12},{7,13},{8,14},{9,15},... | collective-permute-start | bytes 393224 | tf_op jit(solution)/shard_map/ppermute | solution.py:16
  41.1 2.7 %collective-permute-start.7 = (bf16[128,512]{1,0:T(8,128)(2,1)S(1)}, bf16[128,512]{1,0:T(8,128)(2,1)S(1)}, u32[]{:S(2)}, u32[]{:S(2)}) collective-permute-start(bf16[128,512]{1,0:T(8,128)(2,1)S(1)} %bitcast.329), channel_id=1, source_target_pairs={{0,5},{1,6},{2,7},{3,8},{4,9},{5,10},{6,11},{7,12},{8,13},{9,14},{... | collective-permute-start | bytes 393224 | tf_op jit(solution)/shard_map/ppermute | solution.py:16
  43.8 3.1 %collective-permute-start.8 = (bf16[128,512]{1,0:T(8,128)(2,1)S(1)}, bf16[128,512]{1,0:T(8,128)(2,1)S(1)}, u32[]{:S(2)}, u32[]{:S(2)}) collective-permute-start(bf16[128,512]{1,0:T(8,128)(2,1)S(1)} %bitcast.330), channel_id=1, source_target_pairs={{0,4},{1,5},{2,6},{3,7},{4,8},{5,9},{6,10},{7,11},{8,12},{9,13},{1... | collective-permute-start | bytes 393224 | tf_op jit(solution)/shard_map/ppermute | solution.py:16
  46.9 7.6 %collective-permute-start.9 = (bf16[128,512]{1,0:T(8,128)(2,1)S(1)}, bf16[128,512]{1,0:T(8,128)(2,1)S(1)}, u32[]{:S(2)}, u32[]{:S(2)}) collective-permute-start(bf16[128,512]{1,0:T(8,128)(2,1)S(1)} %bitcast.331), channel_id=1, source_target_pairs={{0,3},{1,4},{2,5},{3,6},{4,7},{5,8},{6,9},{7,10},{8,11},{9,12},{10... | collective-permute-start | bytes 393224 | tf_op jit(solution)/shard_map/ppermute | solution.py:16
  54.5 3.1 %collective-permute-start.10 = (bf16[128,512]{1,0:T(8,128)(2,1)S(1)}, bf16[128,512]{1,0:T(8,128)(2,1)S(1)}, u32[]{:S(2)}, u32[]{:S(2)}) collective-permute-start(bf16[128,512]{1,0:T(8,128)(2,1)S(1)} %bitcast.332), channel_id=1, source_target_pairs={{0,2},{1,3},{2,4},{3,5},{4,6},{5,7},{6,8},{7,9},{8,10},{9,11},{10,... | collective-permute-start | bytes 393224 | tf_op jit(solution)/shard_map/ppermute | solution.py:16
  57.9 2.3 %collective-permute-start.11 = (bf16[128,512]{1,0:T(8,128)(2,1)S(1)}, bf16[128,512]{1,0:T(8,128)(2,1)S(1)}, u32[]{:S(2)}, u32[]{:S(2)}) collective-permute-start(bf16[128,512]{1,0:T(8,128)(2,1)S(1)} %bitcast.333), channel_id=1, source_target_pairs={{0,1},{1,2},{2,3},{3,4},{4,5},{5,6},{6,7},{7,8},{8,9},{9,10},{10,1... | collective-permute-start | bytes 393224 | tf_op jit(solution)/shard_map/ppermute | solution.py:16
  60.3 4.0 %collective-permute-start.12 = (bf16[128,512]{1,0:T(8,128)(2,1)S(1)}, bf16[128,512]{1,0:T(8,128)(2,1)S(1)}, u32[]{:S(2)}, u32[]{:S(2)}) collective-permute-start(bf16[128,512]{1,0:T(8,128)(2,1)S(1)} %bitcast.334), channel_id=1, source_target_pairs={{0,6},{1,7},{2,8},{3,9},{4,10},{5,11},{6,12},{7,13},{8,14},{9,15},... | collective-permute-start | bytes 393224 | tf_op jit(solution)/shard_map/ppermute | solution.py:16
  64.3 2.4 %collective-permute-start.13 = (bf16[128,512]{1,0:T(8,128)(2,1)S(1)}, bf16[128,512]{1,0:T(8,128)(2,1)S(1)}, u32[]{:S(2)}, u32[]{:S(2)}) collective-permute-start(bf16[128,512]{1,0:T(8,128)(2,1)S(1)} %bitcast.335), channel_id=1, source_target_pairs={{0,5},{1,6},{2,7},{3,8},{4,9},{5,10},{6,11},{7,12},{8,13},{9,14},{... | collective-permute-start | bytes 393224 | tf_op jit(solution)/shard_map/ppermute | solution.py:16
  66.7 5.6 %collective-permute-start.14 = (bf16[128,512]{1,0:T(8,128)(2,1)S(1)}, bf16[128,512]{1,0:T(8,128)(2,1)S(1)}, u32[]{:S(2)}, u32[]{:S(2)}) collective-permute-start(bf16[128,512]{1,0:T(8,128)(2,1)S(1)} %bitcast.336), channel_id=1, source_target_pairs={{0,4},{1,5},{2,6},{3,7},{4,8},{5,9},{6,10},{7,11},{8,12},{9,13},{1... | collective-permute-start | bytes 393224 | tf_op jit(solution)/shard_map/ppermute | solution.py:16
  72.4 7.6 %collective-permute-start.15 = (bf16[128,512]{1,0:T(8,128)(2,1)S(1)}, bf16[128,512]{1,0:T(8,128)(2,1)S(1)}, u32[]{:S(2)}, u32[]{:S(2)}) collective-permute-start(bf16[128,512]{1,0:T(8,128)(2,1)S(1)} %bitcast.337), channel_id=1, source_target_pairs={{0,3},{1,4},{2,5},{3,6},{4,7},{5,8},{6,9},{7,10},{8,11},{9,12},{10... | collective-permute-start | bytes 393224 | tf_op jit(solution)/shard_map/ppermute | solution.py:16
  87.4 3.1 %fusion.228 = (f32[128,4]{0,1:T(4,128)S(1)}, f32[128,4,896]{2,0,1:T(8,128)}) fusion(pred[128,896]{1,0:T(8,128)(4,1)S(1)} %compare_and_fusion, bf16[16,4,8,128]{3,2,1,0:T(8,128)(2,1)S(1)} %copy-done.11, bf16[896,512]{1,0:T(8,128)(2,1)} %copy-done.14), kind=kOutput, calls=%fused_computation.230 | convolution fusion | flops 119276416 | bytes 2312192 | tf_op jit(solution)/shard_map/sub | solution.py:75
  102.4 3.4 %fusion.9 = f32[128,4,896]{2,0,1:T(8,128)} fusion(bf16[128,4,128]{0,2,1:T(8,128)(2,1)S(1)} %bitcast.327, bf16[896,512]{1,0:T(8,128)(2,1)S(1)} %constant_dynamic-update-slice_fusion.8, f32[128,4,896]{2,0,1:T(8,128)} %get-tuple-element.39, f32[128,4]{0,1:T(4,128)S(1)} %get-tuple-element.38), kind=kOutput, calls=%fused_computation.9 | convolution fusion | flops 118359424 | bytes 4032512 | tf_op jit(solution)/shard_map/sub | solution.py:79
  105.7 5.7 %multiply_reduce_fusion.6 = (f32[128,4]{0,1:T(4,128)S(1)}, f32[128,4,896]{2,0,1:T(8,128)}) fusion(f32[128,4,896]{2,0,1:T(8,128)} %get-tuple-element.39, f32[128,4]{0,1:T(4,128)S(1)} %get-tuple-element.38, f32[128,4,896]{2,0,1:T(8,128)} %fusion.9, f32[896,128,4]{0,1,2:T(8,128)} %fusion.75, bf16[16,4,8,128]{3,2,1,0:T(8,128)(2,1)} %get-tuple-element.10, ...), kind=kOutput, calls=%fused_computation.47 | convolution fusion | flops 239469440 | bytes 9902080 | tf_op jit(solution)/shard_map/sub | solution.py:79
  111.4 3.8 %fusion.37 = bf16[128,4,128]{0,2,1:T(8,128)(2,1)} fusion(f32[128,4,896]{2,0,1:T(8,128)} %get-tuple-element.41, f32[128,4]{0,1:T(4,128)S(1)} %get-tuple-element.40, bf16[896,512]{1,0:T(8,128)(2,1)} %copy-done.14, f32[128,4]{0,1:T(4,128)S(1)} %get-tuple-element.38, pred[128,896]{1,0:T(8,128)(4,1)} %copy-done.13, bf16[16,4,8,128]{3,2,1,0:T(8,128)(2,1)} %get-tuple-element.14), kind=kOutput, calls=%fused_computation.64 | convolution fusion | flops 238224768 | bytes 2674688 | tf_op jit(solution)/shard_map/tgk,kd->tgd/dot_general | solution.py:83
  115.3 3.4 %fusion.6 = f32[128,4,896]{2,0,1:T(8,128)} fusion(bf16[128,4,128]{0,2,1:T(8,128)(2,1)S(1)} %bitcast.325, bf16[896,512]{1,0:T(8,128)(2,1)S(1)} %constant_dynamic-update-slice_fusion.8, f32[128,4,896]{2,0,1:T(8,128)} %get-tuple-element.35, f32[128,4]{0,1:T(4,128)S(1)} %get-tuple-element.34), kind=kOutput, calls=%fused_computation.6 | convolution fusion | flops 118359424 | bytes 4032512 | tf_op jit(solution)/shard_map/sub | solution.py:79
  118.7 5.6 %multiply_reduce_fusion.4 = (f32[128,4]{0,1:T(4,128)S(1)}, f32[128,4,896]{2,0,1:T(8,128)}) fusion(f32[128,4,896]{2,0,1:T(8,128)} %get-tuple-element.35, f32[128,4]{0,1:T(4,128)S(1)} %get-tuple-element.34, f32[128,4,896]{2,0,1:T(8,128)} %fusion.6, f32[896,128,4]{0,1,2:T(8,128)} %fusion.74, bf16[16,4,8,128]{3,2,1,0:T(8,128)(2,1)S(1)} %copy-done.12, ...), kind=kOutput, calls=%fused_computation.41 | convolution fusion | flops 239469440 | bytes 9902080 | tf_op jit(solution)/shard_map/sub | solution.py:79
  124.3 3.2 %fusion.38 = bf16[128,4,128]{0,2,1:T(8,128)(2,1)S(1)} fusion(f32[128,4,896]{2,0,1:T(8,128)} %get-tuple-element.37, f32[128,4]{0,1:T(4,128)S(1)} %get-tuple-element.36, bf16[896,512]{1,0:T(8,128)(2,1)} %copy-done.14, f32[128,4]{0,1:T(4,128)S(1)} %get-tuple-element.34, pred[128,896]{1,0:T(8,128)(4,1)} %copy-done.13, bf16[16,4,8,128]{3,2,1,0:T(8,128)(2,1)} %get-tuple-element.17), kind=kOutput, calls=%fused_computation.65 | convolution fusion | flops 238224768 | bytes 2674688 | tf_op jit(solution)/shard_map/tgk,kd->tgd/dot_general | solution.py:83
  127.4 3.4 %fusion.3 = f32[128,4,896]{2,0,1:T(8,128)} fusion(bf16[128,4,128]{0,2,1:T(8,128)(2,1)S(1)} %bitcast.323, bf16[896,512]{1,0:T(8,128)(2,1)S(1)} %constant_dynamic-update-slice_fusion.8, f32[128,4,896]{2,0,1:T(8,128)} %get-tuple-element.31, f32[128,4]{0,1:T(4,128)S(1)} %get-tuple-element.30), kind=kOutput, calls=%fused_computation.3 | convolution fusion | flops 118359424 | bytes 4032512 | tf_op jit(solution)/shard_map/sub | solution.py:79
  130.8 5.8 %multiply_reduce_fusion.2 = (f32[128,4]{0,1:T(4,128)S(1)}, f32[128,4,896]{2,0,1:T(8,128)}) fusion(f32[128,4,896]{2,0,1:T(8,128)} %get-tuple-element.31, f32[128,4]{0,1:T(4,128)S(1)} %get-tuple-element.30, f32[128,4,896]{2,0,1:T(8,128)} %fusion.3, f32[896,128,4]{0,1,2:T(8,128)} %fusion.73, bf16[16,4,8,128]{3,2,1,0:T(8,128)(2,1)S(1)} %copy-done.10, ...), kind=kOutput, calls=%fused_computation.35 | convolution fusion | flops 239469440 | bytes 9902080 | tf_op jit(solution)/shard_map/sub | solution.py:79
  136.7 3.2 %fusion.39 = bf16[128,4,128]{0,2,1:T(8,128)(2,1)S(1)} fusion(f32[128,4,896]{2,0,1:T(8,128)} %get-tuple-element.33, f32[128,4]{0,1:T(4,128)S(1)} %get-tuple-element.32, bf16[896,512]{1,0:T(8,128)(2,1)} %copy-done.14, f32[128,4]{0,1:T(4,128)S(1)} %get-tuple-element.30, pred[128,896]{1,0:T(8,128)(4,1)} %copy-done.13, bf16[16,4,8,128]{3,2,1,0:T(8,128)(2,1)} %copy-done.7), kind=kOutput, calls=%fused_computation.66 | convolution fusion | flops 238224768 | bytes 2674688 | tf_op jit(solution)/shard_map/tgk,kd->tgd/dot_general | solution.py:83
  139.9 3.3 %fusion = f32[128,4,896]{2,0,1:T(8,128)} fusion(bf16[128,4,128]{0,2,1:T(8,128)(2,1)S(1)} %bitcast.321, bf16[896,512]{1,0:T(8,128)(2,1)S(1)} %constant_dynamic-update-slice_fusion.8, f32[128,4,896]{2,0,1:T(8,128)} %get-tuple-element.27, f32[128,4]{0,1:T(4,128)S(1)} %get-tuple-element.26), kind=kOutput, calls=%fused_computation | convolution fusion | flops 118359424 | bytes 4032512 | tf_op jit(solution)/shard_map/sub | solution.py:79
  143.2 5.1 %multiply_reduce_fusion = (f32[128,4]{0,1:T(4,128)S(1)}, f32[128,4,896]{2,0,1:T(8,128)}) fusion(f32[128,4,896]{2,0,1:T(8,128)} %get-tuple-element.27, f32[128,4]{0,1:T(4,128)S(1)} %get-tuple-element.26, f32[128,4,896]{2,0,1:T(8,128)} %fusion, f32[896,128,4]{0,1,2:T(8,128)S(1)} %fusion.72, bf16[16,4,8,128]{3,2,1,0:T(8,128)(2,1)S(1)} %copy-done.8, ...), kind=kOutput, calls=%fused_computation.29 | convolution fusion | flops 239469440 | bytes 9902080 | tf_op jit(solution)/shard_map/sub | solution.py:79
  148.3 3.2 %fusion.40 = bf16[128,4,128]{0,2,1:T(8,128)(2,1)S(1)} fusion(f32[128,4,896]{2,0,1:T(8,128)} %get-tuple-element.29, f32[128,4]{0,1:T(4,128)S(1)} %get-tuple-element.28, bf16[896,512]{1,0:T(8,128)(2,1)S(1)} %copy-done.16, f32[128,4]{0,1:T(4,128)S(1)} %get-tuple-element.26, pred[128,896]{1,0:T(8,128)(4,1)} %copy-done.13, bf16[16,4,8,128]{3,2,1,0:T(8,128)(2,1)} %copy-done.6), kind=kOutput, calls=%fused_computation.67 | convolution fusion | flops 238224768 | bytes 2674688 | tf_op jit(solution)/shard_map/tgk,kd->tgd/dot_general | solution.py:83
  152.5 29.1 %all-to-all-start = ((f32[64,1,512]{2,1,0:T(1,128)}), f32[64,1,512]{2,1,0:T(1,128)S(1)}, u32[]{:S(2)}, u32[]{:S(2)}) async-start(f32[64,1,512]{2,1,0:T(1,128)} %all_to_all.18), calls=%async_computation | async-start | bytes 262144 | tf_op jit(solution)/shard_map/all_to_all | solution.py:27
  182.3 12.0 %all-to-all-done = f32[64,1,512]{2,1,0:T(1,128)S(1)} async-done(((f32[64,1,512]{2,1,0:T(1,128)}), f32[64,1,512]{2,1,0:T(1,128)S(1)}, u32[]{:S(2)}, u32[]{:S(2)}) %all-to-all-start) | async-done | bytes 131104 | tf_op jit(solution)/shard_map/all_to_all | solution.py:27
  197.7 4.6 %all-to-all-start.1 = ((f32[64,1,3]{2,1,0:T(1,128)}), f32[64,1,3]{2,1,0:T(1,128)S(1)}, u32[]{:S(2)}, u32[]{:S(2)}) async-start(f32[64,1,3]{2,1,0:T(1,128)} %broadcast_in_dim.30), calls=%async_computation.1 | async-start | bytes 65536 | tf_op jit(solution)/shard_map/all_to_all | solution.py:33
  203.2 10.8 %all-to-all-done.1 = f32[64,1,3]{2,1,0:T(1,128)S(1)} async-done(((f32[64,1,3]{2,1,0:T(1,128)}), f32[64,1,3]{2,1,0:T(1,128)S(1)}, u32[]{:S(2)}, u32[]{:S(2)}) %all-to-all-start.1) | async-done | bytes 800 | tf_op jit(solution)/shard_map/all_to_all | solution.py:33
  219.9 9.1 %all_to_all.22 = f32[8,1,512]{2,1,0:T(1,128)S(1)} all-to-all(f32[8,1,512]{2,1,0:T(1,128)S(1)} %broadcast_in_dim.31), channel_id=1, replica_groups=mesh['task'=8,'ctx'=64] {'task'}, dimensions={0} | all-to-all | bytes 32768 | tf_op jit(solution)/shard_map/all_to_all | solution.py:33
  (120 shorter events, 35.6 us)
Async XLA Ops:
  0.6 23.5 %copy-start = (bf16[1,16,2048]{2,1,0:T(8,128)(2,1)S(1)}, bf16[1,16,2048]{2,1,0:T(8,128)(2,1)}, u32[]{:S(2)}) copy-start(bf16[1,16,2048]{2,1,0:T(8,128)(2,1)} %param.13) | copy-start | bytes 196612
  0.6 25.6 %copy-start.1 = (bf16[1,128,2048]{2,1,0:T(8,128)(2,1)S(1)}, bf16[1,128,2048]{2,1,0:T(8,128)(2,1)}, u32[]{:S(2)}) copy-start(bf16[1,128,2048]{2,1,0:T(8,128)(2,1)} %param.16) | copy-start | bytes 1572868
  0.7 28.9 %collective-permute-start = (s32[128]{0:T(128)}, s32[128]{0:T(128)S(1)}, u32[]{:S(2)}, u32[]{:S(2)}) collective-permute-start(s32[128]{0:T(128)} %bitcast.344), channel_id=1, source_target_pairs={{0,6},{1,7},{2,8},{3,9},{4,10},{5,11},{6,12},{7,13},{8,14},{9,15},... | collective-permute-start | bytes 1544 | tf_op jit(solution)/shard_map/ppermute | solution.py:16
  9.2 24.8 %collective-permute-start.1 = (s32[128]{0:T(128)}, s32[128]{0:T(128)S(1)}, u32[]{:S(2)}, u32[]{:S(2)}) collective-permute-start(s32[128]{0:T(128)} %bitcast.345), channel_id=1, source_target_pairs={{0,5},{1,6},{2,7},{3,8},{4,9},{5,10},{6,11},{7,12},{8,13},{9,14},{... | collective-permute-start | bytes 1544 | tf_op jit(solution)/shard_map/ppermute | solution.py:16
  17.1 24.0 %collective-permute-start.2 = (s32[128]{0:T(128)}, s32[128]{0:T(128)S(1)}, u32[]{:S(2)}, u32[]{:S(2)}) collective-permute-start(s32[128]{0:T(128)} %bitcast.346), channel_id=1, source_target_pairs={{0,4},{1,5},{2,6},{3,7},{4,8},{5,9},{6,10},{7,11},{8,12},{9,13},{1... | collective-permute-start | bytes 1544 | tf_op jit(solution)/shard_map/ppermute | solution.py:16
  18.4 25.4 %collective-permute-start.3 = (s32[128]{0:T(128)}, s32[128]{0:T(128)S(1)}, u32[]{:S(2)}, u32[]{:S(2)}) collective-permute-start(s32[128]{0:T(128)} %bitcast.347), channel_id=1, source_target_pairs={{0,3},{1,4},{2,5},{3,6},{4,7},{5,8},{6,9},{7,10},{8,11},{9,12},{10... | collective-permute-start | bytes 1544 | tf_op jit(solution)/shard_map/ppermute | solution.py:16
  22.4 24.5 %collective-permute-start.4 = (s32[128]{0:T(128)}, s32[128]{0:T(128)S(1)}, u32[]{:S(2)}, u32[]{:S(2)}) collective-permute-start(s32[128]{0:T(128)} %bitcast.348), channel_id=1, source_target_pairs={{0,2},{1,3},{2,4},{3,5},{4,6},{5,7},{6,8},{7,9},{8,10},{9,11},{10,... | collective-permute-start | bytes 1544 | tf_op jit(solution)/shard_map/ppermute | solution.py:16
  26.3 69.8 %copy-start.7 = (bf16[16,4,8,128]{3,2,1,0:T(8,128)(2,1)}, bf16[16,4,8,128]{3,2,1,0:T(8,128)(2,1)S(1)}, u32[]{:S(2)}) copy-start(bf16[16,4,8,128]{3,2,1,0:T(8,128)(2,1)S(1)} %get-tuple-element.16) | copy-start | bytes 393220
  26.3 73.6 %copy-start.6 = (bf16[16,4,8,128]{3,2,1,0:T(8,128)(2,1)}, bf16[16,4,8,128]{3,2,1,0:T(8,128)(2,1)S(1)}, u32[]{:S(2)}) copy-start(bf16[16,4,8,128]{3,2,1,0:T(8,128)(2,1)S(1)} %get-tuple-element.15) | copy-start | bytes 393220
  26.6 7.5 %copy-start.4 = (bf16[1,128,512]{2,1,0:T(8,128)(2,1)S(1)}, bf16[1,128,512]{2,1,0:T(8,128)(2,1)}, u32[]{:S(2)}) copy-start(bf16[1,128,512]{2,1,0:T(8,128)(2,1)} %param.14) | copy-start | bytes 393220
  26.6 33.7 %copy-start.5 = (bf16[1,128,512]{2,1,0:T(8,128)(2,1)S(1)}, bf16[1,128,512]{2,1,0:T(8,128)(2,1)}, u32[]{:S(2)}) copy-start(bf16[1,128,512]{2,1,0:T(8,128)(2,1)} %param.15) | copy-start | bytes 393220
  29.6 24.9 %collective-permute-start.5 = (s32[128]{0:T(128)S(1)}, s32[128]{0:T(128)S(1)}, u32[]{:S(2)}, u32[]{:S(2)}) collective-permute-start(s32[128]{0:T(128)S(1)} %bitcast.349), channel_id=1, source_target_pairs={{0,1},{1,2},{2,3},{3,4},{4,5},{5,6},{6,7},{7,8},{8,9},{9,10},{10,1... | collective-permute-start | bytes 1544 | tf_op jit(solution)/shard_map/ppermute | solution.py:16
  34.0 23.9 %collective-permute-start.6 = (bf16[128,512]{1,0:T(8,128)(2,1)S(1)}, bf16[128,512]{1,0:T(8,128)(2,1)S(1)}, u32[]{:S(2)}, u32[]{:S(2)}) collective-permute-start(bf16[128,512]{1,0:T(8,128)(2,1)S(1)} %bitcast.328), channel_id=1, source_target_pairs={{0,6},{1,7},{2,8},{3,9},{4,10},{5,11},{6,12},{7,13},{8,14},{9,15},... | collective-permute-start | bytes 393224 | tf_op jit(solution)/shard_map/ppermute | solution.py:16
  41.1 19.2 %collective-permute-start.7 = (bf16[128,512]{1,0:T(8,128)(2,1)S(1)}, bf16[128,512]{1,0:T(8,128)(2,1)S(1)}, u32[]{:S(2)}, u32[]{:S(2)}) collective-permute-start(bf16[128,512]{1,0:T(8,128)(2,1)S(1)} %bitcast.329), channel_id=1, source_target_pairs={{0,5},{1,6},{2,7},{3,8},{4,9},{5,10},{6,11},{7,12},{8,13},{9,14},{... | collective-permute-start | bytes 393224 | tf_op jit(solution)/shard_map/ppermute | solution.py:16
  43.8 20.6 %collective-permute-start.8 = (bf16[128,512]{1,0:T(8,128)(2,1)S(1)}, bf16[128,512]{1,0:T(8,128)(2,1)S(1)}, u32[]{:S(2)}, u32[]{:S(2)}) collective-permute-start(bf16[128,512]{1,0:T(8,128)(2,1)S(1)} %bitcast.330), channel_id=1, source_target_pairs={{0,4},{1,5},{2,6},{3,7},{4,8},{5,9},{6,10},{7,11},{8,12},{9,13},{1... | collective-permute-start | bytes 393224 | tf_op jit(solution)/shard_map/ppermute | solution.py:16
  46.9 19.8 %collective-permute-start.9 = (bf16[128,512]{1,0:T(8,128)(2,1)S(1)}, bf16[128,512]{1,0:T(8,128)(2,1)S(1)}, u32[]{:S(2)}, u32[]{:S(2)}) collective-permute-start(bf16[128,512]{1,0:T(8,128)(2,1)S(1)} %bitcast.331), channel_id=1, source_target_pairs={{0,3},{1,4},{2,5},{3,6},{4,7},{5,8},{6,9},{7,10},{8,11},{9,12},{10... | collective-permute-start | bytes 393224 | tf_op jit(solution)/shard_map/ppermute | solution.py:16
  54.5 17.8 %collective-permute-start.10 = (bf16[128,512]{1,0:T(8,128)(2,1)S(1)}, bf16[128,512]{1,0:T(8,128)(2,1)S(1)}, u32[]{:S(2)}, u32[]{:S(2)}) collective-permute-start(bf16[128,512]{1,0:T(8,128)(2,1)S(1)} %bitcast.332), channel_id=1, source_target_pairs={{0,2},{1,3},{2,4},{3,5},{4,6},{5,7},{6,8},{7,9},{8,10},{9,11},{10,... | collective-permute-start | bytes 393224 | tf_op jit(solution)/shard_map/ppermute | solution.py:16
  57.9 42.0 %copy-start.13 = (pred[128,896]{1,0:T(8,128)(4,1)}, pred[128,896]{1,0:T(8,128)(4,1)S(1)}, u32[]{:S(2)}) copy-start(pred[128,896]{1,0:T(8,128)(4,1)S(1)} %compare_and_fusion) | copy-start | bytes 344068
  57.9 29.5 %copy-start.11 = (bf16[16,4,8,128]{3,2,1,0:T(8,128)(2,1)S(1)}, bf16[16,4,8,128]{3,2,1,0:T(8,128)(2,1)}, u32[]{:S(2)}) copy-start(bf16[16,4,8,128]{3,2,1,0:T(8,128)(2,1)} %get-tuple-element.14) | copy-start | bytes 393220
  57.9 22.2 %collective-permute-start.11 = (bf16[128,512]{1,0:T(8,128)(2,1)S(1)}, bf16[128,512]{1,0:T(8,128)(2,1)S(1)}, u32[]{:S(2)}, u32[]{:S(2)}) collective-permute-start(bf16[128,512]{1,0:T(8,128)(2,1)S(1)} %bitcast.333), channel_id=1, source_target_pairs={{0,1},{1,2},{2,3},{3,4},{4,5},{5,6},{6,7},{7,8},{8,9},{9,10},{10,1... | collective-permute-start | bytes 393224 | tf_op jit(solution)/shard_map/ppermute | solution.py:16
  60.3 22.1 %collective-permute-start.12 = (bf16[128,512]{1,0:T(8,128)(2,1)S(1)}, bf16[128,512]{1,0:T(8,128)(2,1)S(1)}, u32[]{:S(2)}, u32[]{:S(2)}) collective-permute-start(bf16[128,512]{1,0:T(8,128)(2,1)S(1)} %bitcast.334), channel_id=1, source_target_pairs={{0,6},{1,7},{2,8},{3,9},{4,10},{5,11},{6,12},{7,13},{8,14},{9,15},... | collective-permute-start | bytes 393224 | tf_op jit(solution)/shard_map/ppermute | solution.py:16
  64.3 21.3 %collective-permute-start.13 = (bf16[128,512]{1,0:T(8,128)(2,1)S(1)}, bf16[128,512]{1,0:T(8,128)(2,1)S(1)}, u32[]{:S(2)}, u32[]{:S(2)}) collective-permute-start(bf16[128,512]{1,0:T(8,128)(2,1)S(1)} %bitcast.335), channel_id=1, source_target_pairs={{0,5},{1,6},{2,7},{3,8},{4,9},{5,10},{6,11},{7,12},{8,13},{9,14},{... | collective-permute-start | bytes 393224 | tf_op jit(solution)/shard_map/ppermute | solution.py:16
  66.7 18.9 %collective-permute-start.14 = (bf16[128,512]{1,0:T(8,128)(2,1)S(1)}, bf16[128,512]{1,0:T(8,128)(2,1)S(1)}, u32[]{:S(2)}, u32[]{:S(2)}) collective-permute-start(bf16[128,512]{1,0:T(8,128)(2,1)S(1)} %bitcast.336), channel_id=1, source_target_pairs={{0,4},{1,5},{2,6},{3,7},{4,8},{5,9},{6,10},{7,11},{8,12},{9,13},{1... | collective-permute-start | bytes 393224 | tf_op jit(solution)/shard_map/ppermute | solution.py:16
  72.4 13.3 %collective-permute-start.15 = (bf16[128,512]{1,0:T(8,128)(2,1)S(1)}, bf16[128,512]{1,0:T(8,128)(2,1)S(1)}, u32[]{:S(2)}, u32[]{:S(2)}) collective-permute-start(bf16[128,512]{1,0:T(8,128)(2,1)S(1)} %bitcast.337), channel_id=1, source_target_pairs={{0,3},{1,4},{2,5},{3,6},{4,7},{5,8},{6,9},{7,10},{8,11},{9,12},{10... | collective-permute-start | bytes 393224 | tf_op jit(solution)/shard_map/ppermute | solution.py:16
  80.1 5.6 %collective-permute-start.16 = (bf16[128,512]{1,0:T(8,128)(2,1)S(1)}, bf16[128,512]{1,0:T(8,128)(2,1)S(1)}, u32[]{:S(2)}, u32[]{:S(2)}) collective-permute-start(bf16[128,512]{1,0:T(8,128)(2,1)S(1)} %bitcast.338), channel_id=1, source_target_pairs={{0,2},{1,3},{2,4},{3,5},{4,6},{5,7},{6,8},{7,9},{8,10},{9,11},{10,... | collective-permute-start | bytes 393224 | tf_op jit(solution)/shard_map/ppermute | solution.py:16
  83.3 4.0 %collective-permute-start.17 = (bf16[128,512]{1,0:T(8,128)(2,1)S(1)}, bf16[128,512]{1,0:T(8,128)(2,1)S(1)}, u32[]{:S(2)}, u32[]{:S(2)}) collective-permute-start(bf16[128,512]{1,0:T(8,128)(2,1)S(1)} %bitcast.339), channel_id=1, source_target_pairs={{0,1},{1,2},{2,3},{3,4},{4,5},{5,6},{6,7},{7,8},{8,9},{9,10},{10,1... | collective-permute-start | bytes 393224 | tf_op jit(solution)/shard_map/ppermute | solution.py:16
  127.4 3.4 %copy-start.10 = (bf16[16,4,8,128]{3,2,1,0:T(8,128)(2,1)S(1)}, bf16[16,4,8,128]{3,2,1,0:T(8,128)(2,1)}, u32[]{:S(2)}) copy-start(bf16[16,4,8,128]{3,2,1,0:T(8,128)(2,1)} %get-tuple-element.12) | copy-start | bytes 393220
  143.2 5.1 %copy-start.16 = (bf16[896,512]{1,0:T(8,128)(2,1)S(1)}, bf16[896,512]{1,0:T(8,128)(2,1)}, u32[]{:S(2)}) copy-start(bf16[896,512]{1,0:T(8,128)(2,1)} %copy-done.14) | copy-start | bytes 2752516
  151.5 30.8 %copy-start.3 = (f32[1,32768]{1,0:T(1,128)S(1)}, f32[1,32768]{1,0:T(1,128)}, u32[]{:S(2)}) copy-start(f32[1,32768]{1,0:T(1,128)} %param.19) | copy-start | bytes 393220
  152.5 41.8 %all-to-all-start = ((f32[64,1,512]{2,1,0:T(1,128)}), f32[64,1,512]{2,1,0:T(1,128)S(1)}, u32[]{:S(2)}, u32[]{:S(2)}) async-start(f32[64,1,512]{2,1,0:T(1,128)} %all_to_all.18), calls=%async_computation | async-start | bytes 262144 | tf_op jit(solution)/shard_map/all_to_all | solution.py:27
  197.7 16.2 %all-to-all-start.1 = ((f32[64,1,3]{2,1,0:T(1,128)}), f32[64,1,3]{2,1,0:T(1,128)S(1)}, u32[]{:S(2)}, u32[]{:S(2)}) async-start(f32[64,1,3]{2,1,0:T(1,128)} %broadcast_in_dim.30), calls=%async_computation.1 | async-start | bytes 65536 | tf_op jit(solution)/shard_map/all_to_all | solution.py:33
  219.9 9.8 %copy-start.18 = (f32[1,512]{1,0:T(1,128)}, f32[1,512]{1,0:T(1,128)S(1)}, u32[]{:S(2)}) copy-start(f32[1,512]{1,0:T(1,128)S(1)} %get-tuple-element.22) | copy-start | bytes 6148
  (9 other events, 24.4 us)
where the time goes:
time: 231 us; the launch traced here: 230 us
  starting transfers between devices  111 us (48%)
  matrix products  66.2 us (29%)
  waiting for transfers between devices  24.5 us (11%)
  blocking collectives  9.13 us (4%)
  other arithmetic  6.74 us (3%)
  between operations  6.01 us (3%)
  local copies, waits for them, and re-layouts  5.64 us (2%)
    ppermute x18, starting transfers between devices, passed_along(): lax.ppermute(value, axis, [(source, source + steps) for source in range(l...  77.8 us
    sub x8, matrix products, attend(): centred = (slopes - mean_slope) * (pulls - mean_pull)  35.7 us
    all_to_all x1, starting transfers between devices, summed_on_arrival(): blocks = lax.all_to_all(cut_along(shard, dim, size), axis, 0, 0, tiled=True)  29.1 us
    dot_general x4, matrix products, attend(): jnp.einsum('tgk,kd->tgd', coef_rounded, key_head, preferred_element_type=...  13.3 us
    all_to_all x1, waiting for transfers between devices, summed_on_arrival(): blocks = lax.all_to_all(cut_along(shard, dim, size), axis, 0, 0, tiled=True)  12 us
    all_to_all x1, waiting for transfers between devices, copy_for_each(): lax.all_to_all(jnp.broadcast_to(shard[None], (size, *shard.shape)), axis,...  10.8 us
    sub x4, matrix products, attend(): exp_terms = jnp.exp(masked - row_max)  9.37 us
    all_to_all x1, blocking collectives, copy_for_each(): lax.all_to_all(jnp.broadcast_to(shard[None], (size, *shard.shape)), axis,...  9.13 us
  transfers between devices with their start and end apart: 20, of which 3 were waited for; matrix products, arithmetic and copies ran while one was open for 3% of the time, Pallas kernels for 0%

commit v1 on v0

v1 whole, which is shorter than its diff:
```python
import math

import jax
import jax.numpy as jnp
from jax import lax
from jax.experimental import pallas as pl
from jax.experimental.pallas import tpu as pltpu
from jax.sharding import Mesh
from jax.sharding import PartitionSpec as P

HEAD_DIM = 128
RANK = 16
BLOCK = 128
CHUNK = 2 * BLOCK
SPAN = 3
WINDOW = 7 * BLOCK
GROUPS = 2
PER_GROUP = 4
HALF = GROUPS * PER_GROUP * HEAD_DIM
KHALF = GROUPS * HEAD_DIM
GFEAT = PER_GROUP * HEAD_DIM
SEG_ROWS = 16
F32 = jnp.float32
BF16 = jnp.bfloat16
CTX = ("yh", "z", "core")
NT = (((1,), (1,)), ((), ()))
NN = (((1,), (0,)), ((), ()))


def dot(a, b, dims=NN):
    return lax.dot_general(a, b, dims, preferred_element_type=F32)


def fold(x):
    return x.reshape(x.shape[0] // 8, 8, x.shape[1])


def attend_kernel(
    qg, c0, c1, c2, c3, up, dmat, rmat, out, keys, keys_t, vals, bias, qs, ts, at, s_ref, t_ref, u_ref, c_ref
):
    chunks = (c0, c1, c2, c3)
    a_pad = qg[:, 2 * HALF : 2 * HALF + 128]
    a = a_pad[:, :RANK]
    qs[...] = (qg[:, :HALF].astype(F32) + dot(a, up[...])).astype(BF16)
    d = dmat[...]
    d1 = d.astype(BF16)
    rest = d - d1.astype(F32)
    d2 = rest.astype(BF16)
    d3 = (rest - d2.astype(F32)).astype(BF16)
    ts[...] = (dot(a, d1) + dot(a, d2) + dot(a, d3)).astype(BF16)
    at[...] = jnp.transpose(a_pad.astype(F32))[:RANK].astype(BF16)
    for j, c in enumerate(chunks):
        rows = slice(j * CHUNK, (j + 1) * CHUNK)
        for g in range(GROUPS):
            k = c[:CHUNK, g * HEAD_DIM : (g + 1) * HEAD_DIM]
            keys[g, rows, :] = k
            keys_t[g, :, rows] = jnp.transpose(k.astype(F32)).astype(BF16)
            vals[g, rows, :] = c[:CHUNK, KHALF + g * HEAD_DIM : KHALF + (g + 1) * HEAD_DIM]
    seg_rows = [c[CHUNK : CHUNK + SEG_ROWS, :CHUNK].astype(F32)[0:1] for c in chunks]
    tri = lax.broadcasted_iota(jnp.int32, (BLOCK, BLOCK), 0) <= lax.broadcasted_iota(jnp.int32, (BLOCK, BLOCK), 1)
    key_seg = []
    for kb in range(8):
        row = seg_rows[kb // 2][:, (kb % 2) * BLOCK : (kb % 2 + 1) * BLOCK]
        key_seg.append(jnp.transpose(jnp.broadcast_to(row, (BLOCK, BLOCK))))
    for b in range(2):
        query_seg = jnp.broadcast_to(seg_rows[3][:, b * BLOCK : (b + 1) * BLOCK], (BLOCK, BLOCK))
        for w in range(7):
            ok = key_seg[w + b] == query_seg
            if w == 6:
                ok = ok & tri
            bias[b, w * BLOCK : (w + 1) * BLOCK, :] = jnp.where(ok, 0.0, -1e30)
    out[...] = jnp.zeros_like(out)
    cexp = HEAD_DIM**-0.5 * math.log2(math.e)

    def step(i, carry):
        g, b = i // 2, i % 2
        off = pl.multiple_of(b * BLOCK, BLOCK)
        kw = keys[g, pl.ds(off, WINDOW), :]
        vw = vals[g, pl.ds(off, WINDOW), :]
        ktw = keys_t[g, :, pl.ds(off, WINDOW)]
        for pair in range(2):

            def two(ref, base):
                parts = []
                for e in range(2):
                    col = pl.multiple_of(base + g * GFEAT + (pair * 2 + e) * HEAD_DIM, HEAD_DIM)
                    parts.append(ref[pl.ds(off, BLOCK), pl.ds(col, HEAD_DIM)])
                return jnp.concatenate(parts, axis=0)

            s_ref[pair] = dot(kw, two(qs, 0), NT)
            t_ref[pair] = dot(kw, two(ts, 0), NT)
            u_ref[pair] = dot(vw, two(qg, HALF), NT)
        for pair in range(2):
            scales = []
            for e in range(2):
                lanes = slice(e * BLOCK, (e + 1) * BLOCK)
                m8 = jnp.full((8, BLOCK), -3e38, F32)
                for w in range(7):
                    rows = slice(w * BLOCK, (w + 1) * BLOCK)
                    m8 = jnp.maximum(m8, jnp.max(fold(s_ref[pair, rows, lanes] + bias[b, rows, :]), axis=0))
                m = jnp.max(m8, axis=0, keepdims=True)
                z8 = et8 = eu8 = etu8 = jnp.zeros((8, BLOCK), F32)
                for w in range(7):
                    rows = slice(w * BLOCK, (w + 1) * BLOCK)
                    ex = jnp.exp2((s_ref[pair, rows, lanes] + bias[b, rows, :] - m) * cexp)
                    s_ref[pair, rows, lanes] = ex
                    et = ex * t_ref[pair, rows, lanes]
                    u = u_ref[pair, rows, lanes]
                    z8 = z8 + jnp.sum(fold(ex), axis=0)
                    et8 = et8 + jnp.sum(fold(et), axis=0)
                    eu8 = eu8 + jnp.sum(fold(ex * u), axis=0)
                    etu8 = etu8 + jnp.sum(fold(et * u), axis=0)
                inv = 1.0 / jnp.sum(z8, axis=0, keepdims=True)
                mt = jnp.sum(et8, axis=0, keepdims=True) * inv
                mu = jnp.sum(eu8, axis=0, keepdims=True) * inv
                cov = jnp.sum(etu8, axis=0, keepdims=True) * inv - mt * mu
                for w in range(7):
                    rows = slice(w * BLOCK, (w + 1) * BLOCK)
                    coef = s_ref[pair, rows, lanes] * (
                        (t_ref[pair, rows, lanes] - mt) * (u_ref[pair, rows, lanes] - mu) - cov
                    )
                    c_ref[pair, rows, lanes] = coef.astype(BF16)
                scales.append(inv * (1.0 / HEAD_DIM))
            hv = dot(ktw, c_ref[pair])
            ab = at[:, pl.ds(off, BLOCK)]
            for e in range(2):
                lanes = slice(e * BLOCK, (e + 1) * BLOCK)
                head = (hv[:, lanes] * scales[e]).astype(BF16)
                cols = slice((pair * 2 + e) * HEAD_DIM, (pair * 2 + e + 1) * HEAD_DIM)
                out[g, :, cols] += dot(ab, head, NT)
        return carry

    lax.fori_loop(0, 4, step, 0)
    dh = rh = jnp.zeros((1, 1), F32)
    for g in range(GROUPS):
        h = out[g, :, :GFEAT]
        cols = slice(g * GFEAT, (g + 1) * GFEAT)
        dh = dh + jnp.sum(h * d[:, cols], keepdims=True)
        rh = rh + jnp.sum(h * rmat[:, cols], keepdims=True)
    lane = lax.broadcasted_iota(jnp.int32, (RANK, 128), 1)
    tail = jnp.where(lane == 0, dh, jnp.where(lane == 1, rh, 0.0))
    for g in range(GROUPS):
        out[g, :, GFEAT:] = tail


def attend(qg, chunks, up, dmat, rmat):
    vm = pltpu.VMEM
    return pl.pallas_call(
        attend_kernel,
        out_shape=jax.ShapeDtypeStruct((GROUPS, RANK, GFEAT + 128), F32),
        in_specs=[pl.BlockSpec(memory_space=vm)] * 8,
        out_specs=pl.BlockSpec(memory_space=vm),
        scratch_shapes=[
            vm((GROUPS, 4 * CHUNK, HEAD_DIM), BF16),
            vm((GROUPS, HEAD_DIM, 4 * CHUNK), BF16),
            vm((GROUPS, 4 * CHUNK, HEAD_DIM), BF16),
            vm((2, WINDOW, BLOCK), F32),
            vm((CHUNK, HALF), BF16),
            vm((CHUNK, HALF), BF16),
            vm((RANK, CHUNK), BF16),
            vm((2, WINDOW, CHUNK), F32),
            vm((2, WINDOW, CHUNK), F32),
            vm((2, WINDOW, CHUNK), F32),
            vm((2, WINDOW, CHUNK), BF16),
        ],
        compiler_params=pltpu.CompilerParams(vmem_limit_bytes=32 * 1024 * 1024),
        cost_estimate=pl.CostEstimate(flops=2_000_000_000, bytes_accessed=4_000_000, transcendentals=2_000_000),
        name="attend",
    )(qg, *chunks, up, dmat, rmat)


def per_core(x):
    rows, _, _, n = x.shape
    return x.transpose(2, 0, 1, 3).reshape(2, rows, 2 * n)


def per_device(
    base_queries, adapter_input, adapter_up_weight, projected_keys, projected_values, output_gradient,
    segments, solution, residual, direction, damping,
):
    core = lax.axis_index("core")
    n_yh, n_z = lax.axis_size("yh"), lax.axis_size("z")
    ctx_size = n_yh * n_z * 2
    idx = lax.axis_index(CTX)

    keys = per_core(projected_keys[0].reshape(BLOCK, 2, 2, HEAD_DIM))
    values = per_core(projected_values[0].reshape(BLOCK, 2, 2, HEAD_DIM))
    seg = (segments[0] + 1).astype(BF16)
    seg_row = jnp.zeros((SEG_ROWS, 2 * KHALF), BF16).at[0, :BLOCK].set(seg)
    kv = jnp.concatenate([keys, values], axis=2)
    kv = jnp.concatenate([kv, jnp.broadcast_to(seg_row[None], (2, SEG_ROWS, 2 * KHALF))], axis=1)
    kv = lax.all_to_all(kv, "core", 0, 0, tiled=True)
    segs = jnp.concatenate([kv[0, BLOCK:, :BLOCK], kv[1, BLOCK:, :BLOCK], jnp.zeros((SEG_ROWS, 2 * KHALF - CHUNK), BF16)], axis=1)
    own = jnp.concatenate([kv[0, :BLOCK], kv[1, :BLOCK], segs], axis=0)

    pad = jnp.pad(adapter_input[0], ((0, 0), (0, 128 - RANK)))
    qg = jnp.concatenate(
        [
            per_core(base_queries[0].reshape(BLOCK, 2, 2, GFEAT)),
            per_core(output_gradient[0].reshape(BLOCK, 2, 2, GFEAT)),
            jnp.broadcast_to(pad[None], (2, BLOCK, 128)),
        ],
        axis=2,
    )
    qg = lax.all_to_all(qg, "core", 0, 0, tiled=True).reshape(CHUNK, 2 * HALF + 128)

    earlier = []
    for k in range(1, SPAN + 1):
        earlier.append(lax.ppermute(own, CTX, [(s, s + 2 * k) for s in range(ctx_size - 2 * k)]))
    chunks = earlier[::-1] + [own]

    def core_part(x):
        x = x.reshape(RANK, 2, 2, GFEAT)
        return lax.dynamic_index_in_dim(x, core, 2, keepdims=False).reshape(RANK, HALF)

    terms = attend(qg, chunks, core_part(adapter_up_weight[0]), core_part(direction[0]), core_part(residual[0]))

    peers = n_yh * n_z
    terms = terms.transpose(1, 0, 2).reshape(peers, GFEAT + 128)
    got = jnp.sum(lax.all_to_all(terms, ("yh", "z"), 0, 0, tiled=True), axis=0)
    h = got[:GFEAT]
    dh, rh = got[GFEAT], got[GFEAT + 1]
    both = lax.psum(jnp.stack([dh, rh]), "core")
    dh, rh = both[0], both[1]
    hh_part = jnp.sum(h * h)
    hh = jnp.sum(lax.all_to_all(jnp.full((ctx_size, 128), hh_part), CTX, 0, 0, tiled=True)[:, 0])

    damp = damping[0]
    d_full, r_full = direction[0], residual[0]
    old_norm = jnp.sum(r_full * r_full)
    dd = jnp.sum(d_full * d_full)
    rd = jnp.sum(r_full * d_full)
    step_len = old_norm / (dd + dh / damp)
    size = GFEAT
    d_part = lax.dynamic_slice_in_dim(d_full, idx * size, size, 0)
    r_part = lax.dynamic_slice_in_dim(r_full, idx * size, size, 0)
    s_part = lax.dynamic_slice_in_dim(solution[0], idx * size, size, 0)
    new_solution = s_part + step_len * d_part
    n_task = lax.axis_size("task")
    spread = lax.all_to_all(jnp.broadcast_to(new_solution[None], (n_task, size)), "task", 0, 0, tiled=True)
    meta_gradient = jnp.sum(spread, axis=0) / n_task

    curved = d_part + h / damp
    rc = rd + rh / damp
    cc = dd + 2.0 * dh / damp + hh / (damp * damp)
    new_norm = old_norm - 2.0 * step_len * rc + step_len * step_len * cc
    new_residual = r_part - step_len * curved
    new_direction = new_residual + (new_norm / old_norm) * d_part
    return new_solution[None], new_residual[None], new_direction[None], meta_gradient


def solution(mesh):
    n_task, n_ctx = mesh.devices.shape
    split = Mesh(mesh.devices.reshape(n_task, n_ctx // 16, 8, 2), ("task",) + CTX)
    tokens = P("task", CTX, None)
    whole = P("task", None)
    in_specs = (tokens, tokens, P("task", None, None), tokens, tokens, tokens, P("task", CTX), whole, whole, whole, P("task"))
    out_specs = (P("task", CTX), P("task", CTX), P("task", CTX), P(CTX))
    return jax.shard_map(per_device, mesh=split, in_specs=in_specs, out_specs=out_specs, check_vma=False)
```

time: 231 us -> 134 us (0.58)
  matrix products: 66.2 us -> 0 us
  starting transfers between devices: 111 us -> 60.1 us
  Pallas kernels: 0 us -> 10.9 us
  blocking collectives: 9.13 us -> 14.6 us
  local copies, waits for them, and re-layouts: 5.64 us -> 9.55 us
    ppermute x18 -> x3, starting transfers between devices: 77.8 us -> 11.5 us  [per_device(): lax.ppermute(own, CTX, [(s, s + 2 * k) for s in range(ctx_size - 2 * k)])]
    sub x12 -> x0, matrix products: 45.1 us -> none  [the longest x8 35.7 us: attend(): centred = (slopes - mean_slope) * (pulls - mean_pull)]
    dot_general x11 -> x0, matrix products: 21.1 us -> none  [the longest x4 13.3 us: attend(): jnp.einsum('tgk,kd->tgd', coef_rounded, key_head, preferred_element_type=...]
    all_to_all x2 -> x4, starting transfers between devices: 33.7 us -> 48.7 us  [the longest x1 33.9 us: per_device(): got = jnp.sum(lax.all_to_all(terms, ('yh', 'z'), 0, 0, tiled=True), axis=0)]
    pallas_call x0 -> x1, Pallas kernels: none -> 10.9 us  [attend(): pl.pallas_call(attend_kernel, out_shape=jax.ShapeDtypeStruct((GROUPS, RAN...]
    psum x0 -> x1, blocking collectives: none -> 4.01 us  [per_device(): both = lax.psum(jnp.stack([dh, rh]), 'core')]
    another operation x1 -> x10, local copies, waits for them, and re-layouts: 0.03 us -> 2.95 us  [the longest x2 1.01 us: per_device(): keys = per_core(projected_keys[0].reshape(BLOCK, 2, 2, HEAD_DIM))]
    unnamed x64 -> x19, local copies, waits for them, and re-layouts: 3.49 us -> 0.95 us
  transfers between devices with their start and end apart: 20 -> 7, of which waited for: 3 -> 3; matrix products, arithmetic and copies ran while one was open for 3% -> 6% of each run, Pallas kernels for 0% -> 0%
where the time goes in v1:
time: 134 us
  starting transfers between devices  60.1 us (45%)
  waiting for transfers between devices  23 us (17%)
  blocking collectives  14.6 us (11%)
  Pallas kernels  10.9 us (8%)
  local copies, waits for them, and re-layouts  9.55 us (7%)
  between operations  8.1 us (6%)
  other arithmetic  7.38 us (6%)
    all_to_all x1, starting transfers between devices, per_device(): got = jnp.sum(lax.all_to_all(terms, ('yh', 'z'), 0, 0, tiled=True), axis=0)  33.9 us
    ppermute x3, starting transfers between devices, per_device(): lax.ppermute(own, CTX, [(s, s + 2 * k) for s in range(ctx_size - 2 * k)])  11.5 us
    all_to_all x1, waiting for transfers between devices, per_device(): lax.all_to_all(jnp.full((ctx_size, 128), hh_part), CTX, 0, 0, tiled=True)  11.1 us
    pallas_call x1, Pallas kernels, attend(): pl.pallas_call(attend_kernel, out_shape=jax.ShapeDtypeStruct((GROUPS, RAN...  10.9 us
    all_to_all x1, waiting for transfers between devices, per_device(): got = jnp.sum(lax.all_to_all(terms, ('yh', 'z'), 0, 0, tiled=True), axis=0)  10.6 us
    all_to_all x1, blocking collectives, per_device(): kv = lax.all_to_all(kv, 'core', 0, 0, tiled=True)  10.6 us
    all_to_all x1, starting transfers between devices, per_device(): lax.all_to_all(jnp.full((ctx_size, 128), hh_part), CTX, 0, 0, tiled=True)  5.82 us
    all_to_all x1, starting transfers between devices, per_device(): lax.all_to_all(qg, 'core', 0, 0, tiled=True).reshape(CHUNK, 2 * HALF + 128)  4.92 us
  transfers between devices with their start and end apart: 7, of which 3 were waited for; matrix products, arithmetic and copies ran while one was open for 6% of the time, Pallas kernels for 0%

profile of v1, /device:TPU:1, one launch (start us, length us, event | category | flops | bytes accessed | tf_op | source)
XLA Modules:
  0.0 133.7 jit_solution(14957428283205531447)
XLA Ops:
  0.6 0.7 add_convert_fusion
  1.3 0.9 reshape_squeeze.24
  2.4 0.9 reshape_squeeze.23
  3.6 10.6 %all_to_all.35 = bf16[2,144,512]{2,1,0:T(8,128)(2,1)S(1)} all-to-all(bf16[2,144,512]{2,1,0:T(8,128)(2,1)S(1)} %pad_maximum_fusion.1), channel_id=1, replica_groups=mesh['task'=8,'yh'=4,'z'=8,'core'=2] {'core'}, dimensions={0} | all-to-all | bytes 589824 | tf_op jit(solution)/shard_map/all_to_all | solution.py:192
  14.3 2.3 %collective-permute-start = (bf16[272,512]{1,0:T(8,128)(2,1)S(1)}, bf16[272,512]{1,0:T(8,128)(2,1)S(1)}, u32[]{:S(2)}, u32[]{:S(2)}) collective-permute-start(bf16[272,512]{1,0:T(8,128)(2,1)S(1)} %maximum_maximum_fusion.c3), channel_id=1, source_target_pairs={{0,6},{1,7},{2,8},{3,9},{4,10},{5,11},{6,12},{7,13},{8,14},{9,15},... | collective-permute-start | bytes 835592 | tf_op jit(solution)/shard_map/ppermute | solution.py:209
  16.5 6.1 %collective-permute-start.1 = (bf16[272,512]{1,0:T(8,128)(2,1)S(1)}, bf16[272,512]{1,0:T(8,128)(2,1)S(1)}, u32[]{:S(2)}, u32[]{:S(2)}) collective-permute-start(bf16[272,512]{1,0:T(8,128)(2,1)S(1)} %maximum_maximum_fusion.c3), channel_id=1, source_target_pairs={{0,4},{1,5},{2,6},{3,7},{4,8},{5,9},{6,10},{7,11},{8,12},{9,13},{1... | collective-permute-start | bytes 835592 | tf_op jit(solution)/shard_map/ppermute | solution.py:209
  22.7 3.1 %collective-permute-start.2 = (bf16[272,512]{1,0:T(8,128)(2,1)S(1)}, bf16[272,512]{1,0:T(8,128)(2,1)S(1)}, u32[]{:S(2)}, u32[]{:S(2)}) collective-permute-start(bf16[272,512]{1,0:T(8,128)(2,1)S(1)} %maximum_maximum_fusion.c3), channel_id=1, source_target_pairs={{0,2},{1,3},{2,4},{3,5},{4,6},{5,7},{6,8},{7,9},{8,10},{9,11},{10,... | collective-permute-start | bytes 835592 | tf_op jit(solution)/shard_map/ppermute | solution.py:209
  25.9 0.4 reshape_squeeze.22
  26.3 0.4 copy.53
  27.7 0.4 copy.52
  28.5 1.1 pad_maximum_fusion
  29.6 4.9 %all-to-all-start = ((bf16[2,128,2176]{2,1,0:T(8,128)(2,1)}), bf16[2,128,2176]{2,1,0:T(8,128)(2,1)S(1)}, u32[]{:S(2)}, u32[]{:S(2)}) async-start(bf16[2,128,2176]{2,1,0:T(8,128)(2,1)} %pad_maximum_fusion), calls=%async_computation | async-start | bytes 2228224 | tf_op jit(solution)/shard_map/all_to_all | solution.py:205
  34.8 0.5 broadcast.50
  35.3 2.4 %multiply_reduce_fusion = (f32[]{:T(128)}, f32[32768]{0:T(1024)S(1)}, f32[]{:T(128)}, f32[32768]{0:T(1024)S(1)}, f32[]{:T(128)}) fusion(f32[1,32768]{1,0:T(1,128)S(1)} %copy-done.2, f32[1,32768]{1,0:T(1,128)S(1)} %copy-done.3, f32[]{:T(128)} %broadcast.50), kind=kLoop, calls=%fused_computation.7 | loop fusion | flops 196605 | bytes 524304 | tf_op jit(solution)/shard_map/reduce_sum | solution.py:232
  37.9 0.4 dynamic-slice_reduce_fusion
  38.4 10.9 %attend.1 = f32[2,16,640]{2,1,0:T(8,128)S(1)} custom-call(bf16[256,2176]{1,0:T(8,128)(2,1)S(1)} %bitcast.40, bf16[272,512]{1,0:T(8,128)(2,1)S(1)} %collective-permute-done.c0, bf16[272,512]{1,0:T(8,128)(2,1)S(1)} %collective-permute-done.1.c1, bf16[272,512]{1,0:T(8,128)(2,1)S(1)} %collective-permute-done.2.c2, bf16[272,512]{1,0:T(8,128)(2,1)S(1)} %maximum_maximum_fusion.c3, ...), custom_call_target="tpu_custom_call" | custom-call | flops 2000000000 | bytes 4000000 | tf_op jit(solution)/shard_map/attend/pallas_call | solution.py:148
  49.4 0.7 all_to_all.29
  50.1 33.9 %all-to-all-start.2 = ((f32[32,1,640]{2,1,0:T(1,128)}), f32[32,1,640]{2,1,0:T(1,128)S(1)}, u32[]{:S(2)}, u32[]{:S(2)}) async-start(f32[32,1,640]{2,1,0:T(1,128)} %all_to_all.29), calls=%async_computation.2 | async-start | bytes 163840 | tf_op jit(solution)/shard_map/all_to_all | solution.py:220
  84.7 10.6 %all-to-all-done.2 = f32[32,1,640]{2,1,0:T(1,128)S(1)} async-done(((f32[32,1,640]{2,1,0:T(1,128)}), f32[32,1,640]{2,1,0:T(1,128)S(1)}, u32[]{:S(2)}, u32[]{:S(2)}) %all-to-all-start.2) | async-done | bytes 81952 | tf_op jit(solution)/shard_map/all_to_all | solution.py:220
  95.4 4.0 %psum.7 = f32[2]{0:T(128)S(1)} all-reduce(f32[2]{0:T(128)S(1)} %stack.3), channel_id=1, replica_groups=mesh['task'=8,'yh'=4,'z'=8,'core'=2] {'core'}, use_global_device_ids=true, to_apply=%region_3.4 | all-reduce | flops 2 | bytes 16 | tf_op jit(solution)/shard_map/psum | solution.py:223
  99.4 0.6 fusion
  101.9 0.7 constant_dynamic-slice_fusion.1
  102.6 0.6 broadcast_in_dim.38
  103.2 4.0 %all-to-all-start.4 = ((f32[8,1,512]{2,1,0:T(1,128)}), f32[8,1,512]{2,1,0:T(1,128)S(1)}, u32[]{:S(2)}, u32[]{:S(2)}) async-start(f32[8,1,512]{2,1,0:T(1,128)} %broadcast_in_dim.38), calls=%async_computation.4 | async-start | bytes 32768 | tf_op jit(solution)/shard_map/all_to_all | solution.py:240
  107.2 0.6 multiply_reduce_fusion.3
  111.0 1.3 all-to-all-done.4
  112.3 1.3 broadcast_in_dim.36
  113.5 5.8 %all-to-all-start.3 = ((f32[64,1,128]{2,1,0:T(1,128)}), f32[64,1,128]{2,1,0:T(1,128)S(1)}, u32[]{:S(2)}, u32[]{:S(2)}) async-start(f32[64,1,128]{2,1,0:T(1,128)} %broadcast_in_dim.36), calls=%async_computation.3 | async-start | bytes 65536 | tf_op jit(solution)/shard_map/all_to_all | solution.py:226
  119.4 0.6 broadcast_multiply_fusion
  120.0 11.1 %all-to-all-done.3 = f32[64,1,128]{2,1,0:T(1,128)S(1)} async-done(((f32[64,1,128]{2,1,0:T(1,128)}), f32[64,1,128]{2,1,0:T(1,128)S(1)}, u32[]{:S(2)}, u32[]{:S(2)}) %all-to-all-start.3) | async-done | bytes 32800 | tf_op jit(solution)/shard_map/all_to_all | solution.py:226
  131.1 0.6 slice_reduce_fusion
  133.1 0.6 multiply_add_fusion
  (47 shorter events, 2.5 us)
Async XLA Ops:
  3.6 22.2 %copy-start.6 = (bf16[1,128,16]{1,2,0:T(8,128)(2,1)S(1)}, bf16[1,128,16]{1,2,0:T(8,128)(2,1)}, u32[]{:S(2)}) copy-start(bf16[1,128,16]{1,2,0:T(8,128)(2,1)} %param.14) | copy-start | bytes 12292
  3.6 22.4 %copy-start = (bf16[1,128,2048]{2,1,0:T(8,128)(2,1)S(1)}, bf16[1,128,2048]{2,1,0:T(8,128)(2,1)}, u32[]{:S(2)}) copy-start(bf16[1,128,2048]{2,1,0:T(8,128)(2,1)} %param.18) | copy-start | bytes 1572868
  14.3 24.1 %collective-permute-start = (bf16[272,512]{1,0:T(8,128)(2,1)S(1)}, bf16[272,512]{1,0:T(8,128)(2,1)S(1)}, u32[]{:S(2)}, u32[]{:S(2)}) collective-permute-start(bf16[272,512]{1,0:T(8,128)(2,1)S(1)} %maximum_maximum_fusion.c3), channel_id=1, source_target_pairs={{0,6},{1,7},{2,8},{3,9},{4,10},{5,11},{6,12},{7,13},{8,14},{9,15},... | collective-permute-start | bytes 835592 | tf_op jit(solution)/shard_map/ppermute | solution.py:209
  16.5 21.8 %collective-permute-start.1 = (bf16[272,512]{1,0:T(8,128)(2,1)S(1)}, bf16[272,512]{1,0:T(8,128)(2,1)S(1)}, u32[]{:S(2)}, u32[]{:S(2)}) collective-permute-start(bf16[272,512]{1,0:T(8,128)(2,1)S(1)} %maximum_maximum_fusion.c3), channel_id=1, source_target_pairs={{0,4},{1,5},{2,6},{3,7},{4,8},{5,9},{6,10},{7,11},{8,12},{9,13},{1... | collective-permute-start | bytes 835592 | tf_op jit(solution)/shard_map/ppermute | solution.py:209
  22.7 15.7 %collective-permute-start.2 = (bf16[272,512]{1,0:T(8,128)(2,1)S(1)}, bf16[272,512]{1,0:T(8,128)(2,1)S(1)}, u32[]{:S(2)}, u32[]{:S(2)}) collective-permute-start(bf16[272,512]{1,0:T(8,128)(2,1)S(1)} %maximum_maximum_fusion.c3), channel_id=1, source_target_pairs={{0,2},{1,3},{2,4},{3,5},{4,6},{5,7},{6,8},{7,9},{8,10},{9,11},{10,... | collective-permute-start | bytes 835592 | tf_op jit(solution)/shard_map/ppermute | solution.py:209
  26.3 1.0 copy-start.1
  29.6 4.9 %copy-start.4 = (bf16[1,16,2048]{2,1,0:T(8,128)(2,1)S(1)}, bf16[1,16,2048]{2,1,0:T(8,128)(2,1)}, u32[]{:S(2)}) copy-start(bf16[1,16,2048]{2,1,0:T(8,128)(2,1)} %param.15) | copy-start | bytes 196612
  29.6 5.7 %copy-start.2 = (f32[1,32768]{1,0:T(1,128)S(1)}, f32[1,32768]{1,0:T(1,128)}, u32[]{:S(2)}) copy-start(f32[1,32768]{1,0:T(1,128)} %param.21) | copy-start | bytes 393220
  29.6 5.7 %copy-start.3 = (f32[1,32768]{1,0:T(1,128)S(1)}, f32[1,32768]{1,0:T(1,128)}, u32[]{:S(2)}) copy-start(f32[1,32768]{1,0:T(1,128)} %param.22) | copy-start | bytes 393220
  29.6 8.7 %all-to-all-start = ((bf16[2,128,2176]{2,1,0:T(8,128)(2,1)}), bf16[2,128,2176]{2,1,0:T(8,128)(2,1)S(1)}, u32[]{:S(2)}, u32[]{:S(2)}) async-start(bf16[2,128,2176]{2,1,0:T(8,128)(2,1)} %pad_maximum_fusion), calls=%async_computation | async-start | bytes 2228224 | tf_op jit(solution)/shard_map/all_to_all | solution.py:205
  50.1 45.2 %all-to-all-start.2 = ((f32[32,1,640]{2,1,0:T(1,128)}), f32[32,1,640]{2,1,0:T(1,128)S(1)}, u32[]{:S(2)}, u32[]{:S(2)}) async-start(f32[32,1,640]{2,1,0:T(1,128)} %all_to_all.29), calls=%async_computation.2 | async-start | bytes 163840 | tf_op jit(solution)/shard_map/all_to_all | solution.py:220
  102.6 31.1 %copy-start.5 = (f32[1,512]{1,0:T(1,128)}, f32[1,512]{1,0:T(1,128)S(1)}, u32[]{:S(2)}) copy-start(f32[1,512]{1,0:T(1,128)S(1)} %get-tuple-element.28) | copy-start | bytes 6148
  103.2 9.1 %all-to-all-start.4 = ((f32[8,1,512]{2,1,0:T(1,128)}), f32[8,1,512]{2,1,0:T(1,128)S(1)}, u32[]{:S(2)}, u32[]{:S(2)}) async-start(f32[8,1,512]{2,1,0:T(1,128)} %broadcast_in_dim.38), calls=%async_computation.4 | async-start | bytes 32768 | tf_op jit(solution)/shard_map/all_to_all | solution.py:240
  113.5 17.6 %all-to-all-start.3 = ((f32[64,1,128]{2,1,0:T(1,128)}), f32[64,1,128]{2,1,0:T(1,128)S(1)}, u32[]{:S(2)}, u32[]{:S(2)}) async-start(f32[64,1,128]{2,1,0:T(1,128)} %broadcast_in_dim.36), calls=%async_computation.3 | async-start | bytes 65536 | tf_op jit(solution)/shard_map/all_to_all | solution.py:226

commit v2 on v1

--- a/solution.py
+++ b/solution.py
@@ -169,6 +169,77 @@
     )(qg, *chunks, up, dmat, rmat)
 
 
+def sum_spread_kernel(got, out):
+    total = jnp.sum(got[...], axis=0, keepdims=True)
+    out[...] = jnp.broadcast_to(total, out.shape)
+
+
+def norm_kernel(got, h_out, out):
+    total = jnp.sum(got[...], axis=0)
+    h = total[:, : h_out.shape[1]]
+    h_out[...] = h
+    tail = total[:, h_out.shape[1] :]
+    lane = lax.broadcasted_iota(jnp.int32, tail.shape, 1)
+    share = 2.0 / out.shape[0]
+    row = jnp.where(lane == 2, jnp.sum(h * h, keepdims=True), tail * share)
+    out[...] = jnp.broadcast_to(row[None], out.shape)
+
+
+def update_kernel(sizes, got, h_all, dot_in, parts, new_solution, new_residual, new_direction, spread):
+    total = jnp.sum(got[...], axis=0)
+    lane = lax.broadcasted_iota(jnp.int32, total.shape, 1)
+
+    def pick(row, k):
+        return jnp.sum(jnp.where(lane == k, row, 0.0), keepdims=True)
+
+    dh, rh, hh = pick(total, 0), pick(total, 1), pick(total, 2)
+    consts = dot_in[...]
+    rr, dd, rd, damp = (pick(consts, k) for k in range(4))
+    size = new_solution.shape[1]
+    h = h_all[:, pl.ds(pl.multiple_of(sizes[0] * size, 128), size)]
+    sol, res, dirn = parts[0:1], parts[1:2], parts[2:3]
+    step_len = rr / (dd + dh / damp)
+    curved = dirn + h / damp
+    rc = rd + rh / damp
+    cc = dd + 2.0 * dh / damp + hh / (damp * damp)
+    new_norm = rr - 2.0 * step_len * rc + step_len * step_len * cc
+    ns = sol + step_len * dirn
+    nr = res - step_len * curved
+    new_solution[...] = ns
+    new_residual[...] = nr
+    new_direction[...] = nr + (new_norm / rr) * dirn
+    spread[...] = jnp.broadcast_to(ns[None], spread.shape)
+
+
+def in_vmem(kernel, out_shapes, *args, name, smem=0):
+    specs = [pl.BlockSpec(memory_space=pltpu.SMEM)] * smem
+    specs += [pl.BlockSpec(memory_space=pltpu.VMEM)] * (len(args) - smem)
+    return pl.pallas_call(
+        kernel,
+        out_shape=[jax.ShapeDtypeStruct(s, F32) for s in out_shapes],
+        in_specs=specs,
+        out_specs=[pl.BlockSpec(memory_space=pltpu.VMEM)] * len(out_shapes),
+        name=name,
+    )(*args)
+
+
+def exchange(x, axes):
+    return lax.all_to_all(x, axes, 0, 0, tiled=True)
+
+
+def spot(yh, z, core, n_z):
+    return (yh * n_z + z) * 2 + core
+
+
+def moves(n_yh, n_z, kinds):
+    pairs = []
+    for source, target, up in kinds:
+        for yh in range(n_yh - up):
+            for core in range(2):
+                pairs.append((spot(yh, source, core, n_z), spot(yh + up, target, core, n_z)))
+    return pairs
+
+
 def per_core(x):
     rows, _, _, n = x.shape
     return x.transpose(2, 0, 1, 3).reshape(2, rows, 2 * n)
@@ -178,20 +249,33 @@
     base_queries, adapter_input, adapter_up_weight, projected_keys, projected_values, output_gradient,
     segments, solution, residual, direction, damping,
 ):
-    core = lax.axis_index("core")
-    n_yh, n_z = lax.axis_size("yh"), lax.axis_size("z")
-    ctx_size = n_yh * n_z * 2
+    core, z, yh = lax.axis_index("core"), lax.axis_index("z"), lax.axis_index("yh")
+    n_yh, n_z, n_task = lax.axis_size("yh"), lax.axis_size("z"), lax.axis_size("task")
     idx = lax.axis_index(CTX)
 
-    keys = per_core(projected_keys[0].reshape(BLOCK, 2, 2, HEAD_DIM))
-    values = per_core(projected_values[0].reshape(BLOCK, 2, 2, HEAD_DIM))
+    def core_part(x):
+        rows, feats = x.shape[0], x.shape[1] // 4
+        x = x.reshape(rows, 2, 2, feats)
+        return lax.dynamic_index_in_dim(x, core, 2, keepdims=False).reshape(rows, 2 * feats)
+
     seg = (segments[0] + 1).astype(BF16)
-    seg_row = jnp.zeros((SEG_ROWS, 2 * KHALF), BF16).at[0, :BLOCK].set(seg)
-    kv = jnp.concatenate([keys, values], axis=2)
-    kv = jnp.concatenate([kv, jnp.broadcast_to(seg_row[None], (2, SEG_ROWS, 2 * KHALF))], axis=1)
-    kv = lax.all_to_all(kv, "core", 0, 0, tiled=True)
+    width = 4 * KHALF
+    kv = jnp.concatenate([projected_keys[0], projected_values[0]], axis=1)
+    kv = jnp.concatenate([kv, jnp.broadcast_to(jnp.pad(seg, (0, width - BLOCK)), (SEG_ROWS, width))], axis=0)
+    kv = lax.all_gather(kv, "core")
+    own_rows = jnp.concatenate([core_part(kv[:, :BLOCK].reshape(CHUNK, width)[:, : width // 2]),
+                                core_part(kv[:, :BLOCK].reshape(CHUNK, width)[:, width // 2 :])], axis=1)
     segs = jnp.concatenate([kv[0, BLOCK:, :BLOCK], kv[1, BLOCK:, :BLOCK], jnp.zeros((SEG_ROWS, 2 * KHALF - CHUNK), BF16)], axis=1)
-    own = jnp.concatenate([kv[0, :BLOCK], kv[1, :BLOCK], segs], axis=0)
+    own = jnp.concatenate([own_rows, segs], axis=0)
+
+    last = n_z - 1
+    row = [(i, i + 1, 0) for i in range(last)]
+    first = lax.ppermute(own, CTX, moves(n_yh, n_z, row + [(last, 0, 1)]))
+    cross = lax.ppermute(own, CTX, moves(n_yh, n_z, [(last - 1, 0, 1), (last - 2, last, 1)]))
+    second = lax.ppermute(first, CTX, moves(n_yh, n_z, row))
+    passed = jnp.where((z == 0) | (z == last), cross, second)
+    third = lax.ppermute(passed, CTX, moves(n_yh, n_z, row + [(last, 0, 0)]))
+    second = jnp.where(z == 0, cross, second)
 
     pad = jnp.pad(adapter_input[0], ((0, 0), (0, 128 - RANK)))
     qg = jnp.concatenate(
@@ -202,51 +286,37 @@
         ],
         axis=2,
     )
-    qg = lax.all_to_all(qg, "core", 0, 0, tiled=True).reshape(CHUNK, 2 * HALF + 128)
-
-    earlier = []
-    for k in range(1, SPAN + 1):
-        earlier.append(lax.ppermute(own, CTX, [(s, s + 2 * k) for s in range(ctx_size - 2 * k)]))
-    chunks = earlier[::-1] + [own]
-
-    def core_part(x):
-        x = x.reshape(RANK, 2, 2, GFEAT)
-        return lax.dynamic_index_in_dim(x, core, 2, keepdims=False).reshape(RANK, HALF)
-
-    terms = attend(qg, chunks, core_part(adapter_up_weight[0]), core_part(direction[0]), core_part(residual[0]))
-
-    peers = n_yh * n_z
-    terms = terms.transpose(1, 0, 2).reshape(peers, GFEAT + 128)
-    got = jnp.sum(lax.all_to_all(terms, ("yh", "z"), 0, 0, tiled=True), axis=0)
-    h = got[:GFEAT]
-    dh, rh = got[GFEAT], got[GFEAT + 1]
-    both = lax.psum(jnp.stack([dh, rh]), "core")
-    dh, rh = both[0], both[1]
-    hh_part = jnp.sum(h * h)
-    hh = jnp.sum(lax.all_to_all(jnp.full((ctx_size, 128), hh_part), CTX, 0, 0, tiled=True)[:, 0])
-
-    damp = damping[0]
-    d_full, r_full = direction[0], residual[0]
-    old_norm = jnp.sum(r_full * r_full)
-    dd = jnp.sum(d_full * d_full)
-    rd = jnp.sum(r_full * d_full)
-    step_len = old_norm / (dd + dh / damp)
-    size = GFEAT
-    d_part = lax.dynamic_slice_in_dim(d_full, idx * size, size, 0)
-    r_part = lax.dynamic_slice_in_dim(r_full, idx * size, size, 0)
-    s_part = lax.dynamic_slice_in_dim(solution[0], idx * size, size, 0)
-    new_solution = s_part + step_len * d_part
-    n_task = lax.axis_size("task")
-    spread = lax.all_to_all(jnp.broadcast_to(new_solution[None], (n_task, size)), "task", 0, 0, tiled=True)
-    meta_gradient = jnp.sum(spread, axis=0) / n_task
-
-    curved = d_part + h / damp
-    rc = rd + rh / damp
-    cc = dd + 2.0 * dh / damp + hh / (damp * damp)
-    new_norm = old_norm - 2.0 * step_len * rc + step_len * step_len * cc
-    new_residual = r_part - step_len * curved
-    new_direction = new_residual + (new_norm / old_norm) * d_part
-    return new_solution[None], new_residual[None], new_direction[None], meta_gradient
+    qg = exchange(qg, "core").reshape(CHUNK, 2 * HALF + 128)
+
+    up, dmat, rmat = (core_part(x.reshape(RANK, 2 * HALF)) for x in (adapter_up_weight[0], direction[0], residual[0]))
+    size = direction.shape[1] // (n_yh * n_z * 2)
+    parts = jnp.concatenate([lax.dynamic_slice_in_dim(x, idx * size, size, 1) for x in (solution, residual, direction)])
+    consts = jnp.stack([jnp.sum(residual * residual), jnp.sum(direction * direction), jnp.sum(residual * direction), damping[0]])
+    consts = jnp.pad(consts, (0, 124))[None]
+
+    terms = attend(qg, [third, second, first, own], up, dmat, rmat)
+
+    tail = terms[0, :1, GFEAT:]
+    body = terms[:, :, :GFEAT].reshape(2, n_yh, n_z // 2, GFEAT).transpose(2, 0, 1, 3).reshape(n_z, n_yh * GFEAT)
+    body = jnp.concatenate([body, jnp.broadcast_to(tail, (n_z, 128))], axis=1)
+    width = body.shape[1]
+    (row_sum,) = in_vmem(sum_spread_kernel, [(n_yh, 1, width)], exchange(body.reshape(n_z, 1, width), "z"), name="row_sum")
+    h_all, scalars = in_vmem(
+        norm_kernel, [(1, width - 128), (2 * n_z, 1, 128)], exchange(row_sum, "yh"), name="norm"
+    )
+    new_solution, new_residual, new_direction, spread = in_vmem(
+        update_kernel,
+        [(1, size)] * 3 + [(n_task, 1, size)],
+        yh.reshape(1),
+        exchange(scalars, ("z", "core")),
+        h_all,
+        consts,
+        parts,
+        name="update",
+        smem=1,
+    )
+    meta_gradient = jnp.sum(exchange(spread, "task"), axis=(0, 1)) / n_task
+    return new_solution, new_residual, new_direction, meta_gradient
 
 
 def solution(mesh):

time: 134 us -> 126 us (0.940)
  starting transfers between devices: 60.1 us -> 46.6 us
  between operations: 8.1 us -> 1.65 us
  blocking collectives: 14.6 us -> 19.3 us
  Pallas kernels: 10.9 us -> 15.4 us
  other arithmetic: 7.38 us -> 9.95 us
    all_to_all x4, starting transfers between devices: 48.7 us -> 35.6 us  [exchange(): return lax.all_to_all(x, axes, 0, 0, tiled=True)]
    all_gather x0 -> x1, blocking collectives: none -> 8.73 us  [per_device(): kv = lax.all_gather(kv, 'core')]
    ppermute x3 -> x4, waiting for transfers between devices: 0.01 us -> 6.88 us  [the longest x1 5.27 us: per_device(): first = lax.ppermute(own, CTX, moves(n_yh, n_z, row + [(last, 0, 1)]))]
    all_to_all x4, waiting for transfers between devices: 23 us -> 17.1 us  [exchange(): return lax.all_to_all(x, axes, 0, 0, tiled=True)]
    pallas_call x0 -> x3, Pallas kernels: none -> 4.54 us  [in_vmem(): pl.pallas_call(kernel, out_shape=[jax.ShapeDtypeStruct(s, F32) for s in o...]
    psum x1 -> x0, blocking collectives: 4.01 us -> none  [per_device(): both = lax.psum(jnp.stack([dh, rh]), 'core')]
    broadcast_in_dim x0 -> x1, other arithmetic: none -> 2.55 us  [per_device(): consts = jnp.pad(consts, (0, 124))[None]]
    another operation x8 -> x3, local copies, waits for them, and re-layouts: 2.2 us -> 0.17 us  [core_part(): x = x.reshape(rows, 2, 2, feats)]
  transfers between devices with their start and end apart: 7 -> 8, of which waited for: 3 -> 5; matrix products, arithmetic and copies ran while one was open for 6% -> 8% of each run, Pallas kernels for 0% -> 0%
where the time goes in v2:
time: 126 us
  starting transfers between devices  46.6 us (37%)
  waiting for transfers between devices  24 us (19%)
  blocking collectives  19.3 us (15%)
  Pallas kernels  15.4 us (12%)
  other arithmetic  9.95 us (8%)
  local copies, waits for them, and re-layouts  8.72 us (7%)
  between operations  1.65 us (1%)
    all_to_all x4, starting transfers between devices, exchange(): return lax.all_to_all(x, axes, 0, 0, tiled=True)  35.6 us
    all_to_all x4, waiting for transfers between devices, exchange(): return lax.all_to_all(x, axes, 0, 0, tiled=True)  17.1 us
    pallas_call x1, Pallas kernels, attend(): pl.pallas_call(attend_kernel, out_shape=jax.ShapeDtypeStruct((GROUPS, RAN...  10.9 us
    all_to_all x1, blocking collectives, exchange(): return lax.all_to_all(x, axes, 0, 0, tiled=True)  10.5 us
    all_gather x1, blocking collectives, per_device(): kv = lax.all_gather(kv, 'core')  8.73 us
    ppermute x1, waiting for transfers between devices, per_device(): first = lax.ppermute(own, CTX, moves(n_yh, n_z, row + [(last, 0, 1)]))  5.27 us
    ppermute x1, starting transfers between devices, per_device(): second = lax.ppermute(first, CTX, moves(n_yh, n_z, row))  4.81 us
    pallas_call x3, Pallas kernels, in_vmem(): pl.pallas_call(kernel, out_shape=[jax.ShapeDtypeStruct(s, F32) for s in o...  4.54 us
  transfers between devices with their start and end apart: 8, of which 5 were waited for; matrix products, arithmetic and copies ran while one was open for 8% of the time, Pallas kernels for 0%

profile of v2, /device:TPU:1, one launch (start us, length us, event | category | flops | bytes accessed | tf_op | source)
XLA Modules:
  0.0 125.6 jit_solution(5614042379047178125)
XLA Ops:
  0.6 0.7 convert_bitcast_fusion
  1.4 1.0 pad_maximum_fusion.1
  2.4 8.7 %all-gather = bf16[288,1024]{1,0:T(8,128)(2,1)S(1)} all-gather(bf16[144,1024]{1,0:T(8,128)(2,1)S(1)} %pad_maximum_fusion.1), channel_id=2, replica_groups=mesh['task'=8,'yh'=4,'z'=8,'core'=2] {'core'}, dimensions={0}, use_global_device_ids=true | all-gather | bytes 884736 | tf_op jit(solution)/shard_map/all_gather | solution.py:265
  11.3 1.8 %dynamic-slice_reduce_fusion = (bf16[256,2,128]{2,1,0:T(2,128)(2,1)S(1)}, bf16[256,2,128]{2,1,0:T(2,128)(2,1)S(1)}) fusion(bf16[256,2,2,128]{3,2,1,0:T(2,128)(2,1)S(1)} %reshape.71, s32[]{:T(128)S(6)} %select_n.30, bf16[256,2,2,128]{3,2,1,0:T(2,128)(2,1)S(1)} %reshape.69), kind=kLoop, calls=%fused_computation.5 | loop fusion | bytes 524292 | tf_op jit(solution)/shard_map/jit(dynamic_index_in_dim)/dynamic_slice | solution.py:259
  13.2 1.3 %collective-permute-start.1 = (bf16[272,512]{1,0:T(8,128)(2,1)S(1)}, bf16[272,512]{1,0:T(8,128)(2,1)S(1)}, u32[]{:S(2)}, u32[]{:S(2)}) collective-permute-start(bf16[272,512]{1,0:T(8,128)(2,1)S(1)} %maximum_maximum_fusion.c3), channel_id=1, source_target_pairs={{0,2},{1,3},{16,18},{17,19},{32,34},{33,35},{48,50},{49,51},{2,4},... | collective-permute-start | bytes 835592 | tf_op jit(solution)/shard_map/ppermute | solution.py:273
  14.6 0.7 collective-permute-start
  15.2 5.3 %collective-permute-done.1.c2 = bf16[272,512]{1,0:T(8,128)(2,1)S(1)} collective-permute-done((bf16[272,512]{1,0:T(8,128)(2,1)S(1)}, bf16[272,512]{1,0:T(8,128)(2,1)S(1)}, u32[]{:S(2)}, u32[]{:S(2)}) %collective-permute-start.1) | collective-permute-done | bytes 278560 | tf_op jit(solution)/shard_map/ppermute | solution.py:273
  20.5 4.8 %collective-permute-start.2 = (bf16[272,512]{1,0:T(8,128)(2,1)S(1)}, bf16[272,512]{1,0:T(8,128)(2,1)}, u32[]{:S(2)}, u32[]{:S(2)}) collective-permute-start(bf16[272,512]{1,0:T(8,128)(2,1)S(1)} %collective-permute-done.1.c2), channel_id=1, source_target_pairs={{0,2},{1,3},{16,18},{17,19},{32,34},{33,35},{48,50},{49,51},{2,4},... | collective-permute-start | bytes 835592 | tf_op jit(solution)/shard_map/ppermute | solution.py:275
  28.1 1.6 %collective-permute-done.2 = bf16[272,512]{1,0:T(8,128)(2,1)} collective-permute-done((bf16[272,512]{1,0:T(8,128)(2,1)S(1)}, bf16[272,512]{1,0:T(8,128)(2,1)}, u32[]{:S(2)}, u32[]{:S(2)}) %collective-permute-start.2) | collective-permute-done | bytes 278560 | tf_op jit(solution)/shard_map/ppermute | solution.py:275
  29.7 1.0 broadcast_select_fusion
  30.7 4.2 %collective-permute-start.3 = (bf16[272,512]{1,0:T(8,128)(2,1)S(1)}, bf16[272,512]{1,0:T(8,128)(2,1)S(1)}, u32[]{:S(2)}, u32[]{:S(2)}) collective-permute-start(bf16[272,512]{1,0:T(8,128)(2,1)S(1)} %get-tuple-element.24), channel_id=1, source_target_pairs={{0,2},{1,3},{16,18},{17,19},{32,34},{33,35},{48,50},{49,51},{2,4},... | collective-permute-start | bytes 835592 | tf_op jit(solution)/shard_map/ppermute | solution.py:277
  34.9 1.1 pad_maximum_fusion
  36.0 5.8 %all-to-all-start = ((bf16[2,128,2176]{2,1,0:T(8,128)(2,1)}), bf16[2,128,2176]{2,1,0:T(8,128)(2,1)S(1)}, u32[]{:S(2)}, u32[]{:S(2)}) async-start(bf16[2,128,2176]{2,1,0:T(8,128)(2,1)} %pad_maximum_fusion), calls=%async_computation | async-start | bytes 2228224 | tf_op jit(solution)/shard_map/all_to_all | solution.py:227
  42.6 2.4 %multiply_reduce_fusion.2 = (f32[]{:T(128)}, f32[32768]{0:T(1024)S(1)}, f32[]{:T(128)}, f32[]{:T(128)}, f32[32768]{0:T(1024)S(1)}) fusion(f32[1,32768]{1,0:T(1,128)S(1)} %copy-done.5, f32[]{:T(128)} %broadcast.33, f32[1,32768]{1,0:T(1,128)S(1)} %copy-done.6), kind=kLoop, calls=%fused_computation.11 | loop fusion | flops 196605 | bytes 524304 | tf_op jit(solution)/shard_map/reduce_sum | solution.py:294
  45.6 10.9 %attend.1 = f32[2,16,640]{2,1,0:T(8,128)S(1)} custom-call(bf16[256,2176]{1,0:T(8,128)(2,1)S(1)} %bitcast.40, bf16[272,512]{1,0:T(8,128)(2,1)S(1)} %collective-permute-done.3.c0, bf16[272,512]{1,0:T(8,128)(2,1)S(1)} %get-tuple-element.23.c1, bf16[272,512]{1,0:T(8,128)(2,1)S(1)} %collective-permute-done.1.c2, bf16[272,512]{1,0:T(8,128)(2,1)S(1)} %maximum_maximum_fusion.c3, ...), custom_call_target="tpu_custom_call" | custom-call | flops 2000000000 | bytes 4000000 | tf_op jit(solution)/shard_map/attend/pallas_call | solution.py:148
  56.7 0.7 reshape.78
  57.3 7.6 %all-to-all-start.1 = ((f32[8,1,2176]{2,1,0:T(1,128)}), f32[8,1,2176]{2,1,0:T(1,128)S(1)}, u32[]{:S(2)}, u32[]{:S(2)}) async-start(f32[8,1,2176]{2,1,0:T(1,128)} %reshape.78), calls=%async_computation.1 | async-start | bytes 139264 | tf_op jit(solution)/shard_map/all_to_all | solution.py:227
  65.0 7.1 %all-to-all-done.1.got = f32[8,1,2176]{2,1,0:T(1,128)S(1)} async-done(((f32[8,1,2176]{2,1,0:T(1,128)}), f32[8,1,2176]{2,1,0:T(1,128)S(1)}, u32[]{:S(2)}, u32[]{:S(2)}) %all-to-all-start.1) | async-done | bytes 69664 | tf_op jit(solution)/shard_map/all_to_all | solution.py:227
  72.2 0.6 copy-done.3
  72.8 1.5 %row_sum.1 = f32[4,1,2176]{2,1,0:T(1,128)} custom-call(f32[8,1,2176]{2,1,0:T(1,128)} %copy-done.3), custom_call_target="tpu_custom_call" | custom-call | tf_op jit(solution)/shard_map/row_sum/pallas_call | solution.py:217
  74.3 15.9 %all-to-all-start.2 = ((f32[4,1,2176]{2,1,0:T(1,128)}), f32[4,1,2176]{2,1,0:T(1,128)S(1)}, u32[]{:S(2)}, u32[]{:S(2)}) async-start(f32[4,1,2176]{2,1,0:T(1,128)} %row_sum.1), calls=%async_computation.2 | async-start | bytes 69632 | tf_op jit(solution)/shard_map/all_to_all | solution.py:227
  90.2 0.6 pad_maximum_fusion.3.parts
  91.5 5.5 %all-to-all-done.2.got = f32[4,1,2176]{2,1,0:T(1,128)S(1)} async-done(((f32[4,1,2176]{2,1,0:T(1,128)}), f32[4,1,2176]{2,1,0:T(1,128)S(1)}, u32[]{:S(2)}, u32[]{:S(2)}) %all-to-all-start.2) | async-done | bytes 34848 | tf_op jit(solution)/shard_map/all_to_all | solution.py:227
  97.0 0.6 copy-done.4
  97.6 1.5 %norm.1 = (f32[1,2048]{1,0:T(1,128)}, f32[16,1,128]{2,1,0:T(1,128)}) custom-call(f32[4,1,2176]{2,1,0:T(1,128)} %copy-done.4), custom_call_target="tpu_custom_call" | custom-call | tf_op jit(solution)/shard_map/norm/pallas_call | solution.py:217
  99.1 6.3 %all-to-all-start.3 = ((f32[16,1,128]{2,1,0:T(1,128)}), f32[16,1,128]{2,1,0:T(1,128)S(1)}, u32[]{:S(2)}, u32[]{:S(2)}) async-start(f32[16,1,128]{2,1,0:T(1,128)} %get-tuple-element.10), calls=%async_computation.3 | async-start | bytes 16384 | tf_op jit(solution)/shard_map/all_to_all | solution.py:227
  105.3 2.6 %fusion.dot_in = f32[1,128]{1,0:T(1,128)} fusion(f32[1]{0:T(128)S(6)} %copy.40, f32[1]{0:T(128)} %bitcast.16, f32[1]{0:T(128)} %bitcast.15, f32[1]{0:T(128)} %bitcast.14), kind=kLoop, calls=%fused_computation.24 | loop fusion | flops 1024 | bytes 528 | tf_op jit(solution)/shard_map/broadcast_in_dim | solution.py:295
  107.9 4.5 %all-to-all-done.3.got = f32[16,1,128]{2,1,0:T(1,128)S(1)} async-done(((f32[16,1,128]{2,1,0:T(1,128)}), f32[16,1,128]{2,1,0:T(1,128)S(1)}, u32[]{:S(2)}, u32[]{:S(2)}) %all-to-all-start.3) | async-done | bytes 8224 | tf_op jit(solution)/shard_map/all_to_all | solution.py:227
  112.4 0.6 copy-done.8
  113.0 1.5 %update.1 = (f32[1,512]{1,0:T(1,128)}, f32[1,512]{1,0:T(1,128)}, f32[1,512]{1,0:T(1,128)}, f32[8,1,512]{2,1,0:T(1,128)}) custom-call(s32[1]{0:T(128)} %bitcast.sizes, f32[16,1,128]{2,1,0:T(1,128)} %copy-done.8, f32[1,2048]{1,0:T(1,128)} %get-tuple-element.11.h_all, f32[1,128]{1,0:T(1,128)} %fusion.dot_in, f32[3,512]{1,0:T(4,128)} %pad_maximum_fusion.3.parts), custom_call_target="tpu_custom_call" | custom-call | tf_op jit(solution)/shard_map/update/pallas_call | solution.py:217
  114.5 10.5 %all_to_all.25 = f32[8,1,512]{2,1,0:T(1,128)S(1)} all-to-all(f32[8,1,512]{2,1,0:T(1,128)} %get-tuple-element.15), channel_id=1, replica_groups=mesh['task'=8,'yh'=4,'z'=8,'core'=2] {'task'}, dimensions={0} | all-to-all | bytes 32768 | tf_op jit(solution)/shard_map/all_to_all | solution.py:227
  125.1 0.6 broadcast_multiply_fusion
  (59 shorter events, 4.5 us)
Async XLA Ops:
  0.6 64.3 %copy-start = (f32[1,32768]{1,0:T(1,128)S(1)}, f32[1,32768]{1,0:T(1,128)}, u32[]{:S(2)}) copy-start(f32[1,32768]{1,0:T(1,128)} %param.18) | copy-start | bytes 393220
  11.3 14.1 %copy-start.9 = (bf16[1,128,16]{1,2,0:T(8,128)(2,1)S(1)}, bf16[1,128,16]{1,2,0:T(8,128)(2,1)}, u32[]{:S(2)}) copy-start(bf16[1,128,16]{1,2,0:T(8,128)(2,1)} %param.12) | copy-start | bytes 12292
  11.3 14.1 %copy-start.1 = (bf16[1,128,2048]{2,1,0:T(8,128)(2,1)S(1)}, bf16[1,128,2048]{2,1,0:T(8,128)(2,1)}, u32[]{:S(2)}) copy-start(bf16[1,128,2048]{2,1,0:T(8,128)(2,1)} %param.16) | copy-start | bytes 1572868
  13.2 7.3 %collective-permute-start.1 = (bf16[272,512]{1,0:T(8,128)(2,1)S(1)}, bf16[272,512]{1,0:T(8,128)(2,1)S(1)}, u32[]{:S(2)}, u32[]{:S(2)}) collective-permute-start(bf16[272,512]{1,0:T(8,128)(2,1)S(1)} %maximum_maximum_fusion.c3), channel_id=1, source_target_pairs={{0,2},{1,3},{16,18},{17,19},{32,34},{33,35},{48,50},{49,51},{2,4},... | collective-permute-start | bytes 835592 | tf_op jit(solution)/shard_map/ppermute | solution.py:273
  14.6 13.5 %collective-permute-start = (bf16[272,512]{1,0:T(8,128)(2,1)S(1)}, bf16[272,512]{1,0:T(8,128)(2,1)S(1)}, u32[]{:S(2)}, u32[]{:S(2)}) collective-permute-start(bf16[272,512]{1,0:T(8,128)(2,1)S(1)} %maximum_maximum_fusion.c3), channel_id=1, source_target_pairs={{12,16},{13,17},{28,32},{29,33},{44,48},{45,49},{10,30},{11,31},{2... | collective-permute-start | bytes 835592 | tf_op jit(solution)/shard_map/ppermute | solution.py:274
  20.5 9.2 %collective-permute-start.2 = (bf16[272,512]{1,0:T(8,128)(2,1)S(1)}, bf16[272,512]{1,0:T(8,128)(2,1)}, u32[]{:S(2)}, u32[]{:S(2)}) collective-permute-start(bf16[272,512]{1,0:T(8,128)(2,1)S(1)} %collective-permute-done.1.c2), channel_id=1, source_target_pairs={{0,2},{1,3},{16,18},{17,19},{32,34},{33,35},{48,50},{49,51},{2,4},... | collective-permute-start | bytes 835592 | tf_op jit(solution)/shard_map/ppermute | solution.py:275
  25.8 1.0 copy-start.2
  30.7 14.9 %collective-permute-start.3 = (bf16[272,512]{1,0:T(8,128)(2,1)S(1)}, bf16[272,512]{1,0:T(8,128)(2,1)S(1)}, u32[]{:S(2)}, u32[]{:S(2)}) collective-permute-start(bf16[272,512]{1,0:T(8,128)(2,1)S(1)} %get-tuple-element.24), channel_id=1, source_target_pairs={{0,2},{1,3},{16,18},{17,19},{32,34},{33,35},{48,50},{49,51},{2,4},... | collective-permute-start | bytes 835592 | tf_op jit(solution)/shard_map/ppermute | solution.py:277
  36.0 5.8 %copy-start.7 = (bf16[1,16,2048]{2,1,0:T(8,128)(2,1)S(1)}, bf16[1,16,2048]{2,1,0:T(8,128)(2,1)}, u32[]{:S(2)}) copy-start(bf16[1,16,2048]{2,1,0:T(8,128)(2,1)} %param.13) | copy-start | bytes 196612
  36.0 6.6 %copy-start.5 = (f32[1,32768]{1,0:T(1,128)S(1)}, f32[1,32768]{1,0:T(1,128)}, u32[]{:S(2)}) copy-start(f32[1,32768]{1,0:T(1,128)} %param.19) | copy-start | bytes 393220
  36.0 6.6 %copy-start.6 = (f32[1,32768]{1,0:T(1,128)S(1)}, f32[1,32768]{1,0:T(1,128)}, u32[]{:S(2)}) copy-start(f32[1,32768]{1,0:T(1,128)} %param.20) | copy-start | bytes 393220
  36.0 9.6 %all-to-all-start = ((bf16[2,128,2176]{2,1,0:T(8,128)(2,1)}), bf16[2,128,2176]{2,1,0:T(8,128)(2,1)S(1)}, u32[]{:S(2)}, u32[]{:S(2)}) async-start(bf16[2,128,2176]{2,1,0:T(8,128)(2,1)} %pad_maximum_fusion), calls=%async_computation | async-start | bytes 2228224 | tf_op jit(solution)/shard_map/all_to_all | solution.py:227
  57.3 14.8 %all-to-all-start.1 = ((f32[8,1,2176]{2,1,0:T(1,128)}), f32[8,1,2176]{2,1,0:T(1,128)S(1)}, u32[]{:S(2)}, u32[]{:S(2)}) async-start(f32[8,1,2176]{2,1,0:T(1,128)} %reshape.78), calls=%async_computation.1 | async-start | bytes 139264 | tf_op jit(solution)/shard_map/all_to_all | solution.py:227
  72.2 0.6 copy-start.3
  74.3 22.7 %all-to-all-start.2 = ((f32[4,1,2176]{2,1,0:T(1,128)}), f32[4,1,2176]{2,1,0:T(1,128)S(1)}, u32[]{:S(2)}, u32[]{:S(2)}) async-start(f32[4,1,2176]{2,1,0:T(1,128)} %row_sum.1), calls=%async_computation.2 | async-start | bytes 69632 | tf_op jit(solution)/shard_map/all_to_all | solution.py:227
  97.0 0.6 copy-start.4
  99.1 13.3 %all-to-all-start.3 = ((f32[16,1,128]{2,1,0:T(1,128)}), f32[16,1,128]{2,1,0:T(1,128)S(1)}, u32[]{:S(2)}, u32[]{:S(2)}) async-start(f32[16,1,128]{2,1,0:T(1,128)} %get-tuple-element.10), calls=%async_computation.3 | async-start | bytes 16384 | tf_op jit(solution)/shard_map/all_to_all | solution.py:227
  112.4 0.6 copy-start.8

commit v3 on v2

v3 whole, which is shorter than its diff:
```python
import math

import jax
import jax.numpy as jnp
from jax import lax
from jax.experimental import pallas as pl
from jax.experimental.pallas import tpu as pltpu
from jax.sharding import Mesh
from jax.sharding import PartitionSpec as P

HEAD_DIM = 128
RANK = 16
BLOCK = 128
CHUNK = 2 * BLOCK
SPAN = 3
WINDOW = 7 * BLOCK
GROUPS = 2
PER_GROUP = 4
HALF = GROUPS * PER_GROUP * HEAD_DIM
KHALF = GROUPS * HEAD_DIM
GFEAT = PER_GROUP * HEAD_DIM
ROW = GFEAT + 128
SEG_ROWS = 16
F32 = jnp.float32
BF16 = jnp.bfloat16
CTX = ("yh", "z", "core")
NT = (((1,), (1,)), ((), ()))
NN = (((1,), (0,)), ((), ()))


def dot(a, b, dims=NN):
    return lax.dot_general(a, b, dims, preferred_element_type=F32)


def fold(x):
    return x.reshape(x.shape[0] // 8, 8, x.shape[1])


def pack_kernel(keys, values, seg, out):
    n = keys.shape[1]
    out[:BLOCK, :n] = keys[...]
    out[:BLOCK, n:] = values[...]
    first = lax.broadcasted_iota(jnp.int32, (SEG_ROWS, BLOCK), 0) == 0
    row = jnp.where(first, jnp.broadcast_to(seg[...] + 1, (SEG_ROWS, BLOCK)), 0).astype(F32)
    out[BLOCK:, :BLOCK] = row.astype(BF16)
    out[BLOCK:, BLOCK:] = jnp.zeros((SEG_ROWS, out.shape[1] - BLOCK), BF16)


def attend_kernel(
    core_ref, qg, c0, c1, c2, c3, up, dmat, rmat, out, keys, keys_t, vals, qs, ts, at, qaug, s_ref, t_ref, u_ref, c_ref
):
    chunks = (c0, c1, c2, c3)
    core = core_ref[0]
    a_pad = qg[:, 2 * HALF : 2 * HALF + 128]
    a = a_pad[:, :RANK]
    qs[...] = (qg[:, :HALF].astype(F32) + dot(a, up[...])).astype(BF16)
    d = dmat[...]
    d1 = d.astype(BF16)
    rest = d - d1.astype(F32)
    d2 = rest.astype(BF16)
    d3 = (rest - d2.astype(F32)).astype(BF16)
    ts[...] = (dot(a, d1) + dot(a, d2) + dot(a, d3)).astype(BF16)
    at[...] = jnp.transpose(a_pad.astype(F32))[:RANK].astype(BF16)
    lane = lax.broadcasted_iota(jnp.int32, (BLOCK, BLOCK), 1).astype(F32)
    for j, c in enumerate(chunks):
        for half in range(2):
            rows = slice((j * 2 + half) * BLOCK, (j * 2 + half + 1) * BLOCK)
            seg_row = c[half, BLOCK:, :BLOCK].astype(F32)[0:1]
            seg = jnp.transpose(jnp.broadcast_to(seg_row, (BLOCK, BLOCK)))
            hit = seg == lane
            for g in range(GROUPS):
                col = pl.multiple_of((g * 2 + core) * HEAD_DIM, HEAD_DIM)
                k = c[half, :BLOCK, pl.ds(col, HEAD_DIM)]
                keys[g, rows, :HEAD_DIM] = k
                keys[g, rows, HEAD_DIM:] = jnp.where(hit, 1.0, 0.0).astype(BF16)
                keys_t[g, :, rows] = jnp.transpose(k.astype(F32)).astype(BF16)
                vals[g, rows, :] = c[half, :BLOCK, pl.ds(2 * KHALF + col, HEAD_DIM)]
            if j == 3:
                qaug[half] = jnp.where(hit, 0.0, -1e30).astype(BF16)
    tri = jnp.where(lax.broadcasted_iota(jnp.int32, (BLOCK, BLOCK), 0) <= lax.broadcasted_iota(jnp.int32, (BLOCK, BLOCK), 1), 0.0, -1e30)
    cexp = HEAD_DIM**-0.5 * math.log2(math.e)
    steps = [(g, b, pair) for g in range(GROUPS) for b in range(2) for pair in range(2)]

    def scores(n):
        g, b, pair = steps[n]
        slot = n % 3
        win = slice(b * BLOCK, b * BLOCK + WINDOW)
        own = slice(b * BLOCK, (b + 1) * BLOCK)

        def two(ref, base):
            cols = [base + g * GFEAT + (pair * 2 + e) * HEAD_DIM for e in range(2)]
            return [ref[own, col : col + HEAD_DIM] for col in cols]

        q2 = [jnp.concatenate([q, qaug[b]], axis=1) for q in two(qs, 0)]
        s_ref[slot] = dot(keys[g, win, :], jnp.concatenate(q2, axis=0), NT)
        t_ref[slot] = dot(keys[g, win, :HEAD_DIM], jnp.concatenate(two(ts, 0), axis=0), NT)
        u_ref[slot] = dot(vals[g, win, :], jnp.concatenate(two(qg, HALF), axis=0), NT)

    def weigh(n):
        slot = n % 3
        scales = []
        for e in range(2):
            lanes = slice(e * BLOCK, (e + 1) * BLOCK)
            m8 = None
            for w in range(6, -1, -1):
                rows = slice(w * BLOCK, (w + 1) * BLOCK)
                s = s_ref[slot, rows, lanes]
                if w == 6:
                    s = s + tri
                top = jnp.max(fold(s), axis=0)
                m8 = top if m8 is None else jnp.maximum(m8, top)
            m = jnp.max(m8, axis=0, keepdims=True)
            z8 = et8 = eu8 = etu8 = jnp.zeros((8, BLOCK), F32)
            for w in range(7):
                rows = slice(w * BLOCK, (w + 1) * BLOCK)
                s = s_ref[slot, rows, lanes]
                if w == 6:
                    s = s + tri
                ex = jnp.exp2((s - m) * cexp)
                s_ref[slot, rows, lanes] = ex
                et = ex * t_ref[slot, rows, lanes]
                u = u_ref[slot, rows, lanes]
                z8 = z8 + jnp.sum(fold(ex), axis=0)
                et8 = et8 + jnp.sum(fold(et), axis=0)
                eu8 = eu8 + jnp.sum(fold(ex * u), axis=0)
                etu8 = etu8 + jnp.sum(fold(et * u), axis=0)
            inv = 1.0 / jnp.sum(z8, axis=0, keepdims=True)
            mt = jnp.sum(et8, axis=0, keepdims=True) * inv
            mu = jnp.sum(eu8, axis=0, keepdims=True) * inv
            cov = jnp.sum(etu8, axis=0, keepdims=True) * inv - mt * mu
            for w in range(7):
                rows = slice(w * BLOCK, (w + 1) * BLOCK)
                coef = s_ref[slot, rows, lanes] * (
                    (t_ref[slot, rows, lanes] - mt) * (u_ref[slot, rows, lanes] - mu) - cov
                )
                c_ref[slot, rows, lanes] = coef.astype(BF16)
            scales.append(inv * (1.0 / HEAD_DIM))
        return scales

    def gather(n, scales):
        g, b, pair = steps[n]
        slot = n % 3
        hv = dot(keys_t[g, :, b * BLOCK : b * BLOCK + WINDOW], c_ref[slot])
        ab = at[:, b * BLOCK : (b + 1) * BLOCK]
        for e in range(2):
            lanes = slice(e * BLOCK, (e + 1) * BLOCK)
            head = (hv[:, lanes] * scales[e]).astype(BF16)
            left = g * ROW + (pair * 2 + e) * HEAD_DIM
            cols = slice(left, left + HEAD_DIM)
            part = dot(ab, head, NT)
            if b == 0:
                out[:, cols] = part
            else:
                out[:, cols] += part

    scores(0)
    for n in range(8):
        if n < 7:
            scores(n + 1)
        gather(n, weigh(n))
    dh = rh = jnp.zeros((1, 1), F32)
    for g in range(GROUPS):
        h = out[:, g * ROW : g * ROW + GFEAT]
        cols = slice(g * GFEAT, (g + 1) * GFEAT)
        dh = dh + jnp.sum(h * d[:, cols], keepdims=True)
        rh = rh + jnp.sum(h * rmat[:, cols], keepdims=True)
    lane = lax.broadcasted_iota(jnp.int32, (RANK, 128), 1)
    tail = jnp.where(lane == 0, dh, jnp.where(lane == 1, rh, 0.0))
    for g in range(GROUPS):
        out[:, g * ROW + GFEAT : (g + 1) * ROW] = tail


def attend(core, qg, chunks, up, dmat, rmat):
    vm = pltpu.VMEM
    return pl.pallas_call(
        attend_kernel,
        out_shape=jax.ShapeDtypeStruct((RANK, GROUPS * ROW), F32),
        in_specs=[pl.BlockSpec(memory_space=pltpu.SMEM)] + [pl.BlockSpec(memory_space=vm)] * 8,
        out_specs=pl.BlockSpec(memory_space=vm),
        scratch_shapes=[
            vm((GROUPS, 4 * CHUNK, 2 * HEAD_DIM), BF16),
            vm((GROUPS, HEAD_DIM, 4 * CHUNK), BF16),
            vm((GROUPS, 4 * CHUNK, HEAD_DIM), BF16),
            vm((CHUNK, HALF), BF16),
            vm((CHUNK, HALF), BF16),
            vm((RANK, CHUNK), BF16),
            vm((2, BLOCK, BLOCK), BF16),
            vm((3, WINDOW, CHUNK), F32),
            vm((3, WINDOW, CHUNK), F32),
            vm((3, WINDOW, CHUNK), F32),
            vm((3, WINDOW, CHUNK), BF16),
        ],
        compiler_params=pltpu.CompilerParams(vmem_limit_bytes=48 * 1024 * 1024),
        cost_estimate=pl.CostEstimate(flops=2_000_000_000, bytes_accessed=4_000_000, transcendentals=2_000_000),
        name="attend",
    )(core, qg, *chunks, up, dmat, rmat)


def norm_kernel(got, h_out, out):
    total = jnp.sum(got[...], axis=0)
    h = total[:, : h_out.shape[1]]
    h_out[...] = h
    tail = total[:, h_out.shape[1] :]
    lane = lax.broadcasted_iota(jnp.int32, tail.shape, 1)
    share = 2.0 / out.shape[0]
    row = jnp.where(lane == 2, jnp.sum(h * h, keepdims=True), tail * share)
    out[...] = jnp.broadcast_to(row[None], out.shape)


def update_kernel(got, h_all, dot_in, parts, new_solution, new_residual, new_direction, spread):
    total = jnp.sum(got[...], axis=0)
    lane = lax.broadcasted_iota(jnp.int32, total.shape, 1)

    def pick(row, k):
        return jnp.sum(jnp.where(lane == k, row, 0.0), keepdims=True)

    dh, rh, hh = pick(total, 0), pick(total, 1), pick(total, 2)
    consts = dot_in[...]
    rr, dd, rd, damp = (pick(consts, k) for k in range(4))
    h = h_all[...]
    sol, res, dirn = parts[0:1], parts[1:2], parts[2:3]
    step_len = rr / (dd + dh / damp)
    curved = dirn + h / damp
    rc = rd + rh / damp
    cc = dd + 2.0 * dh / damp + hh / (damp * damp)
    new_norm = rr - 2.0 * step_len * rc + step_len * step_len * cc
    ns = sol + step_len * dirn
    nr = res - step_len * curved
    new_solution[...] = ns
    new_residual[...] = nr
    new_direction[...] = nr + (new_norm / rr) * dirn
    spread[...] = jnp.broadcast_to(ns[None], spread.shape)


def in_vmem(kernel, out_shapes, *args, name, dtype=F32):
    return pl.pallas_call(
        kernel,
        out_shape=[jax.ShapeDtypeStruct(s, dtype) for s in out_shapes],
        in_specs=[pl.BlockSpec(memory_space=pltpu.VMEM)] * len(args),
        out_specs=[pl.BlockSpec(memory_space=pltpu.VMEM)] * len(out_shapes),
        name=name,
    )(*args)


def exchange(x, axes):
    return lax.all_to_all(x, axes, 0, 0, tiled=True)


def spot(yh, z, core, n_z):
    return (yh * n_z + z) * 2 + core


def moves(n_yh, n_z, kinds):
    pairs = []
    for source, target, up in kinds:
        for yh in range(n_yh - up):
            for core in range(2):
                pairs.append((spot(yh, source, core, n_z), spot(yh + up, target, core, n_z)))
    return pairs


def per_core(x):
    rows, _, _, n = x.shape
    return x.transpose(2, 0, 1, 3).reshape(2, rows, 2 * n)


def per_device(
    base_queries, adapter_input, adapter_up_weight, projected_keys, projected_values, output_gradient,
    segments, solution, residual, direction, damping,
):
    core, z = lax.axis_index("core"), lax.axis_index("z")
    n_yh, n_z, n_task = lax.axis_size("yh"), lax.axis_size("z"), lax.axis_size("task")
    idx = lax.axis_index(CTX)

    def core_part(x):
        rows, feats = x.shape[0], x.shape[1] // 4
        x = x.reshape(rows, 2, 2, feats)
        return lax.dynamic_index_in_dim(x, core, 2, keepdims=False).reshape(rows, 2 * feats)

    last = n_z - 1
    row = [(i, i + 1, 0) for i in range(last)]

    def move(x, *kinds):
        return lax.ppermute(x, CTX, moves(n_yh, n_z, kinds))

    (own,) = in_vmem(
        pack_kernel, [(BLOCK + SEG_ROWS, 4 * KHALF)], projected_keys[0], projected_values[0], segments, name="pack", dtype=BF16
    )
    first = move(own, *row, (last, 0, 1))
    cross = move(own, (last - 1, last, 1), (last - 2, last - 1, 1))
    second = move(jnp.where(z == last, cross, first), *row, (last, 0, 0))
    cross = move(cross, (last - 1, last, 0))
    third = move(jnp.where(z == last, cross, second), *row, (last, 0, 0))
    chunks = [lax.all_gather(x, "core") for x in (third, second, first, own)]

    pad = jnp.pad(adapter_input[0], ((0, 0), (0, 128 - RANK)))
    qg = jnp.concatenate(
        [
            per_core(base_queries[0].reshape(BLOCK, 2, 2, GFEAT)),
            per_core(output_gradient[0].reshape(BLOCK, 2, 2, GFEAT)),
            jnp.broadcast_to(pad[None], (2, BLOCK, 128)),
        ],
        axis=2,
    )
    qg = exchange(qg, "core").reshape(CHUNK, 2 * HALF + 128)

    up, dmat, rmat = (core_part(x.reshape(RANK, 2 * HALF)) for x in (adapter_up_weight[0], direction[0], residual[0]))
    size = direction.shape[1] // (n_yh * n_z * 2)
    parts = jnp.concatenate([lax.dynamic_slice_in_dim(x, idx * size, size, 1) for x in (solution, residual, direction)])
    consts = jnp.stack([jnp.sum(residual * residual), jnp.sum(direction * direction), jnp.sum(residual * direction), damping[0]])
    consts = jnp.pad(consts, (0, 124))[None]

    terms = attend(core.reshape(1), qg, chunks, up, dmat, rmat)

    peers = n_yh * n_z
    h, scalars = in_vmem(
        norm_kernel, [(1, GFEAT), (2 * peers, 1, 128)], exchange(terms.reshape(peers, 1, ROW), ("yh", "z")), name="norm"
    )
    new_solution, new_residual, new_direction, spread = in_vmem(
        update_kernel, [(1, size)] * 3 + [(n_task, 1, size)], exchange(scalars, CTX), h, consts, parts, name="update"
    )
    meta_gradient = jnp.sum(exchange(spread, "task"), axis=(0, 1)) / n_task
    return new_solution, new_residual, new_direction, meta_gradient


def solution(mesh):
    n_task, n_ctx = mesh.devices.shape
    split = Mesh(mesh.devices.reshape(n_task, n_ctx // 16, 8, 2), ("task",) + CTX)
    tokens = P("task", CTX, None)
    whole = P("task", None)
    in_specs = (tokens, tokens, P("task", None, None), tokens, tokens, tokens, P("task", CTX), whole, whole, whole, P("task"))
    out_specs = (P("task", CTX), P("task", CTX), P("task", CTX), P(CTX))
    return jax.shard_map(per_device, mesh=split, in_specs=in_specs, out_specs=out_specs, check_vma=False)
```

time: 126 us -> 123 us (0.976)
  starting transfers between devices: 46.6 us -> 33.4 us
  waiting for transfers between devices: 24 us -> 35.3 us
  other arithmetic: 9.95 us -> 7.43 us
  blocking collectives: 19.3 us -> 20.9 us
    all_to_all x4 -> x3, starting transfers between devices: 35.6 us -> 22.6 us  [exchange(): return lax.all_to_all(x, axes, 0, 0, tiled=True)]
    ppermute x4 -> x5, waiting for transfers between devices: 6.88 us -> 16.1 us  [move(): return lax.ppermute(x, CTX, moves(n_yh, n_z, kinds))]
    all_gather x1 -> x4, blocking collectives: 8.73 us -> 11.8 us  [per_device(): chunks = [lax.all_gather(x, 'core') for x in (third, second, first, own)]]
    all_to_all x4 -> x3, waiting for transfers between devices: 17.1 us -> 19.2 us  [exchange(): return lax.all_to_all(x, axes, 0, 0, tiled=True)]
    dynamic_slice x3 -> x2, local copies, waits for them, and re-layouts: 2.42 us -> 0.64 us  [core_part(): lax.dynamic_index_in_dim(x, core, 2, keepdims=False)]
    all_to_all x1, blocking collectives: 10.5 us -> 9.07 us  [exchange(): return lax.all_to_all(x, axes, 0, 0, tiled=True)]
    pallas_call x4, Pallas kernels: 15.4 us -> 14.2 us  [the longest x1 9.17 us: attend(): pl.pallas_call(attend_kernel, out_shape=jax.ShapeDtypeStruct((RANK, GROUP...]
    unnamed x28 -> x27, local copies, waits for them, and re-layouts: 2.83 us -> 3.94 us
  transfers between devices with their start and end apart: 8 -> 8, of which waited for: 5 -> 4; matrix products, arithmetic and copies ran while one was open for 8% -> 11% of each run, Pallas kernels for 0% -> 0%
where the time goes in v3:
time: 123 us; the launch traced here: 122 us
  waiting for transfers between devices  35.3 us (29%)
  starting transfers between devices  33.4 us (27%)
  blocking collectives  20.9 us (17%)
  Pallas kernels  14.2 us (12%)
  local copies, waits for them, and re-layouts  9.41 us (8%)
  other arithmetic  7.43 us (6%)
  between operations  1.53 us (1%)
    all_to_all x3, starting transfers between devices, exchange(): return lax.all_to_all(x, axes, 0, 0, tiled=True)  22.6 us
    all_to_all x3, waiting for transfers between devices, exchange(): return lax.all_to_all(x, axes, 0, 0, tiled=True)  19.2 us
    ppermute x5, waiting for transfers between devices, move(): return lax.ppermute(x, CTX, moves(n_yh, n_z, kinds))  16.1 us
    all_gather x4, blocking collectives, per_device(): chunks = [lax.all_gather(x, 'core') for x in (third, second, first, own)]  11.8 us
    ppermute x5, starting transfers between devices, move(): return lax.ppermute(x, CTX, moves(n_yh, n_z, kinds))  10.9 us
    pallas_call x1, Pallas kernels, attend(): pl.pallas_call(attend_kernel, out_shape=jax.ShapeDtypeStruct((RANK, GROUP...  9.17 us
    all_to_all x1, blocking collectives, exchange(): return lax.all_to_all(x, axes, 0, 0, tiled=True)  9.07 us
    pallas_call x3, Pallas kernels, in_vmem(): pl.pallas_call(kernel, out_shape=[jax.ShapeDtypeStruct(s, dtype) for s in...  5.01 us
  transfers between devices with their start and end apart: 8, of which 4 were waited for; matrix products, arithmetic and copies ran while one was open for 11% of the time, Pallas kernels for 0%

profile of v3, /device:TPU:1, one launch (start us, length us, event | category | flops | bytes accessed | tf_op | source)
XLA Modules:
  0.0 122.2 jit_solution(16571653989716535331)
XLA Ops:
  0.6 1.7 %pack.1 = bf16[144,1024]{1,0:T(8,128)(2,1)} custom-call(bf16[128,512]{1,0:T(8,128)(2,1)} %bitcast.34, bf16[128,512]{1,0:T(8,128)(2,1)} %bitcast.35, s32[1,128]{1,0:T(1,128)} %seg.1), custom_call_target="tpu_custom_call" | custom-call | tf_op jit(solution)/shard_map/pack/pallas_call | solution.py:236
  2.4 0.7 collective-permute-start
  3.1 4.8 %collective-permute-start.2 = (bf16[144,1024]{1,0:T(8,128)(2,1)}, bf16[144,1024]{1,0:T(8,128)(2,1)S(1)}, u32[]{:S(2)}, u32[]{:S(2)}) collective-permute-start(bf16[144,1024]{1,0:T(8,128)(2,1)} %pack.1), channel_id=1, source_target_pairs={{0,2},{1,3},{16,18},{17,19},{32,34},{33,35},{48,50},{49,51},{2,4},... | collective-permute-start | bytes 884744 | tf_op jit(solution)/shard_map/ppermute | solution.py:284
  7.9 0.8 copy.24
  8.7 1.4 %reshape_squeeze.10 = bf16[128,2,2,512]{3,2,1,0:T(2,128)(2,1)S(1)} reshape(bf16[1,128,2048]{2,1,0:T(8,128)(2,1)} %param.16) | data formatting | bytes 1048576 | tf_op jit(solution)/shard_map/reshape;squeeze | solution.py:300
  12.4 1.1 pad_maximum_fusion
  13.5 7.1 %all-to-all-start = ((bf16[2,128,2176]{2,1,0:T(8,128)(2,1)}), bf16[2,128,2176]{2,1,0:T(8,128)(2,1)S(1)}, u32[]{:S(2)}, u32[]{:S(2)}) async-start(bf16[2,128,2176]{2,1,0:T(8,128)(2,1)} %pad_maximum_fusion), calls=%async_computation | async-start | bytes 2228224 | tf_op jit(solution)/shard_map/all_to_all | solution.py:246
  20.6 2.1 %collective-permute-start.3 = (bf16[144,1024]{1,0:T(8,128)(2,1)S(1)}, bf16[144,1024]{1,0:T(8,128)(2,1)S(1)}, u32[]{:S(2)}, u32[]{:S(2)}) collective-permute-start(bf16[144,1024]{1,0:T(8,128)(2,1)S(1)} %broadcast_select_fusion.1), channel_id=1, source_target_pairs={{0,2},{1,3},{16,18},{17,19},{32,34},{33,35},{48,50},{49,51},{2,4},... | collective-permute-start | bytes 884744 | tf_op jit(solution)/shard_map/ppermute | solution.py:284
  22.6 1.4 %collective-permute-start.1 = (bf16[144,1024]{1,0:T(8,128)(2,1)S(1)}, bf16[144,1024]{1,0:T(8,128)(2,1)}, u32[]{:S(2)}, u32[]{:S(2)}) collective-permute-start(bf16[144,1024]{1,0:T(8,128)(2,1)S(1)} %collective-permute-done), channel_id=1, source_target_pairs={{12,14},{13,15},{28,30},{29,31},{44,46},{45,47},{60,62},{61,63},{7... | collective-permute-start | bytes 884744 | tf_op jit(solution)/shard_map/ppermute | solution.py:284
  24.5 2.5 %multiply_reduce_fusion.2 = (f32[]{:T(128)}, f32[32768]{0:T(1024)S(1)}, f32[]{:T(128)}, f32[]{:T(128)}, f32[32768]{0:T(1024)S(1)}) fusion(f32[1,32768]{1,0:T(1,128)S(1)} %copy-done.5, f32[]{:T(128)} %broadcast.25, f32[1,32768]{1,0:T(1,128)S(1)} %copy-done.6), kind=kLoop, calls=%fused_computation.5 | loop fusion | flops 196605 | bytes 524304 | tf_op jit(solution)/shard_map/reduce_sum | solution.py:310
  27.9 0.6 constant_dynamic-slice_fusion
  28.5 2.2 %all-gather.3 = bf16[288,1024]{1,0:T(8,128)(2,1)S(1)} all-gather(bf16[144,1024]{1,0:T(8,128)(2,1)S(1)} %copy-done.2), channel_id=5, replica_groups=mesh['task'=8,'yh'=4,'z'=8,'core'=2] {'core'}, dimensions={0}, use_global_device_ids=true | all-gather | bytes 884736 | tf_op jit(solution)/shard_map/all_gather | solution.py:294
  30.7 3.0 %collective-permute-done.3 = bf16[144,1024]{1,0:T(8,128)(2,1)S(1)} collective-permute-done((bf16[144,1024]{1,0:T(8,128)(2,1)S(1)}, bf16[144,1024]{1,0:T(8,128)(2,1)S(1)}, u32[]{:S(2)}, u32[]{:S(2)}) %collective-permute-start.3) | collective-permute-done | bytes 294944 | tf_op jit(solution)/shard_map/ppermute | solution.py:284
  33.8 1.9 %collective-permute-start.4 = (bf16[144,1024]{1,0:T(8,128)(2,1)S(1)}, bf16[144,1024]{1,0:T(8,128)(2,1)S(1)}, u32[]{:S(2)}, u32[]{:S(2)}) collective-permute-start(bf16[144,1024]{1,0:T(8,128)(2,1)S(1)} %broadcast_select_fusion), channel_id=1, source_target_pairs={{0,2},{1,3},{16,18},{17,19},{32,34},{33,35},{48,50},{49,51},{2,4},... | collective-permute-start | bytes 884744 | tf_op jit(solution)/shard_map/ppermute | solution.py:284
  35.7 4.0 %all-gather.2 = bf16[288,1024]{1,0:T(8,128)(2,1)S(1)} all-gather(bf16[144,1024]{1,0:T(8,128)(2,1)S(1)} %collective-permute-done.2), channel_id=4, replica_groups=mesh['task'=8,'yh'=4,'z'=8,'core'=2] {'core'}, dimensions={0}, use_global_device_ids=true | all-gather | bytes 884736 | tf_op jit(solution)/shard_map/all_gather | solution.py:294
  39.8 2.2 %all-gather.1 = bf16[288,1024]{1,0:T(8,128)(2,1)S(1)} all-gather(bf16[144,1024]{1,0:T(8,128)(2,1)S(1)} %collective-permute-done.3), channel_id=3, replica_groups=mesh['task'=8,'yh'=4,'z'=8,'core'=2] {'core'}, dimensions={0}, use_global_device_ids=true | all-gather | bytes 884736 | tf_op jit(solution)/shard_map/all_gather | solution.py:294
  42.0 13.1 %collective-permute-done.4 = bf16[144,1024]{1,0:T(8,128)(2,1)S(1)} collective-permute-done((bf16[144,1024]{1,0:T(8,128)(2,1)S(1)}, bf16[144,1024]{1,0:T(8,128)(2,1)S(1)}, u32[]{:S(2)}, u32[]{:S(2)}) %collective-permute-start.4) | collective-permute-done | bytes 294944 | tf_op jit(solution)/shard_map/ppermute | solution.py:284
  55.1 3.3 %all-gather = bf16[288,1024]{1,0:T(8,128)(2,1)} all-gather(bf16[144,1024]{1,0:T(8,128)(2,1)S(1)} %collective-permute-done.4), channel_id=2, replica_groups=mesh['task'=8,'yh'=4,'z'=8,'core'=2] {'core'}, dimensions={0}, use_global_device_ids=true | all-gather | bytes 884736 | tf_op jit(solution)/shard_map/all_gather | solution.py:294
  58.4 1.1 copy-done.1
  59.5 9.2 %attend.1 = f32[16,1280]{1,0:T(8,128)S(1)} custom-call(s32[1]{0:T(128)} %bitcast.core_ref, bf16[256,2176]{1,0:T(8,128)(2,1)S(1)} %bitcast.22, bf16[2,144,1024]{2,1,0:T(8,128)(2,1)S(1)} %bitcast.26, bf16[2,144,1024]{2,1,0:T(8,128)(2,1)S(1)} %bitcast.25, bf16[2,144,1024]{2,1,0:T(8,128)(2,1)S(1)} %bitcast.24, bf16[2,144,1024]{2,1,0:T(8,128)(2,1)S(1)} %bitcast.23, ...), custom_call_target="tpu_custom_call" | custom-call | flops 2000000000 | bytes 4000000 | tf_op jit(solution)/shard_map/attend/pallas_call | solution.py:175
  68.7 0.7 reshape.43
  69.4 9.8 %all-to-all-start.1 = ((f32[32,1,640]{2,1,0:T(1,128)}), f32[32,1,640]{2,1,0:T(1,128)S(1)}, u32[]{:S(2)}, u32[]{:S(2)}) async-start(f32[32,1,640]{2,1,0:T(1,128)} %reshape.43), calls=%async_computation.1 | async-start | bytes 163840 | tf_op jit(solution)/shard_map/all_to_all | solution.py:246
  79.8 0.6 pad_maximum_fusion.1.parts
  80.4 10.0 %all-to-all-done.1.got = f32[32,1,640]{2,1,0:T(1,128)S(1)} async-done(((f32[32,1,640]{2,1,0:T(1,128)}), f32[32,1,640]{2,1,0:T(1,128)S(1)}, u32[]{:S(2)}, u32[]{:S(2)}) %all-to-all-start.1) | async-done | bytes 81952 | tf_op jit(solution)/shard_map/all_to_all | solution.py:246
  90.4 0.6 copy-done.4
  91.0 1.7 %norm.1 = (f32[1,512]{1,0:T(1,128)}, f32[64,1,128]{2,1,0:T(1,128)}) custom-call(f32[32,1,640]{2,1,0:T(1,128)} %copy-done.4), custom_call_target="tpu_custom_call" | custom-call | tf_op jit(solution)/shard_map/norm/pallas_call | solution.py:236
  92.7 5.8 %all-to-all-start.2 = ((f32[64,1,128]{2,1,0:T(1,128)}), f32[64,1,128]{2,1,0:T(1,128)S(1)}, u32[]{:S(2)}, u32[]{:S(2)}) async-start(f32[64,1,128]{2,1,0:T(1,128)} %get-tuple-element.10), calls=%async_computation.2 | async-start | bytes 65536 | tf_op jit(solution)/shard_map/all_to_all | solution.py:246
  98.5 2.6 %fusion.dot_in = f32[1,128]{1,0:T(1,128)} fusion(f32[1]{0:T(128)S(6)} %copy.28, f32[1]{0:T(128)} %bitcast.13, f32[1]{0:T(128)} %bitcast.12, f32[1]{0:T(128)} %bitcast.11), kind=kLoop, calls=%fused_computation.15 | loop fusion | flops 1024 | bytes 528 | tf_op jit(solution)/shard_map/broadcast_in_dim | solution.py:311
  101.1 9.2 %all-to-all-done.2.got = f32[64,1,128]{2,1,0:T(1,128)S(1)} async-done(((f32[64,1,128]{2,1,0:T(1,128)}), f32[64,1,128]{2,1,0:T(1,128)S(1)}, u32[]{:S(2)}, u32[]{:S(2)}) %all-to-all-start.2) | async-done | bytes 32800 | tf_op jit(solution)/shard_map/all_to_all | solution.py:246
  110.3 0.6 copy-done.7
  110.9 1.6 %update.1 = (f32[1,512]{1,0:T(1,128)}, f32[1,512]{1,0:T(1,128)}, f32[1,512]{1,0:T(1,128)}, f32[8,1,512]{2,1,0:T(1,128)}) custom-call(f32[64,1,128]{2,1,0:T(1,128)} %copy-done.7, f32[1,512]{1,0:T(1,128)} %get-tuple-element.11.h_all, f32[1,128]{1,0:T(1,128)} %fusion.dot_in, f32[3,512]{1,0:T(4,128)} %pad_maximum_fusion.1.parts), custom_call_target="tpu_custom_call" | custom-call | tf_op jit(solution)/shard_map/update/pallas_call | solution.py:236
  112.5 9.1 %all_to_all.20 = f32[8,1,512]{2,1,0:T(1,128)S(1)} all-to-all(f32[8,1,512]{2,1,0:T(1,128)} %get-tuple-element.15), channel_id=1, replica_groups=mesh['task'=8,'yh'=4,'z'=8,'core'=2] {'task'}, dimensions={0} | all-to-all | bytes 32768 | tf_op jit(solution)/shard_map/all_to_all | solution.py:246
  (44 shorter events, 4.3 us)
Async XLA Ops:
  0.6 78.5 %copy-start = (f32[1,32768]{1,0:T(1,128)S(1)}, f32[1,32768]{1,0:T(1,128)}, u32[]{:S(2)}) copy-start(f32[1,32768]{1,0:T(1,128)} %param.18) | copy-start | bytes 393220
  2.4 18.1 %collective-permute-start = (bf16[144,1024]{1,0:T(8,128)(2,1)}, bf16[144,1024]{1,0:T(8,128)(2,1)S(1)}, u32[]{:S(2)}, u32[]{:S(2)}) collective-permute-start(bf16[144,1024]{1,0:T(8,128)(2,1)} %pack.1), channel_id=1, source_target_pairs={{12,30},{13,31},{28,46},{29,47},{44,62},{45,63},{10,28},{11,29},{2... | collective-permute-start | bytes 884744 | tf_op jit(solution)/shard_map/ppermute | solution.py:284
  3.1 17.5 %collective-permute-start.2 = (bf16[144,1024]{1,0:T(8,128)(2,1)}, bf16[144,1024]{1,0:T(8,128)(2,1)S(1)}, u32[]{:S(2)}, u32[]{:S(2)}) collective-permute-start(bf16[144,1024]{1,0:T(8,128)(2,1)} %pack.1), channel_id=1, source_target_pairs={{0,2},{1,3},{16,18},{17,19},{32,34},{33,35},{48,50},{49,51},{2,4},... | collective-permute-start | bytes 884744 | tf_op jit(solution)/shard_map/ppermute | solution.py:284
  10.2 1.0 copy-start.3
  13.5 11.1 %copy-start.5 = (f32[1,32768]{1,0:T(1,128)S(1)}, f32[1,32768]{1,0:T(1,128)}, u32[]{:S(2)}) copy-start(f32[1,32768]{1,0:T(1,128)} %param.19) | copy-start | bytes 393220
  13.5 11.1 %copy-start.6 = (f32[1,32768]{1,0:T(1,128)S(1)}, f32[1,32768]{1,0:T(1,128)}, u32[]{:S(2)}) copy-start(f32[1,32768]{1,0:T(1,128)} %param.20) | copy-start | bytes 393220
  13.5 44.9 %all-to-all-start = ((bf16[2,128,2176]{2,1,0:T(8,128)(2,1)}), bf16[2,128,2176]{2,1,0:T(8,128)(2,1)S(1)}, u32[]{:S(2)}, u32[]{:S(2)}) async-start(bf16[2,128,2176]{2,1,0:T(8,128)(2,1)} %pad_maximum_fusion), calls=%async_computation | async-start | bytes 2228224 | tf_op jit(solution)/shard_map/all_to_all | solution.py:246
  20.5 6.5 %copy-start.8 = (bf16[1,16,2048]{2,1,0:T(8,128)(2,1)S(1)}, bf16[1,16,2048]{2,1,0:T(8,128)(2,1)}, u32[]{:S(2)}) copy-start(bf16[1,16,2048]{2,1,0:T(8,128)(2,1)} %param.13) | copy-start | bytes 196612
  20.6 7.9 %copy-start.2 = (bf16[144,1024]{1,0:T(8,128)(2,1)S(1)}, bf16[144,1024]{1,0:T(8,128)(2,1)}, u32[]{:S(2)}) copy-start(bf16[144,1024]{1,0:T(8,128)(2,1)} %pack.1) | copy-start | bytes 884740
  20.6 13.2 %collective-permute-start.3 = (bf16[144,1024]{1,0:T(8,128)(2,1)S(1)}, bf16[144,1024]{1,0:T(8,128)(2,1)S(1)}, u32[]{:S(2)}, u32[]{:S(2)}) collective-permute-start(bf16[144,1024]{1,0:T(8,128)(2,1)S(1)} %broadcast_select_fusion.1), channel_id=1, source_target_pairs={{0,2},{1,3},{16,18},{17,19},{32,34},{33,35},{48,50},{49,51},{2,4},... | collective-permute-start | bytes 884744 | tf_op jit(solution)/shard_map/ppermute | solution.py:284
  22.6 8.1 %collective-permute-start.1 = (bf16[144,1024]{1,0:T(8,128)(2,1)S(1)}, bf16[144,1024]{1,0:T(8,128)(2,1)}, u32[]{:S(2)}, u32[]{:S(2)}) collective-permute-start(bf16[144,1024]{1,0:T(8,128)(2,1)S(1)} %collective-permute-done), channel_id=1, source_target_pairs={{12,14},{13,15},{28,30},{29,31},{44,46},{45,47},{60,62},{61,63},{7... | collective-permute-start | bytes 884744 | tf_op jit(solution)/shard_map/ppermute | solution.py:284
  33.8 21.3 %collective-permute-start.4 = (bf16[144,1024]{1,0:T(8,128)(2,1)S(1)}, bf16[144,1024]{1,0:T(8,128)(2,1)S(1)}, u32[]{:S(2)}, u32[]{:S(2)}) collective-permute-start(bf16[144,1024]{1,0:T(8,128)(2,1)S(1)} %broadcast_select_fusion), channel_id=1, source_target_pairs={{0,2},{1,3},{16,18},{17,19},{32,34},{33,35},{48,50},{49,51},{2,4},... | collective-permute-start | bytes 884744 | tf_op jit(solution)/shard_map/ppermute | solution.py:284
  58.4 1.1 copy-start.1
  59.5 20.3 %copy-start.9 = (f32[1,512]{1,0:T(1,128)S(1)}, f32[1,512]{1,0:T(1,128)}, u32[]{:S(2)}) copy-start(f32[1,512]{1,0:T(1,128)} %get-tuple-element.23) | copy-start | bytes 6148
  59.5 20.3 %copy-start.10 = (f32[1,512]{1,0:T(1,128)S(1)}, f32[1,512]{1,0:T(1,128)}, u32[]{:S(2)}) copy-start(f32[1,512]{1,0:T(1,128)} %get-tuple-element.24) | copy-start | bytes 6148
  69.4 21.1 %all-to-all-start.1 = ((f32[32,1,640]{2,1,0:T(1,128)}), f32[32,1,640]{2,1,0:T(1,128)S(1)}, u32[]{:S(2)}, u32[]{:S(2)}) async-start(f32[32,1,640]{2,1,0:T(1,128)} %reshape.43), calls=%async_computation.1 | async-start | bytes 163840 | tf_op jit(solution)/shard_map/all_to_all | solution.py:246
  90.4 0.6 copy-start.4
  92.7 17.6 %all-to-all-start.2 = ((f32[64,1,128]{2,1,0:T(1,128)}), f32[64,1,128]{2,1,0:T(1,128)S(1)}, u32[]{:S(2)}, u32[]{:S(2)}) async-start(f32[64,1,128]{2,1,0:T(1,128)} %get-tuple-element.10), calls=%async_computation.2 | async-start | bytes 65536 | tf_op jit(solution)/shard_map/all_to_all | solution.py:246
  110.3 0.6 copy-start.7

commit v4 on v3

--- a/solution.py
+++ b/solution.py
@@ -46,15 +46,33 @@
     out[BLOCK:, BLOCK:] = jnp.zeros((SEG_ROWS, out.shape[1] - BLOCK), BF16)
 
 
+def pack_queries_kernel(queries, grads, adapter_t, out):
+    a = jnp.concatenate([adapter_t[...].astype(F32), jnp.zeros((BLOCK - RANK, BLOCK), F32)], axis=0)
+    a = jnp.transpose(a).astype(BF16)
+    for core in range(2):
+        for i, ref in enumerate((queries, grads)):
+            for g in range(GROUPS):
+                to, at = i * HALF + g * GFEAT, (g * 2 + core) * GFEAT
+                out[core, :, to : to + GFEAT] = ref[:, at : at + GFEAT]
+        out[core, :, 2 * HALF :] = a
+
+
 def attend_kernel(
-    core_ref, qg, c0, c1, c2, c3, up, dmat, rmat, out, keys, keys_t, vals, qs, ts, at, qaug, s_ref, t_ref, u_ref, c_ref
+    core_ref, qg, far, c1, c2, c3, up, dmat, rmat, out, c0, sem, keys, keys_t, vals, qs, ts, at, qaug, s_ref, t_ref, u_ref, c_ref
 ):
     chunks = (c0, c1, c2, c3)
     core = core_ref[0]
+    copy = pltpu.make_async_copy(far, c0, sem)
+    copy.start()
+
+    def mine(ref):
+        parts = [ref[:, pl.ds(pl.multiple_of((g * 2 + core) * GFEAT, GFEAT), GFEAT)] for g in range(GROUPS)]
+        return jnp.concatenate(parts, axis=1)
+
     a_pad = qg[:, 2 * HALF : 2 * HALF + 128]
     a = a_pad[:, :RANK]
-    qs[...] = (qg[:, :HALF].astype(F32) + dot(a, up[...])).astype(BF16)
-    d = dmat[...]
+    qs[...] = (qg[:, :HALF].astype(F32) + dot(a, mine(up))).astype(BF16)
+    d, r = mine(dmat), mine(rmat)
     d1 = d.astype(BF16)
     rest = d - d1.astype(F32)
     d2 = rest.astype(BF16)
@@ -62,7 +80,10 @@
     ts[...] = (dot(a, d1) + dot(a, d2) + dot(a, d3)).astype(BF16)
     at[...] = jnp.transpose(a_pad.astype(F32))[:RANK].astype(BF16)
     lane = lax.broadcasted_iota(jnp.int32, (BLOCK, BLOCK), 1).astype(F32)
-    for j, c in enumerate(chunks):
+    for j in (3, 2, 1, 0):
+        c = chunks[j]
+        if j == 0:
+            copy.wait()
         for half in range(2):
             rows = slice((j * 2 + half) * BLOCK, (j * 2 + half + 1) * BLOCK)
             seg_row = c[half, BLOCK:, :BLOCK].astype(F32)[0:1]
@@ -92,11 +113,20 @@
             return [ref[own, col : col + HEAD_DIM] for col in cols]
 
         q2 = [jnp.concatenate([q, qaug[b]], axis=1) for q in two(qs, 0)]
-        s_ref[slot] = dot(keys[g, win, :], jnp.concatenate(q2, axis=0), NT)
-        t_ref[slot] = dot(keys[g, win, :HEAD_DIM], jnp.concatenate(two(ts, 0), axis=0), NT)
-        u_ref[slot] = dot(vals[g, win, :], jnp.concatenate(two(qg, HALF), axis=0), NT)
-
-    def weigh(n):
+        q, t, r = (jnp.concatenate(x, axis=0) for x in (q2, two(ts, 0), two(qg, HALF)))
+
+        def do_s():
+            s_ref[slot] = dot(keys[g, win, :], q, NT)
+
+        def do_t():
+            t_ref[slot] = dot(keys[g, win, :HEAD_DIM], t, NT)
+
+        def do_u():
+            u_ref[slot] = dot(vals[g, win, :], r, NT)
+
+        return [do_s, do_t, do_u]
+
+    def weigh(n, ahead):
         slot = n % 3
         scales = []
         for e in range(2):
@@ -110,6 +140,8 @@
                 top = jnp.max(fold(s), axis=0)
                 m8 = top if m8 is None else jnp.maximum(m8, top)
             m = jnp.max(m8, axis=0, keepdims=True)
+            if ahead:
+                ahead.pop(0)()
             z8 = et8 = eu8 = etu8 = jnp.zeros((8, BLOCK), F32)
             for w in range(7):
                 rows = slice(w * BLOCK, (w + 1) * BLOCK)
@@ -134,6 +166,8 @@
                     (t_ref[slot, rows, lanes] - mt) * (u_ref[slot, rows, lanes] - mu) - cov
                 )
                 c_ref[slot, rows, lanes] = coef.astype(BF16)
+            if ahead:
+                ahead.pop(0)()
             scales.append(inv * (1.0 / HEAD_DIM))
         return scales
 
@@ -153,19 +187,16 @@
             else:
                 out[:, cols] += part
 
-    scores(0)
+    for matmul in scores(0):
+        matmul()
     for n in range(8):
-        if n < 7:
-            scores(n + 1)
-        gather(n, weigh(n))
-    dh = rh = jnp.zeros((1, 1), F32)
-    for g in range(GROUPS):
-        h = out[:, g * ROW : g * ROW + GFEAT]
-        cols = slice(g * GFEAT, (g + 1) * GFEAT)
-        dh = dh + jnp.sum(h * d[:, cols], keepdims=True)
-        rh = rh + jnp.sum(h * rmat[:, cols], keepdims=True)
+        gather(n, weigh(n, scores(n + 1) if n < 7 else []))
+    h = jnp.concatenate([out[:, g * ROW : g * ROW + GFEAT] for g in range(GROUPS)], axis=1)
     lane = lax.broadcasted_iota(jnp.int32, (RANK, 128), 1)
-    tail = jnp.where(lane == 0, dh, jnp.where(lane == 1, rh, 0.0))
+    tail = jnp.zeros((RANK, 128), F32)
+    share = 1.0 / (RANK * GROUPS)
+    for k, term in enumerate((h * d, h * r, r * r * share, d * d * share, r * d * share)):
+        tail = jnp.where(lane == k, jnp.sum(term, keepdims=True), tail)
     for g in range(GROUPS):
         out[:, g * ROW + GFEAT : (g + 1) * ROW] = tail
 
@@ -175,9 +206,11 @@
     return pl.pallas_call(
         attend_kernel,
         out_shape=jax.ShapeDtypeStruct((RANK, GROUPS * ROW), F32),
-        in_specs=[pl.BlockSpec(memory_space=pltpu.SMEM)] + [pl.BlockSpec(memory_space=vm)] * 8,
+        in_specs=[pl.BlockSpec(memory_space=x) for x in (pltpu.SMEM, vm, pl.ANY, vm, vm, vm, vm, vm, vm)],
         out_specs=pl.BlockSpec(memory_space=vm),
         scratch_shapes=[
+            vm((2, BLOCK + SEG_ROWS, 4 * KHALF), BF16),
+            pltpu.SemaphoreType.DMA,
             vm((GROUPS, 4 * CHUNK, 2 * HEAD_DIM), BF16),
             vm((GROUPS, HEAD_DIM, 4 * CHUNK), BF16),
             vm((GROUPS, 4 * CHUNK, HEAD_DIM), BF16),
@@ -203,20 +236,19 @@
     tail = total[:, h_out.shape[1] :]
     lane = lax.broadcasted_iota(jnp.int32, tail.shape, 1)
     share = 2.0 / out.shape[0]
-    row = jnp.where(lane == 2, jnp.sum(h * h, keepdims=True), tail * share)
+    row = jnp.where(lane == 5, jnp.sum(h * h, keepdims=True), tail * share)
     out[...] = jnp.broadcast_to(row[None], out.shape)
 
 
-def update_kernel(got, h_all, dot_in, parts, new_solution, new_residual, new_direction, spread):
+def update_kernel(damping, got, h_all, parts, new_solution, new_residual, new_direction, spread):
     total = jnp.sum(got[...], axis=0)
     lane = lax.broadcasted_iota(jnp.int32, total.shape, 1)
 
     def pick(row, k):
         return jnp.sum(jnp.where(lane == k, row, 0.0), keepdims=True)
 
-    dh, rh, hh = pick(total, 0), pick(total, 1), pick(total, 2)
-    consts = dot_in[...]
-    rr, dd, rd, damp = (pick(consts, k) for k in range(4))
+    dh, rh, rr, dd, rd, hh = (pick(total, k) for k in range(6))
+    damp = damping[0]
     h = h_all[...]
     sol, res, dirn = parts[0:1], parts[1:2], parts[2:3]
     step_len = rr / (dd + dh / damp)
@@ -232,11 +264,11 @@
     spread[...] = jnp.broadcast_to(ns[None], spread.shape)
 
 
-def in_vmem(kernel, out_shapes, *args, name, dtype=F32):
+def in_vmem(kernel, out_shapes, *args, name, dtype=F32, smem=0):
     return pl.pallas_call(
         kernel,
         out_shape=[jax.ShapeDtypeStruct(s, dtype) for s in out_shapes],
-        in_specs=[pl.BlockSpec(memory_space=pltpu.VMEM)] * len(args),
+        in_specs=[pl.BlockSpec(memory_space=pltpu.SMEM if i < smem else pltpu.VMEM) for i in range(len(args))],
         out_specs=[pl.BlockSpec(memory_space=pltpu.VMEM)] * len(out_shapes),
         name=name,
     )(*args)
@@ -259,11 +291,6 @@
     return pairs
 
 
-def per_core(x):
-    rows, _, _, n = x.shape
-    return x.transpose(2, 0, 1, 3).reshape(2, rows, 2 * n)
-
-
 def per_device(
     base_queries, adapter_input, adapter_up_weight, projected_keys, projected_values, output_gradient,
     segments, solution, residual, direction, damping,
@@ -272,11 +299,6 @@
     n_yh, n_z, n_task = lax.axis_size("yh"), lax.axis_size("z"), lax.axis_size("task")
     idx = lax.axis_index(CTX)
 
-    def core_part(x):
-        rows, feats = x.shape[0], x.shape[1] // 4
-        x = x.reshape(rows, 2, 2, feats)
-        return lax.dynamic_index_in_dim(x, core, 2, keepdims=False).reshape(rows, 2 * feats)
-
     last = n_z - 1
     row = [(i, i + 1, 0) for i in range(last)]
 
@@ -286,30 +308,24 @@
     (own,) = in_vmem(
         pack_kernel, [(BLOCK + SEG_ROWS, 4 * KHALF)], projected_keys[0], projected_values[0], segments, name="pack", dtype=BF16
     )
+    (qg,) = in_vmem(
+        pack_queries_kernel, [(2, BLOCK, 2 * HALF + 128)], base_queries[0], output_gradient[0], adapter_input[0].T,
+        name="pack_queries", dtype=BF16,
+    )
     first = move(own, *row, (last, 0, 1))
-    cross = move(own, (last - 1, last, 1), (last - 2, last - 1, 1))
-    second = move(jnp.where(z == last, cross, first), *row, (last, 0, 0))
-    cross = move(cross, (last - 1, last, 0))
-    third = move(jnp.where(z == last, cross, second), *row, (last, 0, 0))
+    cross = move(own, (last - 1, 0, 1), (last - 2, last, 1))
+    first, own, qg = lax.optimization_barrier((first, own, qg))
+    second = move(first, *row)
+    qg = exchange(qg, "core").reshape(CHUNK, 2 * HALF + 128)
+    passed = jnp.where((z == 0) | (z == last), cross, second)
+    third = move(passed, *row, (last, 0, 0))
+    second = jnp.where(z == 0, cross, second)
     chunks = [lax.all_gather(x, "core") for x in (third, second, first, own)]
 
-    pad = jnp.pad(adapter_input[0], ((0, 0), (0, 128 - RANK)))
-    qg = jnp.concatenate(
-        [
-            per_core(base_queries[0].reshape(BLOCK, 2, 2, GFEAT)),
-            per_core(output_gradient[0].reshape(BLOCK, 2, 2, GFEAT)),
-            jnp.broadcast_to(pad[None], (2, BLOCK, 128)),
-        ],
-        axis=2,
-    )
-    qg = exchange(qg, "core").reshape(CHUNK, 2 * HALF + 128)
-
-    up, dmat, rmat = (core_part(x.reshape(RANK, 2 * HALF)) for x in (adapter_up_weight[0], direction[0], residual[0]))
     size = direction.shape[1] // (n_yh * n_z * 2)
     parts = jnp.concatenate([lax.dynamic_slice_in_dim(x, idx * size, size, 1) for x in (solution, residual, direction)])
-    consts = jnp.stack([jnp.sum(residual * residual), jnp.sum(direction * direction), jnp.sum(residual * direction), damping[0]])
-    consts = jnp.pad(consts, (0, 124))[None]
-
+
+    up, dmat, rmat = (x.reshape(RANK, 2 * HALF) for x in (adapter_up_weight, direction, residual))
     terms = attend(core.reshape(1), qg, chunks, up, dmat, rmat)
 
     peers = n_yh * n_z
@@ -317,7 +333,7 @@
         norm_kernel, [(1, GFEAT), (2 * peers, 1, 128)], exchange(terms.reshape(peers, 1, ROW), ("yh", "z")), name="norm"
     )
     new_solution, new_residual, new_direction, spread = in_vmem(
-        update_kernel, [(1, size)] * 3 + [(n_task, 1, size)], exchange(scalars, CTX), h, consts, parts, name="update"
+        update_kernel, [(1, size)] * 3 + [(n_task, 1, size)], damping, exchange(scalars, CTX), h, parts, name="update", smem=1
     )
     meta_gradient = jnp.sum(exchange(spread, "task"), axis=(0, 1)) / n_task
     return new_solution, new_residual, new_direction, meta_gradient

time: 123 us -> 124 us (level)
  starting transfers between devices: 33.4 us -> 50.1 us
  waiting for transfers between devices: 35.3 us -> 28.4 us
  local copies, waits for them, and re-layouts: 9.41 us -> 4.3 us
  other arithmetic: 7.43 us -> 3.16 us
  Pallas kernels: 14.2 us -> 16.8 us
  blocking collectives: 20.9 us -> 18.8 us
    all_to_all x3, starting transfers between devices: 22.6 us -> 34.7 us  [exchange(): return lax.all_to_all(x, axes, 0, 0, tiled=True)]
    ppermute x5 -> x4, waiting for transfers between devices: 16.1 us -> 7.29 us  [move(): return lax.ppermute(x, CTX, moves(n_yh, n_z, kinds))]
    ppermute x5 -> x4, starting transfers between devices: 10.9 us -> 15.4 us  [move(): return lax.ppermute(x, CTX, moves(n_yh, n_z, kinds))]
    broadcast_in_dim x1 -> x0, other arithmetic: 2.61 us -> none  [per_device(): consts = jnp.pad(consts, (0, 124))[None]]
    reduce_sum x1 -> x0, other arithmetic: 2.46 us -> none  [per_device(): jnp.sum(residual * residual)]
    pallas_call x3 -> x4, Pallas kernels: 5.01 us -> 7.39 us  [in_vmem(): pl.pallas_call(kernel, out_shape=[jax.ShapeDtypeStruct(s, dtype) for s in...]
    all_gather x4, blocking collectives: 11.8 us -> 9.54 us  [per_device(): chunks = [lax.all_gather(x, 'core') for x in (third, second, first, own)]]
    another operation x5 -> x0, local copies, waits for them, and re-layouts: 1.97 us -> none  [the longest x1 1.43 us: per_device(): output_gradient[0].reshape(BLOCK, 2, 2, GFEAT)]
  transfers between devices with their start and end apart: 8 -> 7, of which waited for: 4 -> 4; matrix products, arithmetic and copies ran while one was open for 11% -> 3% of each run, Pallas kernels for 0% -> 2%
where the time goes in v4:
time: 124 us; the launch traced here: 123 us
  starting transfers between devices  50.1 us (40%)
  waiting for transfers between devices  28.4 us (23%)
  blocking collectives  18.8 us (15%)
  Pallas kernels  16.8 us (14%)
  local copies, waits for them, and re-layouts  4.3 us (3%)
  other arithmetic  3.16 us (3%)
  between operations  1.47 us (1%)
    all_to_all x3, starting transfers between devices, exchange(): return lax.all_to_all(x, axes, 0, 0, tiled=True)  34.7 us
    all_to_all x3, waiting for transfers between devices, exchange(): return lax.all_to_all(x, axes, 0, 0, tiled=True)  21.1 us
    ppermute x4, starting transfers between devices, move(): return lax.ppermute(x, CTX, moves(n_yh, n_z, kinds))  15.4 us
    all_gather x4, blocking collectives, per_device(): chunks = [lax.all_gather(x, 'core') for x in (third, second, first, own)]  9.54 us
    pallas_call x1, Pallas kernels, attend(): pl.pallas_call(attend_kernel, out_shape=jax.ShapeDtypeStruct((RANK, GROUP...  9.41 us
    all_to_all x1, blocking collectives, exchange(): return lax.all_to_all(x, axes, 0, 0, tiled=True)  9.25 us
    pallas_call x4, Pallas kernels, in_vmem(): pl.pallas_call(kernel, out_shape=[jax.ShapeDtypeStruct(s, dtype) for s in...  7.39 us
    ppermute x4, waiting for transfers between devices, move(): return lax.ppermute(x, CTX, moves(n_yh, n_z, kinds))  7.29 us
  transfers between devices with their start and end apart: 7, of which 4 were waited for; matrix products, arithmetic and copies ran while one was open for 3% of the time, Pallas kernels for 2%

profile of v4, /device:TPU:1, one launch (start us, length us, event | category | flops | bytes accessed | tf_op | source)
XLA Modules:
  0.0 123.0 jit_solution(12455874770977880282)
XLA Ops:
  0.6 0.0 copy-start
  0.6 1.8 %pack.1 = bf16[144,1024]{1,0:T(8,128)(2,1)} custom-call(bf16[128,512]{1,0:T(8,128)(2,1)} %bitcast.22, bf16[128,512]{1,0:T(8,128)(2,1)} %bitcast.23, s32[1,128]{1,0:T(1,128)} %seg.1), custom_call_target="tpu_custom_call" | custom-call | tf_op jit(solution)/shard_map/pack/pallas_call | solution.py:268
  2.4 5.0 %collective-permute-start = (bf16[144,1024]{1,0:T(8,128)(2,1)}, bf16[144,1024]{1,0:T(8,128)(2,1)S(1)}, u32[]{:S(2)}, u32[]{:S(2)}) collective-permute-start(bf16[144,1024]{1,0:T(8,128)(2,1)} %pack.1), channel_id=1, source_target_pairs={{0,2},{1,3},{16,18},{17,19},{32,34},{33,35},{48,50},{49,51},{2,4},... | collective-permute-start | bytes 884744 | tf_op jit(solution)/shard_map/ppermute | solution.py:306
  7.4 0.7 collective-permute-start.1
  8.1 2.4 %pack_queries.1 = bf16[2,128,2176]{2,1,0:T(8,128)(2,1)} custom-call(bf16[128,2048]{1,0:T(8,128)(2,1)} %bitcast.20, bf16[128,2048]{1,0:T(8,128)(2,1)} %bitcast.21, bf16[16,128]{1,0:T(8,128)(2,1)} %bitcast.24), custom_call_target="tpu_custom_call" | custom-call | tf_op jit(solution)/shard_map/pack_queries/pallas_call | solution.py:268
  10.4 0.9 collective-permute-done
  11.3 6.0 %collective-permute-start.2 = (bf16[144,1024]{1,0:T(8,128)(2,1)S(1)}, bf16[144,1024]{1,0:T(8,128)(2,1)S(1)}, u32[]{:S(2)}, u32[]{:S(2)}) collective-permute-start(bf16[144,1024]{1,0:T(8,128)(2,1)S(1)} %collective-permute-done), channel_id=1, source_target_pairs={{0,2},{1,3},{16,18},{17,19},{32,34},{33,35},{48,50},{49,51},{2,4},... | collective-permute-start | bytes 884744 | tf_op jit(solution)/shard_map/ppermute | solution.py:306
  17.4 0.5 broadcast.7
  17.9 0.9 reduce.6
  18.9 1.0 reduce.7
  19.9 5.8 %all-to-all-start = ((bf16[2,128,2176]{2,1,0:T(8,128)(2,1)}), bf16[2,128,2176]{2,1,0:T(8,128)(2,1)S(1)}, u32[]{:S(2)}, u32[]{:S(2)}) async-start(bf16[2,128,2176]{2,1,0:T(8,128)(2,1)} %pack_queries.1), calls=%async_computation | async-start | bytes 2228224 | tf_op jit(solution)/shard_map/all_to_all | solution.py:278
  25.7 2.3 %all-gather.2 = bf16[288,1024]{1,0:T(8,128)(2,1)S(1)} all-gather(bf16[144,1024]{1,0:T(8,128)(2,1)S(1)} %collective-permute-done), channel_id=4, replica_groups=mesh['task'=8,'yh'=4,'z'=8,'core'=2] {'core'}, dimensions={0}, use_global_device_ids=true | all-gather | bytes 884736 | tf_op jit(solution)/shard_map/all_gather | solution.py:323
  28.1 3.8 %collective-permute-start.3 = (bf16[144,1024]{1,0:T(8,128)(2,1)S(1)}, bf16[144,1024]{1,0:T(8,128)(2,1)S(1)}, u32[]{:S(2)}, u32[]{:S(2)}) collective-permute-start(bf16[144,1024]{1,0:T(8,128)(2,1)S(1)} %get-tuple-element.23), channel_id=1, source_target_pairs={{0,2},{1,3},{16,18},{17,19},{32,34},{33,35},{48,50},{49,51},{2,4},... | collective-permute-start | bytes 884744 | tf_op jit(solution)/shard_map/ppermute | solution.py:306
  31.9 2.3 %all-gather.3 = bf16[288,1024]{1,0:T(8,128)(2,1)S(1)} all-gather(bf16[144,1024]{1,0:T(8,128)(2,1)S(1)} %copy-done.3), channel_id=5, replica_groups=mesh['task'=8,'yh'=4,'z'=8,'core'=2] {'core'}, dimensions={0}, use_global_device_ids=true | all-gather | bytes 884736 | tf_op jit(solution)/shard_map/all_gather | solution.py:323
  34.2 2.2 %all-gather.1 = bf16[288,1024]{1,0:T(8,128)(2,1)S(1)} all-gather(bf16[144,1024]{1,0:T(8,128)(2,1)S(1)} %get-tuple-element.22), channel_id=3, replica_groups=mesh['task'=8,'yh'=4,'z'=8,'core'=2] {'core'}, dimensions={0}, use_global_device_ids=true | all-gather | bytes 884736 | tf_op jit(solution)/shard_map/all_gather | solution.py:323
  36.4 6.4 %collective-permute-done.3 = bf16[144,1024]{1,0:T(8,128)(2,1)S(1)} collective-permute-done((bf16[144,1024]{1,0:T(8,128)(2,1)S(1)}, bf16[144,1024]{1,0:T(8,128)(2,1)S(1)}, u32[]{:S(2)}, u32[]{:S(2)}) %collective-permute-start.3) | collective-permute-done | bytes 294944 | tf_op jit(solution)/shard_map/ppermute | solution.py:306
  42.8 2.7 %all-gather = bf16[288,1024]{1,0:T(8,128)(2,1)} all-gather(bf16[144,1024]{1,0:T(8,128)(2,1)S(1)} %collective-permute-done.3), channel_id=2, replica_groups=mesh['task'=8,'yh'=4,'z'=8,'core'=2] {'core'}, dimensions={0}, use_global_device_ids=true | all-gather | bytes 884736 | tf_op jit(solution)/shard_map/all_gather | solution.py:323
  45.5 1.1 copy-done.1
  46.5 9.4 %attend.1 = f32[16,1280]{1,0:T(8,128)S(1)} custom-call(s32[1]{0:T(128)} %bitcast.core_ref, bf16[256,2176]{1,0:T(8,128)(2,1)S(1)} %bitcast.14, bf16[2,144,1024]{2,1,0:T(8,128)(2,1)S(1)} %bitcast.18, bf16[2,144,1024]{2,1,0:T(8,128)(2,1)S(1)} %bitcast.17, bf16[2,144,1024]{2,1,0:T(8,128)(2,1)S(1)} %bitcast.15, bf16[2,144,1024]{2,1,0:T(8,128)(2,1)S(1)} %bitcast.16, ...), custom_call_target="tpu_custom_call" | custom-call | flops 2000000000 | bytes 4000000 | tf_op jit(solution)/shard_map/attend/pallas_call | solution.py:206
  55.9 0.7 reshape.31
  56.7 23.1 %all-to-all-start.1 = ((f32[32,1,640]{2,1,0:T(1,128)}), f32[32,1,640]{2,1,0:T(1,128)S(1)}, u32[]{:S(2)}, u32[]{:S(2)}) async-start(f32[32,1,640]{2,1,0:T(1,128)} %reshape.31), calls=%async_computation.1 | async-start | bytes 163840 | tf_op jit(solution)/shard_map/all_to_all | solution.py:278
  80.4 0.7 constant_dynamic-slice_fusion
  81.1 9.9 %all-to-all-done.1.got = f32[32,1,640]{2,1,0:T(1,128)S(1)} async-done(((f32[32,1,640]{2,1,0:T(1,128)}), f32[32,1,640]{2,1,0:T(1,128)S(1)}, u32[]{:S(2)}, u32[]{:S(2)}) %all-to-all-start.1) | async-done | bytes 81952 | tf_op jit(solution)/shard_map/all_to_all | solution.py:278
  91.1 0.6 copy-done.4
  91.7 1.7 %norm.1 = (f32[1,512]{1,0:T(1,128)}, f32[64,1,128]{2,1,0:T(1,128)}) custom-call(f32[32,1,640]{2,1,0:T(1,128)} %copy-done.4), custom_call_target="tpu_custom_call" | custom-call | tf_op jit(solution)/shard_map/norm/pallas_call | solution.py:268
  93.4 5.8 %all-to-all-start.2 = ((f32[64,1,128]{2,1,0:T(1,128)}), f32[64,1,128]{2,1,0:T(1,128)S(1)}, u32[]{:S(2)}, u32[]{:S(2)}) async-start(f32[64,1,128]{2,1,0:T(1,128)} %get-tuple-element.16), calls=%async_computation.2 | async-start | bytes 65536 | tf_op jit(solution)/shard_map/all_to_all | solution.py:278
  99.2 0.6 pad_maximum_fusion.parts
  99.8 11.2 %all-to-all-done.2.got = f32[64,1,128]{2,1,0:T(1,128)S(1)} async-done(((f32[64,1,128]{2,1,0:T(1,128)}), f32[64,1,128]{2,1,0:T(1,128)S(1)}, u32[]{:S(2)}, u32[]{:S(2)}) %all-to-all-start.2) | async-done | bytes 32800 | tf_op jit(solution)/shard_map/all_to_all | solution.py:278
  111.0 0.6 copy-done.7
  111.6 1.6 %update.1 = (f32[1,512]{1,0:T(1,128)}, f32[1,512]{1,0:T(1,128)}, f32[1,512]{1,0:T(1,128)}, f32[8,1,512]{2,1,0:T(1,128)}) custom-call(f32[1]{0:T(128)S(6)} %copy.15.damping, f32[64,1,128]{2,1,0:T(1,128)} %copy-done.7, f32[1,512]{1,0:T(1,128)} %get-tuple-element.17.h_all, f32[3,512]{1,0:T(4,128)} %pad_maximum_fusion.parts), custom_call_target="tpu_custom_call" | custom-call | tf_op jit(solution)/shard_map/update/pallas_call | solution.py:268
  113.2 9.2 %all_to_all.20 = f32[8,1,512]{2,1,0:T(1,128)S(1)} all-to-all(f32[8,1,512]{2,1,0:T(1,128)} %get-tuple-element.21), channel_id=1, replica_groups=mesh['task'=8,'yh'=4,'z'=8,'core'=2] {'task'}, dimensions={0} | all-to-all | bytes 32768 | tf_op jit(solution)/shard_map/all_to_all | solution.py:278
  122.5 0.6 broadcast_multiply_fusion
  (20 shorter events, 0.2 us)
Async XLA Ops:
  0.6 79.1 %copy-start = (f32[1,32768]{1,0:T(1,128)S(1)}, f32[1,32768]{1,0:T(1,128)}, u32[]{:S(2)}) copy-start(f32[1,32768]{1,0:T(1,128)} %param.18) | copy-start | bytes 393220
  2.4 15.5 %copy-start.5 = (f32[1,32768]{1,0:T(1,128)S(1)}, f32[1,32768]{1,0:T(1,128)}, u32[]{:S(2)}) copy-start(f32[1,32768]{1,0:T(1,128)} %param.20) | copy-start | bytes 393220
  2.4 8.9 %collective-permute-start = (bf16[144,1024]{1,0:T(8,128)(2,1)}, bf16[144,1024]{1,0:T(8,128)(2,1)S(1)}, u32[]{:S(2)}, u32[]{:S(2)}) collective-permute-start(bf16[144,1024]{1,0:T(8,128)(2,1)} %pack.1), channel_id=1, source_target_pairs={{0,2},{1,3},{16,18},{17,19},{32,34},{33,35},{48,50},{49,51},{2,4},... | collective-permute-start | bytes 884744 | tf_op jit(solution)/shard_map/ppermute | solution.py:306
  7.4 20.6 %collective-permute-start.1 = (bf16[144,1024]{1,0:T(8,128)(2,1)}, bf16[144,1024]{1,0:T(8,128)(2,1)S(1)}, u32[]{:S(2)}, u32[]{:S(2)}) collective-permute-start(bf16[144,1024]{1,0:T(8,128)(2,1)} %pack.1), channel_id=1, source_target_pairs={{12,16},{13,17},{28,32},{29,33},{44,48},{45,49},{10,30},{11,31},{2... | collective-permute-start | bytes 884744 | tf_op jit(solution)/shard_map/ppermute | solution.py:306
  8.1 10.8 %copy-start.6 = (f32[1,32768]{1,0:T(1,128)S(1)}, f32[1,32768]{1,0:T(1,128)}, u32[]{:S(2)}) copy-start(f32[1,32768]{1,0:T(1,128)} %param.19) | copy-start | bytes 393220
  11.3 16.7 %collective-permute-start.2 = (bf16[144,1024]{1,0:T(8,128)(2,1)S(1)}, bf16[144,1024]{1,0:T(8,128)(2,1)S(1)}, u32[]{:S(2)}, u32[]{:S(2)}) collective-permute-start(bf16[144,1024]{1,0:T(8,128)(2,1)S(1)} %collective-permute-done), channel_id=1, source_target_pairs={{0,2},{1,3},{16,18},{17,19},{32,34},{33,35},{48,50},{49,51},{2,4},... | collective-permute-start | bytes 884744 | tf_op jit(solution)/shard_map/ppermute | solution.py:306
  19.9 25.6 %all-to-all-start = ((bf16[2,128,2176]{2,1,0:T(8,128)(2,1)}), bf16[2,128,2176]{2,1,0:T(8,128)(2,1)S(1)}, u32[]{:S(2)}, u32[]{:S(2)}) async-start(bf16[2,128,2176]{2,1,0:T(8,128)(2,1)} %pack_queries.1), calls=%async_computation | async-start | bytes 2228224 | tf_op jit(solution)/shard_map/all_to_all | solution.py:278
  25.7 6.2 %copy-start.3 = (bf16[144,1024]{1,0:T(8,128)(2,1)S(1)}, bf16[144,1024]{1,0:T(8,128)(2,1)}, u32[]{:S(2)}) copy-start(bf16[144,1024]{1,0:T(8,128)(2,1)} %pack.1) | copy-start | bytes 884740
  28.1 17.4 %copy-start.2 = (bf16[1,16,2048]{2,1,0:T(8,128)(2,1)S(1)}, bf16[1,16,2048]{2,1,0:T(8,128)(2,1)}, u32[]{:S(2)}) copy-start(bf16[1,16,2048]{2,1,0:T(8,128)(2,1)} %param.13) | copy-start | bytes 196612
  28.1 14.7 %collective-permute-start.3 = (bf16[144,1024]{1,0:T(8,128)(2,1)S(1)}, bf16[144,1024]{1,0:T(8,128)(2,1)S(1)}, u32[]{:S(2)}, u32[]{:S(2)}) collective-permute-start(bf16[144,1024]{1,0:T(8,128)(2,1)S(1)} %get-tuple-element.23), channel_id=1, source_target_pairs={{0,2},{1,3},{16,18},{17,19},{32,34},{33,35},{48,50},{49,51},{2,4},... | collective-permute-start | bytes 884744 | tf_op jit(solution)/shard_map/ppermute | solution.py:306
  45.5 1.1 copy-start.1
  56.7 34.4 %all-to-all-start.1 = ((f32[32,1,640]{2,1,0:T(1,128)}), f32[32,1,640]{2,1,0:T(1,128)S(1)}, u32[]{:S(2)}, u32[]{:S(2)}) async-start(f32[32,1,640]{2,1,0:T(1,128)} %reshape.31), calls=%async_computation.1 | async-start | bytes 163840 | tf_op jit(solution)/shard_map/all_to_all | solution.py:278
  91.1 0.6 copy-start.4
  93.4 17.6 %all-to-all-start.2 = ((f32[64,1,128]{2,1,0:T(1,128)}), f32[64,1,128]{2,1,0:T(1,128)S(1)}, u32[]{:S(2)}, u32[]{:S(2)}) async-start(f32[64,1,128]{2,1,0:T(1,128)} %get-tuple-element.16), calls=%async_computation.2 | async-start | bytes 65536 | tf_op jit(solution)/shard_map/all_to_all | solution.py:278
  111.0 0.6 copy-start.7

commit v5 on v4

--- a/solution.py
+++ b/solution.py
@@ -314,18 +314,18 @@
     )
     first = move(own, *row, (last, 0, 1))
     cross = move(own, (last - 1, 0, 1), (last - 2, last, 1))
-    first, own, qg = lax.optimization_barrier((first, own, qg))
+    qg = exchange(qg, "core").reshape(CHUNK, 2 * HALF + 128)
+    own = lax.all_gather(own, "core")
+    up, dmat, rmat = (x.reshape(RANK, 2 * HALF) for x in (adapter_up_weight, direction, residual))
+    size = direction.shape[1] // (n_yh * n_z * 2)
+    parts = jnp.concatenate([lax.dynamic_slice_in_dim(x, idx * size, size, 1) for x in (solution, residual, direction)])
+    first, own, qg, dmat, rmat, parts = lax.optimization_barrier((first, own, qg, dmat, rmat, parts))
     second = move(first, *row)
-    qg = exchange(qg, "core").reshape(CHUNK, 2 * HALF + 128)
     passed = jnp.where((z == 0) | (z == last), cross, second)
     third = move(passed, *row, (last, 0, 0))
     second = jnp.where(z == 0, cross, second)
-    chunks = [lax.all_gather(x, "core") for x in (third, second, first, own)]
-
-    size = direction.shape[1] // (n_yh * n_z * 2)
-    parts = jnp.concatenate([lax.dynamic_slice_in_dim(x, idx * size, size, 1) for x in (solution, residual, direction)])
-
-    up, dmat, rmat = (x.reshape(RANK, 2 * HALF) for x in (adapter_up_weight, direction, residual))
+    chunks = [lax.all_gather(x, "core") for x in (third, second, first)] + [own]
+
     terms = attend(core.reshape(1), qg, chunks, up, dmat, rmat)
 
     peers = n_yh * n_z

time: 124 us -> 116 us (0.935)
  starting transfers between devices: 50.1 us -> 24.2 us
  blocking collectives: 18.8 us -> 44.5 us
  waiting for transfers between devices: 28.4 us -> 24.2 us
  local copies, waits for them, and re-layouts: 4.3 us -> 1.3 us
    all_to_all x1 -> x2, blocking collectives: 9.25 us -> 33.9 us  [exchange(): return lax.all_to_all(x, axes, 0, 0, tiled=True)]
    all_to_all x3 -> x2, starting transfers between devices: 34.7 us -> 12.8 us  [exchange(): return lax.all_to_all(x, axes, 0, 0, tiled=True)]
    all_to_all x3 -> x2, waiting for transfers between devices: 21.1 us -> 11.2 us  [exchange(): return lax.all_to_all(x, axes, 0, 0, tiled=True)]
    ppermute x4, waiting for transfers between devices: 7.29 us -> 13 us  [move(): return lax.ppermute(x, CTX, moves(n_yh, n_z, kinds))]
    ppermute x4, starting transfers between devices: 15.4 us -> 11.4 us  [move(): return lax.ppermute(x, CTX, moves(n_yh, n_z, kinds))]
    unnamed x17 -> x13, local copies, waits for them, and re-layouts: 2.83 us -> 1.15 us
  transfers between devices with their start and end apart: 7 -> 6, of which waited for: 4 -> 3; matrix products, arithmetic and copies ran while one was open for 3% -> 3% of each run, Pallas kernels for 2% -> 2%
where the time goes in v5:
time: 116 us
  blocking collectives  44.5 us (38%)
  starting transfers between devices  24.2 us (21%)
  waiting for transfers between devices  24.2 us (21%)
  Pallas kernels  16.7 us (14%)
  other arithmetic  3.16 us (3%)
  between operations  1.43 us (1%)
  local copies, waits for them, and re-layouts  1.3 us (1%)
    all_to_all x2, blocking collectives, exchange(): return lax.all_to_all(x, axes, 0, 0, tiled=True)  33.9 us
    ppermute x4, waiting for transfers between devices, move(): return lax.ppermute(x, CTX, moves(n_yh, n_z, kinds))  13 us
    all_to_all x2, starting transfers between devices, exchange(): return lax.all_to_all(x, axes, 0, 0, tiled=True)  12.8 us
    ppermute x4, starting transfers between devices, move(): return lax.ppermute(x, CTX, moves(n_yh, n_z, kinds))  11.4 us
    all_to_all x2, waiting for transfers between devices, exchange(): return lax.all_to_all(x, axes, 0, 0, tiled=True)  11.2 us
    pallas_call x1, Pallas kernels, attend(): pl.pallas_call(attend_kernel, out_shape=jax.ShapeDtypeStruct((RANK, GROUP...  9.41 us
    all_gather x3, blocking collectives, per_device(): chunks = [lax.all_gather(x, 'core') for x in (third, second, first)] + [own]  8.42 us
    pallas_call x4, Pallas kernels, in_vmem(): pl.pallas_call(kernel, out_shape=[jax.ShapeDtypeStruct(s, dtype) for s in...  7.33 us
  transfers between devices with their start and end apart: 6, of which 3 were waited for; matrix products, arithmetic and copies ran while one was open for 3% of the time, Pallas kernels for 2%

profile of v5, /device:TPU:1, one launch (start us, length us, event | category | flops | bytes accessed | tf_op | source)
XLA Modules:
  0.0 115.6 jit_solution(13786489634388502016)
XLA Ops:
  0.6 0.0 copy-start
  0.6 1.8 %pack.1 = bf16[144,1024]{1,0:T(8,128)(2,1)} custom-call(bf16[128,512]{1,0:T(8,128)(2,1)} %bitcast.22, bf16[128,512]{1,0:T(8,128)(2,1)} %bitcast.23, s32[1,128]{1,0:T(1,128)} %seg.1), custom_call_target="tpu_custom_call" | custom-call | tf_op jit(solution)/shard_map/pack/pallas_call | solution.py:268
  2.4 4.8 %collective-permute-start = (bf16[144,1024]{1,0:T(8,128)(2,1)}, bf16[144,1024]{1,0:T(8,128)(2,1)S(1)}, u32[]{:S(2)}, u32[]{:S(2)}) collective-permute-start(bf16[144,1024]{1,0:T(8,128)(2,1)} %pack.1), channel_id=1, source_target_pairs={{0,2},{1,3},{16,18},{17,19},{32,34},{33,35},{48,50},{49,51},{2,4},... | collective-permute-start | bytes 884744 | tf_op jit(solution)/shard_map/ppermute | solution.py:306
  7.2 0.7 collective-permute-start.1
  7.9 2.3 %pack_queries.1 = bf16[2,128,2176]{2,1,0:T(8,128)(2,1)} custom-call(bf16[128,2048]{1,0:T(8,128)(2,1)} %bitcast.20, bf16[128,2048]{1,0:T(8,128)(2,1)} %bitcast.21, bf16[16,128]{1,0:T(8,128)(2,1)} %bitcast.24), custom_call_target="tpu_custom_call" | custom-call | tf_op jit(solution)/shard_map/pack_queries/pallas_call | solution.py:268
  10.3 7.1 %all-to-all-start = ((bf16[2,128,2176]{2,1,0:T(8,128)(2,1)}), bf16[2,128,2176]{2,1,0:T(8,128)(2,1)S(1)}, u32[]{:S(2)}, u32[]{:S(2)}) async-start(bf16[2,128,2176]{2,1,0:T(8,128)(2,1)} %pack_queries.1), calls=%async_computation | async-start | bytes 2228224 | tf_op jit(solution)/shard_map/all_to_all | solution.py:278
  17.3 0.5 broadcast.7
  17.9 0.9 reduce.6
  18.8 1.0 reduce.7
  19.8 0.6 pad_maximum_fusion.parts
  20.5 2.2 %all-gather = bf16[288,1024]{1,0:T(8,128)(2,1)S(1)} all-gather(bf16[144,1024]{1,0:T(8,128)(2,1)S(1)} %copy-done.2), channel_id=2, replica_groups=mesh['task'=8,'yh'=4,'z'=8,'core'=2] {'core'}, dimensions={0}, use_global_device_ids=true | all-gather | bytes 884736 | tf_op jit(solution)/shard_map/all_gather | solution.py:318
  22.7 0.0 all-to-all-done
  22.7 0.0 collective-permute-done
  22.7 1.6 %collective-permute-start.2 = (bf16[144,1024]{1,0:T(8,128)(2,1)S(1)}, bf16[144,1024]{1,0:T(8,128)(2,1)S(1)}, u32[]{:S(2)}, u32[]{:S(2)}) collective-permute-start(bf16[144,1024]{1,0:T(8,128)(2,1)S(1)} %collective-permute-done), channel_id=1, source_target_pairs={{0,2},{1,3},{16,18},{17,19},{32,34},{33,35},{48,50},{49,51},{2,4},... | collective-permute-start | bytes 884744 | tf_op jit(solution)/shard_map/ppermute | solution.py:306
  24.3 0.0 collective-permute-done.1
  24.3 6.2 %collective-permute-done.2 = bf16[144,1024]{1,0:T(8,128)(2,1)S(1)} collective-permute-done((bf16[144,1024]{1,0:T(8,128)(2,1)S(1)}, bf16[144,1024]{1,0:T(8,128)(2,1)S(1)}, u32[]{:S(2)}, u32[]{:S(2)}) %collective-permute-start.2) | collective-permute-done | bytes 294944 | tf_op jit(solution)/shard_map/ppermute | solution.py:306
  30.6 0.0 copy-start.1
  30.6 4.2 %collective-permute-start.3 = (bf16[144,1024]{1,0:T(8,128)(2,1)S(1)}, bf16[144,1024]{1,0:T(8,128)(2,1)S(1)}, u32[]{:S(2)}, u32[]{:S(2)}) collective-permute-start(bf16[144,1024]{1,0:T(8,128)(2,1)S(1)} %get-tuple-element.29), channel_id=1, source_target_pairs={{0,2},{1,3},{16,18},{17,19},{32,34},{33,35},{48,50},{49,51},{2,4},... | collective-permute-start | bytes 884744 | tf_op jit(solution)/shard_map/ppermute | solution.py:306
  34.8 3.1 %all-gather.3 = bf16[288,1024]{1,0:T(8,128)(2,1)S(1)} all-gather(bf16[144,1024]{1,0:T(8,128)(2,1)S(1)} %collective-permute-done), channel_id=5, replica_groups=mesh['task'=8,'yh'=4,'z'=8,'core'=2] {'core'}, dimensions={0}, use_global_device_ids=true | all-gather | bytes 884736 | tf_op jit(solution)/shard_map/all_gather | solution.py:327
  37.9 2.2 %all-gather.2 = bf16[288,1024]{1,0:T(8,128)(2,1)S(1)} all-gather(bf16[144,1024]{1,0:T(8,128)(2,1)S(1)} %get-tuple-element.28), channel_id=4, replica_groups=mesh['task'=8,'yh'=4,'z'=8,'core'=2] {'core'}, dimensions={0}, use_global_device_ids=true | all-gather | bytes 884736 | tf_op jit(solution)/shard_map/all_gather | solution.py:327
  40.1 6.8 %collective-permute-done.3 = bf16[144,1024]{1,0:T(8,128)(2,1)S(1)} collective-permute-done((bf16[144,1024]{1,0:T(8,128)(2,1)S(1)}, bf16[144,1024]{1,0:T(8,128)(2,1)S(1)}, u32[]{:S(2)}, u32[]{:S(2)}) %collective-permute-start.3) | collective-permute-done | bytes 294944 | tf_op jit(solution)/shard_map/ppermute | solution.py:306
  47.0 3.1 %all-gather.1 = bf16[288,1024]{1,0:T(8,128)(2,1)S(1)} all-gather(bf16[144,1024]{1,0:T(8,128)(2,1)S(1)} %collective-permute-done.3), channel_id=3, replica_groups=mesh['task'=8,'yh'=4,'z'=8,'core'=2] {'core'}, dimensions={0}, use_global_device_ids=true | all-gather | bytes 884736 | tf_op jit(solution)/shard_map/all_gather | solution.py:327
  50.1 9.4 %attend.1 = f32[16,1280]{1,0:T(8,128)S(1)} custom-call(s32[1]{0:T(128)} %bitcast.core_ref, bf16[256,2176]{1,0:T(8,128)(2,1)S(1)} %bitcast.14, bf16[2,144,1024]{2,1,0:T(8,128)(2,1)S(1)} %bitcast.18, bf16[2,144,1024]{2,1,0:T(8,128)(2,1)S(1)} %bitcast.17, bf16[2,144,1024]{2,1,0:T(8,128)(2,1)S(1)} %bitcast.16, bf16[2,144,1024]{2,1,0:T(8,128)(2,1)S(1)} %bitcast.15, ...), custom_call_target="tpu_custom_call" | custom-call | flops 2000000000 | bytes 4000000 | tf_op jit(solution)/shard_map/attend/pallas_call | solution.py:206
  59.5 0.1 reshape.31
  59.6 23.5 %all_to_all.20.got = f32[32,1,640]{2,1,0:T(1,128)} all-to-all(f32[32,1,640]{2,1,0:T(1,128)S(1)} %reshape.31), channel_id=1, replica_groups=mesh['task'=8,'yh'=4,'z'=8,'core'=2] {'yh','z'}, dimensions={0} | all-to-all | bytes 163840 | tf_op jit(solution)/shard_map/all_to_all | solution.py:278
  83.1 1.7 %norm.1 = (f32[1,512]{1,0:T(1,128)}, f32[64,1,128]{2,1,0:T(1,128)}) custom-call(f32[32,1,640]{2,1,0:T(1,128)} %all_to_all.20.got), custom_call_target="tpu_custom_call" | custom-call | tf_op jit(solution)/shard_map/norm/pallas_call | solution.py:268
  84.7 5.8 %all-to-all-start.2 = ((f32[64,1,128]{2,1,0:T(1,128)}), f32[64,1,128]{2,1,0:T(1,128)S(1)}, u32[]{:S(2)}, u32[]{:S(2)}) async-start(f32[64,1,128]{2,1,0:T(1,128)} %get-tuple-element.21), calls=%async_computation.2 | async-start | bytes 65536 | tf_op jit(solution)/shard_map/all_to_all | solution.py:278
  91.2 11.2 %all-to-all-done.2.got = f32[64,1,128]{2,1,0:T(1,128)S(1)} async-done(((f32[64,1,128]{2,1,0:T(1,128)}), f32[64,1,128]{2,1,0:T(1,128)S(1)}, u32[]{:S(2)}, u32[]{:S(2)}) %all-to-all-start.2) | async-done | bytes 32800 | tf_op jit(solution)/shard_map/all_to_all | solution.py:278
  102.4 0.6 copy-done.5
  103.0 1.6 %update.1 = (f32[1,512]{1,0:T(1,128)}, f32[1,512]{1,0:T(1,128)}, f32[1,512]{1,0:T(1,128)}, f32[8,1,512]{2,1,0:T(1,128)}) custom-call(f32[1]{0:T(128)S(6)} %copy.15.damping, f32[64,1,128]{2,1,0:T(1,128)} %copy-done.5, f32[1,512]{1,0:T(1,128)} %get-tuple-element.22.h_all, f32[3,512]{1,0:T(4,128)} %pad_maximum_fusion.parts), custom_call_target="tpu_custom_call" | custom-call | tf_op jit(solution)/shard_map/update/pallas_call | solution.py:268
  104.6 10.4 %all_to_all.21 = f32[8,1,512]{2,1,0:T(1,128)S(1)} all-to-all(f32[8,1,512]{2,1,0:T(1,128)} %get-tuple-element.27), channel_id=1, replica_groups=mesh['task'=8,'yh'=4,'z'=8,'core'=2] {'task'}, dimensions={0} | all-to-all | bytes 32768 | tf_op jit(solution)/shard_map/all_to_all | solution.py:278
  115.0 0.6 broadcast_multiply_fusion
  (15 shorter events, 0.2 us)
Async XLA Ops:
  0.6 16.7 %copy-start = (f32[1,32768]{1,0:T(1,128)S(1)}, f32[1,32768]{1,0:T(1,128)}, u32[]{:S(2)}) copy-start(f32[1,32768]{1,0:T(1,128)} %param.18) | copy-start | bytes 393220
  2.4 20.3 %collective-permute-start = (bf16[144,1024]{1,0:T(8,128)(2,1)}, bf16[144,1024]{1,0:T(8,128)(2,1)S(1)}, u32[]{:S(2)}, u32[]{:S(2)}) collective-permute-start(bf16[144,1024]{1,0:T(8,128)(2,1)} %pack.1), channel_id=1, source_target_pairs={{0,2},{1,3},{16,18},{17,19},{32,34},{33,35},{48,50},{49,51},{2,4},... | collective-permute-start | bytes 884744 | tf_op jit(solution)/shard_map/ppermute | solution.py:306
  7.2 17.1 %collective-permute-start.1 = (bf16[144,1024]{1,0:T(8,128)(2,1)}, bf16[144,1024]{1,0:T(8,128)(2,1)S(1)}, u32[]{:S(2)}, u32[]{:S(2)}) collective-permute-start(bf16[144,1024]{1,0:T(8,128)(2,1)} %pack.1), channel_id=1, source_target_pairs={{12,16},{13,17},{28,32},{29,33},{44,48},{45,49},{10,30},{11,31},{2... | collective-permute-start | bytes 884744 | tf_op jit(solution)/shard_map/ppermute | solution.py:306
  10.2 7.1 %copy-start.3 = (f32[1,32768]{1,0:T(1,128)S(1)}, f32[1,32768]{1,0:T(1,128)}, u32[]{:S(2)}) copy-start(f32[1,32768]{1,0:T(1,128)} %param.20) | copy-start | bytes 393220
  10.2 7.1 %copy-start.4 = (f32[1,32768]{1,0:T(1,128)S(1)}, f32[1,32768]{1,0:T(1,128)}, u32[]{:S(2)}) copy-start(f32[1,32768]{1,0:T(1,128)} %param.19) | copy-start | bytes 393220
  10.3 12.4 %all-to-all-start = ((bf16[2,128,2176]{2,1,0:T(8,128)(2,1)}), bf16[2,128,2176]{2,1,0:T(8,128)(2,1)S(1)}, u32[]{:S(2)}, u32[]{:S(2)}) async-start(bf16[2,128,2176]{2,1,0:T(8,128)(2,1)} %pack_queries.1), calls=%async_computation | async-start | bytes 2228224 | tf_op jit(solution)/shard_map/all_to_all | solution.py:278
  17.3 3.1 %copy-start.2 = (bf16[144,1024]{1,0:T(8,128)(2,1)S(1)}, bf16[144,1024]{1,0:T(8,128)(2,1)}, u32[]{:S(2)}) copy-start(bf16[144,1024]{1,0:T(8,128)(2,1)} %pack.1) | copy-start | bytes 884740
  22.7 7.8 %collective-permute-start.2 = (bf16[144,1024]{1,0:T(8,128)(2,1)S(1)}, bf16[144,1024]{1,0:T(8,128)(2,1)S(1)}, u32[]{:S(2)}, u32[]{:S(2)}) collective-permute-start(bf16[144,1024]{1,0:T(8,128)(2,1)S(1)} %collective-permute-done), channel_id=1, source_target_pairs={{0,2},{1,3},{16,18},{17,19},{32,34},{33,35},{48,50},{49,51},{2,4},... | collective-permute-start | bytes 884744 | tf_op jit(solution)/shard_map/ppermute | solution.py:306
  30.6 19.5 %copy-start.1 = (bf16[1,16,2048]{2,1,0:T(8,128)(2,1)S(1)}, bf16[1,16,2048]{2,1,0:T(8,128)(2,1)}, u32[]{:S(2)}) copy-start(bf16[1,16,2048]{2,1,0:T(8,128)(2,1)} %param.13) | copy-start | bytes 196612
  30.6 16.4 %collective-permute-start.3 = (bf16[144,1024]{1,0:T(8,128)(2,1)S(1)}, bf16[144,1024]{1,0:T(8,128)(2,1)S(1)}, u32[]{:S(2)}, u32[]{:S(2)}) collective-permute-start(bf16[144,1024]{1,0:T(8,128)(2,1)S(1)} %get-tuple-element.29), channel_id=1, source_target_pairs={{0,2},{1,3},{16,18},{17,19},{32,34},{33,35},{48,50},{49,51},{2,4},... | collective-permute-start | bytes 884744 | tf_op jit(solution)/shard_map/ppermute | solution.py:306
  84.7 17.6 %all-to-all-start.2 = ((f32[64,1,128]{2,1,0:T(1,128)}), f32[64,1,128]{2,1,0:T(1,128)S(1)}, u32[]{:S(2)}, u32[]{:S(2)}) async-start(f32[64,1,128]{2,1,0:T(1,128)} %get-tuple-element.21), calls=%async_computation.2 | async-start | bytes 65536 | tf_op jit(solution)/shard_map/all_to_all | solution.py:278
  102.4 0.6 copy-start.5

commit v6 on v5

--- a/solution.py
+++ b/solution.py
@@ -312,18 +312,19 @@
         pack_queries_kernel, [(2, BLOCK, 2 * HALF + 128)], base_queries[0], output_gradient[0], adapter_input[0].T,
         name="pack_queries", dtype=BF16,
     )
-    first = move(own, *row, (last, 0, 1))
-    cross = move(own, (last - 1, 0, 1), (last - 2, last, 1))
+    cross = move(own, (last, 1, 1), (last - 1, 0, 1), (last - 2, 2, 1))
+    first = move(own, *row)
     qg = exchange(qg, "core").reshape(CHUNK, 2 * HALF + 128)
     own = lax.all_gather(own, "core")
     up, dmat, rmat = (x.reshape(RANK, 2 * HALF) for x in (adapter_up_weight, direction, residual))
     size = direction.shape[1] // (n_yh * n_z * 2)
     parts = jnp.concatenate([lax.dynamic_slice_in_dim(x, idx * size, size, 1) for x in (solution, residual, direction)])
     first, own, qg, dmat, rmat, parts = lax.optimization_barrier((first, own, qg, dmat, rmat, parts))
-    second = move(first, *row)
-    passed = jnp.where((z == 0) | (z == last), cross, second)
-    third = move(passed, *row, (last, 0, 0))
-    second = jnp.where(z == 0, cross, second)
+    second = jnp.where(z <= 1, cross, move(first, *row[1:]))
+    back = move(cross, (1, 0, 0))
+    far = move(cross, (2, 0, 0))
+    third = jnp.where(z == 0, far, move(second, *row))
+    first = jnp.where(z == 0, back, first)
     chunks = [lax.all_gather(x, "core") for x in (third, second, first)] + [own]
 
     terms = attend(core.reshape(1), qg, chunks, up, dmat, rmat)

time: 116 us -> 115 us (level)
  starting transfers between devices: 24.2 us -> 30.2 us
  waiting for transfers between devices: 24.2 us -> 18.2 us
    ppermute x4 -> x6, starting transfers between devices: 11.4 us -> 17.3 us  [move(): return lax.ppermute(x, CTX, moves(n_yh, n_z, kinds))]
    ppermute x4 -> x6, waiting for transfers between devices: 13 us -> 7.1 us  [move(): return lax.ppermute(x, CTX, moves(n_yh, n_z, kinds))]
  transfers between devices with their start and end apart: 6 -> 8, of which waited for: 3 -> 2; matrix products, arithmetic and copies ran while one was open for 3% -> 3% of each run, Pallas kernels for 2% -> 2%
where the time goes in v6:
time: 115 us
  blocking collectives  43.4 us (38%)
  starting transfers between devices  30.2 us (26%)
  waiting for transfers between devices  18.2 us (16%)
  Pallas kernels  16.7 us (15%)
  other arithmetic  3.23 us (3%)
  between operations  1.46 us (1%)
  local copies, waits for them, and re-layouts  1.3 us (1%)
    all_to_all x2, blocking collectives, exchange(): return lax.all_to_all(x, axes, 0, 0, tiled=True)  33.8 us
    ppermute x6, starting transfers between devices, move(): return lax.ppermute(x, CTX, moves(n_yh, n_z, kinds))  17.3 us
    all_to_all x2, starting transfers between devices, exchange(): return lax.all_to_all(x, axes, 0, 0, tiled=True)  12.9 us
    all_to_all x2, waiting for transfers between devices, exchange(): return lax.all_to_all(x, axes, 0, 0, tiled=True)  11.1 us
    pallas_call x1, Pallas kernels, attend(): pl.pallas_call(attend_kernel, out_shape=jax.ShapeDtypeStruct((RANK, GROUP...  9.41 us
    all_gather x3, blocking collectives, per_device(): chunks = [lax.all_gather(x, 'core') for x in (third, second, first)] + [own]  7.39 us
    pallas_call x4, Pallas kernels, in_vmem(): pl.pallas_call(kernel, out_shape=[jax.ShapeDtypeStruct(s, dtype) for s in...  7.33 us
    ppermute x6, waiting for transfers between devices, move(): return lax.ppermute(x, CTX, moves(n_yh, n_z, kinds))  7.1 us
  transfers between devices with their start and end apart: 8, of which 2 were waited for; matrix products, arithmetic and copies ran while one was open for 3% of the time, Pallas kernels for 2%

profile of v6, /device:TPU:1, one launch (start us, length us, event | category | flops | bytes accessed | tf_op | source)
XLA Modules:
  0.0 114.5 jit_solution(5995990890314473276)
XLA Ops:
  0.6 0.0 copy-start
  0.6 1.8 %pack.1 = bf16[144,1024]{1,0:T(8,128)(2,1)} custom-call(bf16[128,512]{1,0:T(8,128)(2,1)} %bitcast.22, bf16[128,512]{1,0:T(8,128)(2,1)} %bitcast.23, s32[1,128]{1,0:T(1,128)} %seg.1), custom_call_target="tpu_custom_call" | custom-call | tf_op jit(solution)/shard_map/pack/pallas_call | solution.py:268
  2.4 4.8 %collective-permute-start = (bf16[144,1024]{1,0:T(8,128)(2,1)}, bf16[144,1024]{1,0:T(8,128)(2,1)S(1)}, u32[]{:S(2)}, u32[]{:S(2)}) collective-permute-start(bf16[144,1024]{1,0:T(8,128)(2,1)} %pack.1), channel_id=1, source_target_pairs={{0,2},{1,3},{16,18},{17,19},{32,34},{33,35},{48,50},{49,51},{2,4},... | collective-permute-start | bytes 884744 | tf_op jit(solution)/shard_map/ppermute | solution.py:306
  7.3 0.7 collective-permute-start.1
  7.9 2.3 %pack_queries.1 = bf16[2,128,2176]{2,1,0:T(8,128)(2,1)} custom-call(bf16[128,2048]{1,0:T(8,128)(2,1)} %bitcast.20, bf16[128,2048]{1,0:T(8,128)(2,1)} %bitcast.21, bf16[16,128]{1,0:T(8,128)(2,1)} %bitcast.24), custom_call_target="tpu_custom_call" | custom-call | tf_op jit(solution)/shard_map/pack_queries/pallas_call | solution.py:268
  10.3 7.1 %all-to-all-start = ((bf16[2,128,2176]{2,1,0:T(8,128)(2,1)}), bf16[2,128,2176]{2,1,0:T(8,128)(2,1)S(1)}, u32[]{:S(2)}, u32[]{:S(2)}) async-start(bf16[2,128,2176]{2,1,0:T(8,128)(2,1)} %pack_queries.1), calls=%async_computation | async-start | bytes 2228224 | tf_op jit(solution)/shard_map/all_to_all | solution.py:278
  17.4 2.2 %all-gather = bf16[288,1024]{1,0:T(8,128)(2,1)S(1)} all-gather(bf16[144,1024]{1,0:T(8,128)(2,1)S(1)} %copy-done.2), channel_id=2, replica_groups=mesh['task'=8,'yh'=4,'z'=8,'core'=2] {'core'}, dimensions={0}, use_global_device_ids=true | all-gather | bytes 884736 | tf_op jit(solution)/shard_map/all_gather | solution.py:318
  19.6 0.6 pad_maximum_fusion.parts
  20.2 0.5 broadcast.7
  20.7 0.9 reduce.6
  21.7 1.0 reduce.7
  22.7 0.0 all-to-all-done
  22.7 1.4 %collective-permute-start.3 = (bf16[144,1024]{1,0:T(8,128)(2,1)S(1)}, bf16[144,1024]{1,0:T(8,128)(2,1)}, u32[]{:S(2)}, u32[]{:S(2)}) collective-permute-start(bf16[144,1024]{1,0:T(8,128)(2,1)S(1)} %collective-permute-done), channel_id=1, source_target_pairs={{2,4},{3,5},{18,20},{19,21},{34,36},{35,37},{50,52},{51,53},{4,6},... | collective-permute-start | bytes 884744 | tf_op jit(solution)/shard_map/ppermute | solution.py:306
  24.1 1.3 %collective-permute-start.5 = (bf16[144,1024]{1,0:T(8,128)(2,1)S(1)}, bf16[144,1024]{1,0:T(8,128)(2,1)S(1)}, u32[]{:S(2)}, u32[]{:S(2)}) collective-permute-start(bf16[144,1024]{1,0:T(8,128)(2,1)S(1)} %collective-permute-done.1), channel_id=1, source_target_pairs={{2,0},{3,1},{18,16},{19,17},{34,32},{35,33},{50,48},{51,49},{66,64... | collective-permute-start | bytes 884744 | tf_op jit(solution)/shard_map/ppermute | solution.py:306
  25.4 1.3 %collective-permute-start.2 = (bf16[144,1024]{1,0:T(8,128)(2,1)S(1)}, bf16[144,1024]{1,0:T(8,128)(2,1)S(1)}, u32[]{:S(2)}, u32[]{:S(2)}) collective-permute-start(bf16[144,1024]{1,0:T(8,128)(2,1)S(1)} %collective-permute-done.1), channel_id=1, source_target_pairs={{4,0},{5,1},{20,16},{21,17},{36,32},{37,33},{52,48},{53,49},{68,64... | collective-permute-start | bytes 884744 | tf_op jit(solution)/shard_map/ppermute | solution.py:306
  26.7 0.0 collective-permute-done.3
  26.8 7.9 %collective-permute-start.4 = (bf16[144,1024]{1,0:T(8,128)(2,1)S(1)}, bf16[144,1024]{1,0:T(8,128)(2,1)S(1)}, u32[]{:S(2)}, u32[]{:S(2)}) collective-permute-start(bf16[144,1024]{1,0:T(8,128)(2,1)S(1)} %broadcast_select_fusion), channel_id=1, source_target_pairs={{0,2},{1,3},{16,18},{17,19},{32,34},{33,35},{48,50},{49,51},{2,4},... | collective-permute-start | bytes 884744 | tf_op jit(solution)/shard_map/ppermute | solution.py:306
  34.6 7.1 %collective-permute-done.5 = bf16[144,1024]{1,0:T(8,128)(2,1)S(1)} collective-permute-done((bf16[144,1024]{1,0:T(8,128)(2,1)S(1)}, bf16[144,1024]{1,0:T(8,128)(2,1)S(1)}, u32[]{:S(2)}, u32[]{:S(2)}) %collective-permute-start.5) | collective-permute-done | bytes 294944 | tf_op jit(solution)/shard_map/ppermute | solution.py:306
  41.8 2.8 %all-gather.2 = bf16[288,1024]{1,0:T(8,128)(2,1)S(1)} all-gather(bf16[144,1024]{1,0:T(8,128)(2,1)S(1)} %broadcast_select_fusion), channel_id=4, replica_groups=mesh['task'=8,'yh'=4,'z'=8,'core'=2] {'core'}, dimensions={0}, use_global_device_ids=true | all-gather | bytes 884736 | tf_op jit(solution)/shard_map/all_gather | solution.py:328
  44.6 2.3 %all-gather.3 = bf16[288,1024]{1,0:T(8,128)(2,1)S(1)} all-gather(bf16[144,1024]{1,0:T(8,128)(2,1)S(1)} %broadcast_select_fusion.1), channel_id=5, replica_groups=mesh['task'=8,'yh'=4,'z'=8,'core'=2] {'core'}, dimensions={0}, use_global_device_ids=true | all-gather | bytes 884736 | tf_op jit(solution)/shard_map/all_gather | solution.py:328
  46.9 0.0 collective-permute-done.4
  47.0 2.2 %all-gather.1 = bf16[288,1024]{1,0:T(8,128)(2,1)S(1)} all-gather(bf16[144,1024]{1,0:T(8,128)(2,1)S(1)} %broadcast_select_fusion.2), channel_id=3, replica_groups=mesh['task'=8,'yh'=4,'z'=8,'core'=2] {'core'}, dimensions={0}, use_global_device_ids=true | all-gather | bytes 884736 | tf_op jit(solution)/shard_map/all_gather | solution.py:328
  49.2 9.4 %attend.1 = f32[16,1280]{1,0:T(8,128)S(1)} custom-call(s32[1]{0:T(128)} %bitcast.core_ref, bf16[256,2176]{1,0:T(8,128)(2,1)S(1)} %bitcast.14, bf16[2,144,1024]{2,1,0:T(8,128)(2,1)S(1)} %bitcast.18, bf16[2,144,1024]{2,1,0:T(8,128)(2,1)S(1)} %bitcast.16, bf16[2,144,1024]{2,1,0:T(8,128)(2,1)S(1)} %bitcast.17, bf16[2,144,1024]{2,1,0:T(8,128)(2,1)S(1)} %bitcast.15, ...), custom_call_target="tpu_custom_call" | custom-call | flops 2000000000 | bytes 4000000 | tf_op jit(solution)/shard_map/attend/pallas_call | solution.py:206
  58.6 0.1 reshape.31
  58.7 24.2 %all_to_all.20.got = f32[32,1,640]{2,1,0:T(1,128)} all-to-all(f32[32,1,640]{2,1,0:T(1,128)S(1)} %reshape.31), channel_id=1, replica_groups=mesh['task'=8,'yh'=4,'z'=8,'core'=2] {'yh','z'}, dimensions={0} | all-to-all | bytes 163840 | tf_op jit(solution)/shard_map/all_to_all | solution.py:278
  82.9 1.7 %norm.1 = (f32[1,512]{1,0:T(1,128)}, f32[64,1,128]{2,1,0:T(1,128)}) custom-call(f32[32,1,640]{2,1,0:T(1,128)} %all_to_all.20.got), custom_call_target="tpu_custom_call" | custom-call | tf_op jit(solution)/shard_map/norm/pallas_call | solution.py:268
  84.5 5.8 %all-to-all-start.2 = ((f32[64,1,128]{2,1,0:T(1,128)}), f32[64,1,128]{2,1,0:T(1,128)S(1)}, u32[]{:S(2)}, u32[]{:S(2)}) async-start(f32[64,1,128]{2,1,0:T(1,128)} %get-tuple-element.21), calls=%async_computation.2 | async-start | bytes 65536 | tf_op jit(solution)/shard_map/all_to_all | solution.py:278
  91.0 11.1 %all-to-all-done.2.got = f32[64,1,128]{2,1,0:T(1,128)S(1)} async-done(((f32[64,1,128]{2,1,0:T(1,128)}), f32[64,1,128]{2,1,0:T(1,128)S(1)}, u32[]{:S(2)}, u32[]{:S(2)}) %all-to-all-start.2) | async-done | bytes 32800 | tf_op jit(solution)/shard_map/all_to_all | solution.py:278
  102.1 0.6 copy-done.5
  102.8 1.6 %update.1 = (f32[1,512]{1,0:T(1,128)}, f32[1,512]{1,0:T(1,128)}, f32[1,512]{1,0:T(1,128)}, f32[8,1,512]{2,1,0:T(1,128)}) custom-call(f32[1]{0:T(128)S(6)} %copy.15.damping, f32[64,1,128]{2,1,0:T(1,128)} %copy-done.5, f32[1,512]{1,0:T(1,128)} %get-tuple-element.22.h_all, f32[3,512]{1,0:T(4,128)} %pad_maximum_fusion.parts), custom_call_target="tpu_custom_call" | custom-call | tf_op jit(solution)/shard_map/update/pallas_call | solution.py:268
  104.3 9.6 %all_to_all.21 = f32[8,1,512]{2,1,0:T(1,128)S(1)} all-to-all(f32[8,1,512]{2,1,0:T(1,128)} %get-tuple-element.27), channel_id=1, replica_groups=mesh['task'=8,'yh'=4,'z'=8,'core'=2] {'task'}, dimensions={0} | all-to-all | bytes 32768 | tf_op jit(solution)/shard_map/all_to_all | solution.py:278
  113.9 0.6 broadcast_multiply_fusion
  (21 shorter events, 0.2 us)
Async XLA Ops:
  0.6 16.7 %copy-start = (f32[1,32768]{1,0:T(1,128)S(1)}, f32[1,32768]{1,0:T(1,128)}, u32[]{:S(2)}) copy-start(f32[1,32768]{1,0:T(1,128)} %param.18) | copy-start | bytes 393220
  2.4 20.3 %collective-permute-start = (bf16[144,1024]{1,0:T(8,128)(2,1)}, bf16[144,1024]{1,0:T(8,128)(2,1)S(1)}, u32[]{:S(2)}, u32[]{:S(2)}) collective-permute-start(bf16[144,1024]{1,0:T(8,128)(2,1)} %pack.1), channel_id=1, source_target_pairs={{0,2},{1,3},{16,18},{17,19},{32,34},{33,35},{48,50},{49,51},{2,4},... | collective-permute-start | bytes 884744 | tf_op jit(solution)/shard_map/ppermute | solution.py:306
  7.3 16.8 %collective-permute-start.1 = (bf16[144,1024]{1,0:T(8,128)(2,1)}, bf16[144,1024]{1,0:T(8,128)(2,1)S(1)}, u32[]{:S(2)}, u32[]{:S(2)}) collective-permute-start(bf16[144,1024]{1,0:T(8,128)(2,1)} %pack.1), channel_id=1, source_target_pairs={{14,18},{15,19},{30,34},{31,35},{46,50},{47,51},{12,16},{13,17},{2... | collective-permute-start | bytes 884744 | tf_op jit(solution)/shard_map/ppermute | solution.py:306
  10.3 7.1 %copy-start.3 = (f32[1,32768]{1,0:T(1,128)S(1)}, f32[1,32768]{1,0:T(1,128)}, u32[]{:S(2)}) copy-start(f32[1,32768]{1,0:T(1,128)} %param.20) | copy-start | bytes 393220
  10.3 7.1 %copy-start.4 = (f32[1,32768]{1,0:T(1,128)S(1)}, f32[1,32768]{1,0:T(1,128)}, u32[]{:S(2)}) copy-start(f32[1,32768]{1,0:T(1,128)} %param.19) | copy-start | bytes 393220
  10.3 7.1 %copy-start.2 = (bf16[144,1024]{1,0:T(8,128)(2,1)S(1)}, bf16[144,1024]{1,0:T(8,128)(2,1)}, u32[]{:S(2)}) copy-start(bf16[144,1024]{1,0:T(8,128)(2,1)} %pack.1) | copy-start | bytes 884740
  10.3 12.4 %all-to-all-start = ((bf16[2,128,2176]{2,1,0:T(8,128)(2,1)}), bf16[2,128,2176]{2,1,0:T(8,128)(2,1)S(1)}, u32[]{:S(2)}, u32[]{:S(2)}) async-start(bf16[2,128,2176]{2,1,0:T(8,128)(2,1)} %pack_queries.1), calls=%async_computation | async-start | bytes 2228224 | tf_op jit(solution)/shard_map/all_to_all | solution.py:278
  22.7 4.0 %collective-permute-start.3 = (bf16[144,1024]{1,0:T(8,128)(2,1)S(1)}, bf16[144,1024]{1,0:T(8,128)(2,1)}, u32[]{:S(2)}, u32[]{:S(2)}) collective-permute-start(bf16[144,1024]{1,0:T(8,128)(2,1)S(1)} %collective-permute-done), channel_id=1, source_target_pairs={{2,4},{3,5},{18,20},{19,21},{34,36},{35,37},{50,52},{51,53},{4,6},... | collective-permute-start | bytes 884744 | tf_op jit(solution)/shard_map/ppermute | solution.py:306
  24.1 17.6 %collective-permute-start.5 = (bf16[144,1024]{1,0:T(8,128)(2,1)S(1)}, bf16[144,1024]{1,0:T(8,128)(2,1)S(1)}, u32[]{:S(2)}, u32[]{:S(2)}) collective-permute-start(bf16[144,1024]{1,0:T(8,128)(2,1)S(1)} %collective-permute-done.1), channel_id=1, source_target_pairs={{2,0},{3,1},{18,16},{19,17},{34,32},{35,33},{50,48},{51,49},{66,64... | collective-permute-start | bytes 884744 | tf_op jit(solution)/shard_map/ppermute | solution.py:306
  25.4 21.5 %collective-permute-start.2 = (bf16[144,1024]{1,0:T(8,128)(2,1)S(1)}, bf16[144,1024]{1,0:T(8,128)(2,1)S(1)}, u32[]{:S(2)}, u32[]{:S(2)}) collective-permute-start(bf16[144,1024]{1,0:T(8,128)(2,1)S(1)} %collective-permute-done.1), channel_id=1, source_target_pairs={{4,0},{5,1},{20,16},{21,17},{36,32},{37,33},{52,48},{53,49},{68,64... | collective-permute-start | bytes 884744 | tf_op jit(solution)/shard_map/ppermute | solution.py:306
  26.8 20.2 %collective-permute-start.4 = (bf16[144,1024]{1,0:T(8,128)(2,1)S(1)}, bf16[144,1024]{1,0:T(8,128)(2,1)S(1)}, u32[]{:S(2)}, u32[]{:S(2)}) collective-permute-start(bf16[144,1024]{1,0:T(8,128)(2,1)S(1)} %broadcast_select_fusion), channel_id=1, source_target_pairs={{0,2},{1,3},{16,18},{17,19},{32,34},{33,35},{48,50},{49,51},{2,4},... | collective-permute-start | bytes 884744 | tf_op jit(solution)/shard_map/ppermute | solution.py:306
  44.6 4.6 %copy-start.1 = (bf16[1,16,2048]{2,1,0:T(8,128)(2,1)S(1)}, bf16[1,16,2048]{2,1,0:T(8,128)(2,1)}, u32[]{:S(2)}) copy-start(bf16[1,16,2048]{2,1,0:T(8,128)(2,1)} %param.13) | copy-start | bytes 196612
  84.5 17.6 %all-to-all-start.2 = ((f32[64,1,128]{2,1,0:T(1,128)}), f32[64,1,128]{2,1,0:T(1,128)S(1)}, u32[]{:S(2)}, u32[]{:S(2)}) async-start(f32[64,1,128]{2,1,0:T(1,128)} %get-tuple-element.21), calls=%async_computation.2 | async-start | bytes 65536 | tf_op jit(solution)/shard_map/all_to_all | solution.py:278
  102.1 0.6 copy-start.5

commit v7 on v6

--- a/solution.py
+++ b/solution.py
@@ -13,7 +13,7 @@
 BLOCK = 128
 CHUNK = 2 * BLOCK
 SPAN = 3
-WINDOW = 7 * BLOCK
+KEYS = (SPAN + 1) * CHUNK
 GROUPS = 2
 PER_GROUP = 4
 HALF = GROUPS * PER_GROUP * HEAD_DIM
@@ -105,7 +105,7 @@
     def scores(n):
         g, b, pair = steps[n]
         slot = n % 3
-        win = slice(b * BLOCK, b * BLOCK + WINDOW)
+        win = slice(0, KEYS - (1 - b) * BLOCK)
         own = slice(b * BLOCK, (b + 1) * BLOCK)
 
         def two(ref, base):
@@ -116,26 +116,27 @@
         q, t, r = (jnp.concatenate(x, axis=0) for x in (q2, two(ts, 0), two(qg, HALF)))
 
         def do_s():
-            s_ref[slot] = dot(keys[g, win, :], q, NT)
+            s_ref[slot, win, :] = dot(keys[g, win, :], q, NT)
 
         def do_t():
-            t_ref[slot] = dot(keys[g, win, :HEAD_DIM], t, NT)
+            t_ref[slot, win, :] = dot(keys[g, win, :HEAD_DIM], t, NT)
 
         def do_u():
-            u_ref[slot] = dot(vals[g, win, :], r, NT)
+            u_ref[slot, win, :] = dot(vals[g, win, :], r, NT)
 
         return [do_s, do_t, do_u]
 
     def weigh(n, ahead):
         slot = n % 3
+        blocks = 7 + steps[n][1]
         scales = []
         for e in range(2):
             lanes = slice(e * BLOCK, (e + 1) * BLOCK)
             m8 = None
-            for w in range(6, -1, -1):
+            for w in range(blocks - 1, -1, -1):
                 rows = slice(w * BLOCK, (w + 1) * BLOCK)
                 s = s_ref[slot, rows, lanes]
-                if w == 6:
+                if w == blocks - 1:
                     s = s + tri
                 top = jnp.max(fold(s), axis=0)
                 m8 = top if m8 is None else jnp.maximum(m8, top)
@@ -143,10 +144,10 @@
             if ahead:
                 ahead.pop(0)()
             z8 = et8 = eu8 = etu8 = jnp.zeros((8, BLOCK), F32)
-            for w in range(7):
+            for w in range(blocks):
                 rows = slice(w * BLOCK, (w + 1) * BLOCK)
                 s = s_ref[slot, rows, lanes]
-                if w == 6:
+                if w == blocks - 1:
                     s = s + tri
                 ex = jnp.exp2((s - m) * cexp)
                 s_ref[slot, rows, lanes] = ex
@@ -160,7 +161,7 @@
             mt = jnp.sum(et8, axis=0, keepdims=True) * inv
             mu = jnp.sum(eu8, axis=0, keepdims=True) * inv
             cov = jnp.sum(etu8, axis=0, keepdims=True) * inv - mt * mu
-            for w in range(7):
+            for w in range(blocks):
                 rows = slice(w * BLOCK, (w + 1) * BLOCK)
                 coef = s_ref[slot, rows, lanes] * (
                     (t_ref[slot, rows, lanes] - mt) * (u_ref[slot, rows, lanes] - mu) - cov
@@ -174,7 +175,8 @@
     def gather(n, scales):
         g, b, pair = steps[n]
         slot = n % 3
-        hv = dot(keys_t[g, :, b * BLOCK : b * BLOCK + WINDOW], c_ref[slot])
+        win = slice(0, KEYS - (1 - b) * BLOCK)
+        hv = dot(keys_t[g, :, win], c_ref[slot, win, :])
         ab = at[:, b * BLOCK : (b + 1) * BLOCK]
         for e in range(2):
             lanes = slice(e * BLOCK, (e + 1) * BLOCK)
@@ -218,10 +220,10 @@
             vm((CHUNK, HALF), BF16),
             vm((RANK, CHUNK), BF16),
             vm((2, BLOCK, BLOCK), BF16),
-            vm((3, WINDOW, CHUNK), F32),
-            vm((3, WINDOW, CHUNK), F32),
-            vm((3, WINDOW, CHUNK), F32),
-            vm((3, WINDOW, CHUNK), BF16),
+            vm((3, KEYS, CHUNK), F32),
+            vm((3, KEYS, CHUNK), F32),
+            vm((3, KEYS, CHUNK), F32),
+            vm((3, KEYS, CHUNK), BF16),
         ],
         compiler_params=pltpu.CompilerParams(vmem_limit_bytes=48 * 1024 * 1024),
         cost_estimate=pl.CostEstimate(flops=2_000_000_000, bytes_accessed=4_000_000, transcendentals=2_000_000),
@@ -323,9 +325,9 @@
     second = jnp.where(z <= 1, cross, move(first, *row[1:]))
     back = move(cross, (1, 0, 0))
     far = move(cross, (2, 0, 0))
-    third = jnp.where(z == 0, far, move(second, *row))
-    first = jnp.where(z == 0, back, first)
-    chunks = [lax.all_gather(x, "core") for x in (third, second, first)] + [own]
+    third = move(second, *row)
+    chunks = [jnp.where(z == 0, back, third), second, jnp.where(z == 0, far, first)]
+    chunks = [lax.all_gather(x, "core") for x in chunks] + [own]
 
     terms = attend(core.reshape(1), qg, chunks, up, dmat, rmat)
 

time: 115 us -> 116 us (level)
  waiting for transfers between devices: 18.2 us -> 14.3 us
  blocking collectives: 43.4 us -> 47 us
    ppermute x6, waiting for transfers between devices: 7.1 us -> 3.16 us  [move(): return lax.ppermute(x, CTX, moves(n_yh, n_z, kinds))]
    all_to_all x2, blocking collectives: 33.8 us -> 37.3 us  [exchange(): return lax.all_to_all(x, axes, 0, 0, tiled=True)]
where the time goes in v7:
time: 116 us; the launch traced here: 115 us
  blocking collectives  47 us (41%)
  starting transfers between devices  30.2 us (26%)
  Pallas kernels  17.4 us (15%)
  waiting for transfers between devices  14.3 us (12%)
  other arithmetic  3.23 us (3%)
  between operations  1.46 us (1%)
  local copies, waits for them, and re-layouts  1.3 us (1%)
    all_to_all x2, blocking collectives, exchange(): return lax.all_to_all(x, axes, 0, 0, tiled=True)  37.3 us
    ppermute x6, starting transfers between devices, move(): return lax.ppermute(x, CTX, moves(n_yh, n_z, kinds))  17.3 us
    all_to_all x2, starting transfers between devices, exchange(): return lax.all_to_all(x, axes, 0, 0, tiled=True)  12.9 us
    all_to_all x2, waiting for transfers between devices, exchange(): return lax.all_to_all(x, axes, 0, 0, tiled=True)  11.1 us
    pallas_call x1, Pallas kernels, attend(): pl.pallas_call(attend_kernel, out_shape=jax.ShapeDtypeStruct((RANK, GROUP...  10.1 us
    all_gather x3, blocking collectives, per_device(): chunks = [lax.all_gather(x, 'core') for x in chunks] + [own]  7.45 us
    pallas_call x4, Pallas kernels, in_vmem(): pl.pallas_call(kernel, out_shape=[jax.ShapeDtypeStruct(s, dtype) for s in...  7.33 us
    ppermute x6, waiting for transfers between devices, move(): return lax.ppermute(x, CTX, moves(n_yh, n_z, kinds))  3.16 us
  transfers between devices with their start and end apart: 8, of which 2 were waited for; matrix products, arithmetic and copies ran while one was open for 3% of the time, Pallas kernels for 2%

profile of v7, /device:TPU:1, one launch (start us, length us, event | category | flops | bytes accessed | tf_op | source)
XLA Modules:
  0.0 114.9 jit_solution(18414122211881972553)
XLA Ops:
  0.6 0.0 copy-start
  0.6 1.8 %pack.1 = bf16[144,1024]{1,0:T(8,128)(2,1)} custom-call(bf16[128,512]{1,0:T(8,128)(2,1)} %bitcast.22, bf16[128,512]{1,0:T(8,128)(2,1)} %bitcast.23, s32[1,128]{1,0:T(1,128)} %seg.1), custom_call_target="tpu_custom_call" | custom-call | tf_op jit(solution)/shard_map/pack/pallas_call | solution.py:270
  2.4 4.8 %collective-permute-start = (bf16[144,1024]{1,0:T(8,128)(2,1)}, bf16[144,1024]{1,0:T(8,128)(2,1)S(1)}, u32[]{:S(2)}, u32[]{:S(2)}) collective-permute-start(bf16[144,1024]{1,0:T(8,128)(2,1)} %pack.1), channel_id=1, source_target_pairs={{0,2},{1,3},{16,18},{17,19},{32,34},{33,35},{48,50},{49,51},{2,4},... | collective-permute-start | bytes 884744 | tf_op jit(solution)/shard_map/ppermute | solution.py:308
  7.3 0.7 collective-permute-start.1
  7.9 2.3 %pack_queries.1 = bf16[2,128,2176]{2,1,0:T(8,128)(2,1)} custom-call(bf16[128,2048]{1,0:T(8,128)(2,1)} %bitcast.20, bf16[128,2048]{1,0:T(8,128)(2,1)} %bitcast.21, bf16[16,128]{1,0:T(8,128)(2,1)} %bitcast.24), custom_call_target="tpu_custom_call" | custom-call | tf_op jit(solution)/shard_map/pack_queries/pallas_call | solution.py:270
  10.3 7.1 %all-to-all-start = ((bf16[2,128,2176]{2,1,0:T(8,128)(2,1)}), bf16[2,128,2176]{2,1,0:T(8,128)(2,1)S(1)}, u32[]{:S(2)}, u32[]{:S(2)}) async-start(bf16[2,128,2176]{2,1,0:T(8,128)(2,1)} %pack_queries.1), calls=%async_computation | async-start | bytes 2228224 | tf_op jit(solution)/shard_map/all_to_all | solution.py:280
  17.4 2.2 %all-gather = bf16[288,1024]{1,0:T(8,128)(2,1)S(1)} all-gather(bf16[144,1024]{1,0:T(8,128)(2,1)S(1)} %copy-done.2), channel_id=2, replica_groups=mesh['task'=8,'yh'=4,'z'=8,'core'=2] {'core'}, dimensions={0}, use_global_device_ids=true | all-gather | bytes 884736 | tf_op jit(solution)/shard_map/all_gather | solution.py:320
  19.6 0.6 pad_maximum_fusion.parts
  20.2 0.5 broadcast.7
  20.7 0.9 reduce.6
  21.7 1.0 reduce.7
  22.7 0.0 all-to-all-done
  22.7 1.4 %collective-permute-start.3 = (bf16[144,1024]{1,0:T(8,128)(2,1)S(1)}, bf16[144,1024]{1,0:T(8,128)(2,1)}, u32[]{:S(2)}, u32[]{:S(2)}) collective-permute-start(bf16[144,1024]{1,0:T(8,128)(2,1)S(1)} %collective-permute-done), channel_id=1, source_target_pairs={{2,4},{3,5},{18,20},{19,21},{34,36},{35,37},{50,52},{51,53},{4,6},... | collective-permute-start | bytes 884744 | tf_op jit(solution)/shard_map/ppermute | solution.py:308
  24.1 1.3 %collective-permute-start.5 = (bf16[144,1024]{1,0:T(8,128)(2,1)S(1)}, bf16[144,1024]{1,0:T(8,128)(2,1)S(1)}, u32[]{:S(2)}, u32[]{:S(2)}) collective-permute-start(bf16[144,1024]{1,0:T(8,128)(2,1)S(1)} %collective-permute-done.1), channel_id=1, source_target_pairs={{4,0},{5,1},{20,16},{21,17},{36,32},{37,33},{52,48},{53,49},{68,64... | collective-permute-start | bytes 884744 | tf_op jit(solution)/shard_map/ppermute | solution.py:308
  25.4 1.3 %collective-permute-start.2 = (bf16[144,1024]{1,0:T(8,128)(2,1)S(1)}, bf16[144,1024]{1,0:T(8,128)(2,1)S(1)}, u32[]{:S(2)}, u32[]{:S(2)}) collective-permute-start(bf16[144,1024]{1,0:T(8,128)(2,1)S(1)} %collective-permute-done.1), channel_id=1, source_target_pairs={{2,0},{3,1},{18,16},{19,17},{34,32},{35,33},{50,48},{51,49},{66,64... | collective-permute-start | bytes 884744 | tf_op jit(solution)/shard_map/ppermute | solution.py:308
  26.7 0.0 collective-permute-done.3
  26.8 7.9 %collective-permute-start.4 = (bf16[144,1024]{1,0:T(8,128)(2,1)S(1)}, bf16[144,1024]{1,0:T(8,128)(2,1)S(1)}, u32[]{:S(2)}, u32[]{:S(2)}) collective-permute-start(bf16[144,1024]{1,0:T(8,128)(2,1)S(1)} %broadcast_select_fusion), channel_id=1, source_target_pairs={{0,2},{1,3},{16,18},{17,19},{32,34},{33,35},{48,50},{49,51},{2,4},... | collective-permute-start | bytes 884744 | tf_op jit(solution)/shard_map/ppermute | solution.py:308
  34.6 3.1 %collective-permute-done.5 = bf16[144,1024]{1,0:T(8,128)(2,1)S(1)} collective-permute-done((bf16[144,1024]{1,0:T(8,128)(2,1)S(1)}, bf16[144,1024]{1,0:T(8,128)(2,1)S(1)}, u32[]{:S(2)}, u32[]{:S(2)}) %collective-permute-start.5) | collective-permute-done | bytes 294944 | tf_op jit(solution)/shard_map/ppermute | solution.py:308
  37.8 2.9 %all-gather.2 = bf16[288,1024]{1,0:T(8,128)(2,1)S(1)} all-gather(bf16[144,1024]{1,0:T(8,128)(2,1)S(1)} %broadcast_select_fusion), channel_id=4, replica_groups=mesh['task'=8,'yh'=4,'z'=8,'core'=2] {'core'}, dimensions={0}, use_global_device_ids=true | all-gather | bytes 884736 | tf_op jit(solution)/shard_map/all_gather | solution.py:330
  40.7 2.3 %all-gather.3 = bf16[288,1024]{1,0:T(8,128)(2,1)S(1)} all-gather(bf16[144,1024]{1,0:T(8,128)(2,1)S(1)} %broadcast_select_fusion.1), channel_id=5, replica_groups=mesh['task'=8,'yh'=4,'z'=8,'core'=2] {'core'}, dimensions={0}, use_global_device_ids=true | all-gather | bytes 884736 | tf_op jit(solution)/shard_map/all_gather | solution.py:330
  43.0 0.0 collective-permute-done.2
  43.1 2.2 %all-gather.1 = bf16[288,1024]{1,0:T(8,128)(2,1)S(1)} all-gather(bf16[144,1024]{1,0:T(8,128)(2,1)S(1)} %broadcast_select_fusion.2), channel_id=3, replica_groups=mesh['task'=8,'yh'=4,'z'=8,'core'=2] {'core'}, dimensions={0}, use_global_device_ids=true | all-gather | bytes 884736 | tf_op jit(solution)/shard_map/all_gather | solution.py:330
  45.3 10.1 %attend.1 = f32[16,1280]{1,0:T(8,128)S(1)} custom-call(s32[1]{0:T(128)} %bitcast.core_ref, bf16[256,2176]{1,0:T(8,128)(2,1)S(1)} %bitcast.14, bf16[2,144,1024]{2,1,0:T(8,128)(2,1)S(1)} %bitcast.18, bf16[2,144,1024]{2,1,0:T(8,128)(2,1)S(1)} %bitcast.16, bf16[2,144,1024]{2,1,0:T(8,128)(2,1)S(1)} %bitcast.17, bf16[2,144,1024]{2,1,0:T(8,128)(2,1)S(1)} %bitcast.15, ...), custom_call_target="tpu_custom_call" | custom-call | flops 2000000000 | bytes 4000000 | tf_op jit(solution)/shard_map/attend/pallas_call | solution.py:208
  55.4 0.1 reshape.31
  55.5 28.1 %all_to_all.20.got = f32[32,1,640]{2,1,0:T(1,128)} all-to-all(f32[32,1,640]{2,1,0:T(1,128)S(1)} %reshape.31), channel_id=1, replica_groups=mesh['task'=8,'yh'=4,'z'=8,'core'=2] {'yh','z'}, dimensions={0} | all-to-all | bytes 163840 | tf_op jit(solution)/shard_map/all_to_all | solution.py:280
  83.5 1.7 %norm.1 = (f32[1,512]{1,0:T(1,128)}, f32[64,1,128]{2,1,0:T(1,128)}) custom-call(f32[32,1,640]{2,1,0:T(1,128)} %all_to_all.20.got), custom_call_target="tpu_custom_call" | custom-call | tf_op jit(solution)/shard_map/norm/pallas_call | solution.py:270
  85.2 5.8 %all-to-all-start.2 = ((f32[64,1,128]{2,1,0:T(1,128)}), f32[64,1,128]{2,1,0:T(1,128)S(1)}, u32[]{:S(2)}, u32[]{:S(2)}) async-start(f32[64,1,128]{2,1,0:T(1,128)} %get-tuple-element.21), calls=%async_computation.2 | async-start | bytes 65536 | tf_op jit(solution)/shard_map/all_to_all | solution.py:280
  91.7 11.1 %all-to-all-done.2.got = f32[64,1,128]{2,1,0:T(1,128)S(1)} async-done(((f32[64,1,128]{2,1,0:T(1,128)}), f32[64,1,128]{2,1,0:T(1,128)S(1)}, u32[]{:S(2)}, u32[]{:S(2)}) %all-to-all-start.2) | async-done | bytes 32800 | tf_op jit(solution)/shard_map/all_to_all | solution.py:280
  102.8 0.6 copy-done.5
  103.4 1.6 %update.1 = (f32[1,512]{1,0:T(1,128)}, f32[1,512]{1,0:T(1,128)}, f32[1,512]{1,0:T(1,128)}, f32[8,1,512]{2,1,0:T(1,128)}) custom-call(f32[1]{0:T(128)S(6)} %copy.15.damping, f32[64,1,128]{2,1,0:T(1,128)} %copy-done.5, f32[1,512]{1,0:T(1,128)} %get-tuple-element.22.h_all, f32[3,512]{1,0:T(4,128)} %pad_maximum_fusion.parts), custom_call_target="tpu_custom_call" | custom-call | tf_op jit(solution)/shard_map/update/pallas_call | solution.py:270
  105.0 9.3 %all_to_all.21 = f32[8,1,512]{2,1,0:T(1,128)S(1)} all-to-all(f32[8,1,512]{2,1,0:T(1,128)} %get-tuple-element.27), channel_id=1, replica_groups=mesh['task'=8,'yh'=4,'z'=8,'core'=2] {'task'}, dimensions={0} | all-to-all | bytes 32768 | tf_op jit(solution)/shard_map/all_to_all | solution.py:280
  114.3 0.6 broadcast_multiply_fusion
  (21 shorter events, 0.2 us)
Async XLA Ops:
  0.6 16.7 %copy-start = (f32[1,32768]{1,0:T(1,128)S(1)}, f32[1,32768]{1,0:T(1,128)}, u32[]{:S(2)}) copy-start(f32[1,32768]{1,0:T(1,128)} %param.18) | copy-start | bytes 393220
  2.4 20.3 %collective-permute-start = (bf16[144,1024]{1,0:T(8,128)(2,1)}, bf16[144,1024]{1,0:T(8,128)(2,1)S(1)}, u32[]{:S(2)}, u32[]{:S(2)}) collective-permute-start(bf16[144,1024]{1,0:T(8,128)(2,1)} %pack.1), channel_id=1, source_target_pairs={{0,2},{1,3},{16,18},{17,19},{32,34},{33,35},{48,50},{49,51},{2,4},... | collective-permute-start | bytes 884744 | tf_op jit(solution)/shard_map/ppermute | solution.py:308
  7.3 16.8 %collective-permute-start.1 = (bf16[144,1024]{1,0:T(8,128)(2,1)}, bf16[144,1024]{1,0:T(8,128)(2,1)S(1)}, u32[]{:S(2)}, u32[]{:S(2)}) collective-permute-start(bf16[144,1024]{1,0:T(8,128)(2,1)} %pack.1), channel_id=1, source_target_pairs={{14,18},{15,19},{30,34},{31,35},{46,50},{47,51},{12,16},{13,17},{2... | collective-permute-start | bytes 884744 | tf_op jit(solution)/shard_map/ppermute | solution.py:308
  10.3 7.1 %copy-start.3 = (f32[1,32768]{1,0:T(1,128)S(1)}, f32[1,32768]{1,0:T(1,128)}, u32[]{:S(2)}) copy-start(f32[1,32768]{1,0:T(1,128)} %param.20) | copy-start | bytes 393220
  10.3 7.1 %copy-start.4 = (f32[1,32768]{1,0:T(1,128)S(1)}, f32[1,32768]{1,0:T(1,128)}, u32[]{:S(2)}) copy-start(f32[1,32768]{1,0:T(1,128)} %param.19) | copy-start | bytes 393220
  10.3 7.1 %copy-start.2 = (bf16[144,1024]{1,0:T(8,128)(2,1)S(1)}, bf16[144,1024]{1,0:T(8,128)(2,1)}, u32[]{:S(2)}) copy-start(bf16[144,1024]{1,0:T(8,128)(2,1)} %pack.1) | copy-start | bytes 884740
  10.3 12.4 %all-to-all-start = ((bf16[2,128,2176]{2,1,0:T(8,128)(2,1)}), bf16[2,128,2176]{2,1,0:T(8,128)(2,1)S(1)}, u32[]{:S(2)}, u32[]{:S(2)}) async-start(bf16[2,128,2176]{2,1,0:T(8,128)(2,1)} %pack_queries.1), calls=%async_computation | async-start | bytes 2228224 | tf_op jit(solution)/shard_map/all_to_all | solution.py:280
  22.7 4.0 %collective-permute-start.3 = (bf16[144,1024]{1,0:T(8,128)(2,1)S(1)}, bf16[144,1024]{1,0:T(8,128)(2,1)}, u32[]{:S(2)}, u32[]{:S(2)}) collective-permute-start(bf16[144,1024]{1,0:T(8,128)(2,1)S(1)} %collective-permute-done), channel_id=1, source_target_pairs={{2,4},{3,5},{18,20},{19,21},{34,36},{35,37},{50,52},{51,53},{4,6},... | collective-permute-start | bytes 884744 | tf_op jit(solution)/shard_map/ppermute | solution.py:308
  24.1 13.7 %collective-permute-start.5 = (bf16[144,1024]{1,0:T(8,128)(2,1)S(1)}, bf16[144,1024]{1,0:T(8,128)(2,1)S(1)}, u32[]{:S(2)}, u32[]{:S(2)}) collective-permute-start(bf16[144,1024]{1,0:T(8,128)(2,1)S(1)} %collective-permute-done.1), channel_id=1, source_target_pairs={{4,0},{5,1},{20,16},{21,17},{36,32},{37,33},{52,48},{53,49},{68,64... | collective-permute-start | bytes 884744 | tf_op jit(solution)/shard_map/ppermute | solution.py:308
  25.4 17.6 %collective-permute-start.2 = (bf16[144,1024]{1,0:T(8,128)(2,1)S(1)}, bf16[144,1024]{1,0:T(8,128)(2,1)S(1)}, u32[]{:S(2)}, u32[]{:S(2)}) collective-permute-start(bf16[144,1024]{1,0:T(8,128)(2,1)S(1)} %collective-permute-done.1), channel_id=1, source_target_pairs={{2,0},{3,1},{18,16},{19,17},{34,32},{35,33},{50,48},{51,49},{66,64... | collective-permute-start | bytes 884744 | tf_op jit(solution)/shard_map/ppermute | solution.py:308
  26.8 16.3 %collective-permute-start.4 = (bf16[144,1024]{1,0:T(8,128)(2,1)S(1)}, bf16[144,1024]{1,0:T(8,128)(2,1)S(1)}, u32[]{:S(2)}, u32[]{:S(2)}) collective-permute-start(bf16[144,1024]{1,0:T(8,128)(2,1)S(1)} %broadcast_select_fusion), channel_id=1, source_target_pairs={{0,2},{1,3},{16,18},{17,19},{32,34},{33,35},{48,50},{49,51},{2,4},... | collective-permute-start | bytes 884744 | tf_op jit(solution)/shard_map/ppermute | solution.py:308
  40.7 4.6 %copy-start.1 = (bf16[1,16,2048]{2,1,0:T(8,128)(2,1)S(1)}, bf16[1,16,2048]{2,1,0:T(8,128)(2,1)}, u32[]{:S(2)}) copy-start(bf16[1,16,2048]{2,1,0:T(8,128)(2,1)} %param.13) | copy-start | bytes 196612
  85.2 17.6 %all-to-all-start.2 = ((f32[64,1,128]{2,1,0:T(1,128)}), f32[64,1,128]{2,1,0:T(1,128)S(1)}, u32[]{:S(2)}, u32[]{:S(2)}) async-start(f32[64,1,128]{2,1,0:T(1,128)} %get-tuple-element.21), calls=%async_computation.2 | async-start | bytes 65536 | tf_op jit(solution)/shard_map/all_to_all | solution.py:280
  102.8 0.6 copy-start.5

commit v8 on v7

--- a/solution.py
+++ b/solution.py
@@ -321,13 +321,17 @@
     up, dmat, rmat = (x.reshape(RANK, 2 * HALF) for x in (adapter_up_weight, direction, residual))
     size = direction.shape[1] // (n_yh * n_z * 2)
     parts = jnp.concatenate([lax.dynamic_slice_in_dim(x, idx * size, size, 1) for x in (solution, residual, direction)])
-    first, own, qg, dmat, rmat, parts = lax.optimization_barrier((first, own, qg, dmat, rmat, parts))
-    second = jnp.where(z <= 1, cross, move(first, *row[1:]))
+    first, qg = lax.optimization_barrier((first, qg))
+    second = move(first, *row[1:])
+    cross, own, dmat, rmat, parts = lax.optimization_barrier((cross, own, dmat, rmat, parts))
+    second = jnp.where(z <= 1, cross, second)
     back = move(cross, (1, 0, 0))
     far = move(cross, (2, 0, 0))
     third = move(second, *row)
-    chunks = [jnp.where(z == 0, back, third), second, jnp.where(z == 0, far, first)]
-    chunks = [lax.all_gather(x, "core") for x in chunks] + [own]
+    second = lax.all_gather(second, "core")
+    second, far, first = lax.optimization_barrier((second, far, first))
+    first = lax.all_gather(jnp.where(z == 0, far, first), "core")
+    chunks = [lax.all_gather(jnp.where(z == 0, back, third), "core"), second, first, own]
 
     terms = attend(core.reshape(1), qg, chunks, up, dmat, rmat)
 

time: 116 us -> 113 us (0.974)
  waiting for transfers between devices: 14.3 us -> 18.8 us
  starting transfers between devices: 30.2 us -> 26.3 us
  blocking collectives: 47 us -> 43.6 us
    all_to_all x2, blocking collectives: 37.3 us -> 33.2 us  [exchange(): return lax.all_to_all(x, axes, 0, 0, tiled=True)]
    ppermute x6, starting transfers between devices: 17.3 us -> 13.4 us  [move(): return lax.ppermute(x, CTX, moves(n_yh, n_z, kinds))]
    ppermute x6, waiting for transfers between devices: 3.16 us -> 5.9 us  [move(): return lax.ppermute(x, CTX, moves(n_yh, n_z, kinds))]
    all_to_all x2, waiting for transfers between devices: 11.1 us -> 12.9 us  [exchange(): return lax.all_to_all(x, axes, 0, 0, tiled=True)]
  transfers between devices with their start and end apart: 8 -> 8, of which waited for: 2 -> 4; matrix products, arithmetic and copies ran while one was open for 3% -> 3% of each run, Pallas kernels for 2% -> 2%
where the time goes in v8:
time: 113 us; the launch traced here: 112 us
  blocking collectives  43.6 us (39%)
  starting transfers between devices  26.3 us (23%)
  waiting for transfers between devices  18.8 us (17%)
  Pallas kernels  17.4 us (15%)
  other arithmetic  3.22 us (3%)
  between operations  1.46 us (1%)
  local copies, waits for them, and re-layouts  1.31 us (1%)
    all_to_all x2, blocking collectives, exchange(): return lax.all_to_all(x, axes, 0, 0, tiled=True)  33.2 us
    ppermute x6, starting transfers between devices, move(): return lax.ppermute(x, CTX, moves(n_yh, n_z, kinds))  13.4 us
    all_to_all x2, waiting for transfers between devices, exchange(): return lax.all_to_all(x, axes, 0, 0, tiled=True)  12.9 us
    all_to_all x2, starting transfers between devices, exchange(): return lax.all_to_all(x, axes, 0, 0, tiled=True)  12.9 us
    pallas_call x1, Pallas kernels, attend(): pl.pallas_call(attend_kernel, out_shape=jax.ShapeDtypeStruct((RANK, GROUP...  10 us
    pallas_call x4, Pallas kernels, in_vmem(): pl.pallas_call(kernel, out_shape=[jax.ShapeDtypeStruct(s, dtype) for s in...  7.33 us
    ppermute x6, waiting for transfers between devices, move(): return lax.ppermute(x, CTX, moves(n_yh, n_z, kinds))  5.9 us
    all_gather x1, blocking collectives, per_device(): first = lax.all_gather(jnp.where(z == 0, far, first), 'core')  2.93 us
  transfers between devices with their start and end apart: 8, of which 4 were waited for; matrix products, arithmetic and copies ran while one was open for 3% of the time, Pallas kernels for 2%

profile of v8, /device:TPU:1, one launch (start us, length us, event | category | flops | bytes accessed | tf_op | source)
XLA Modules:
  0.0 112.0 jit_solution(11167780102158995741)
XLA Ops:
  0.6 0.0 copy-start
  0.6 1.8 %pack.1 = bf16[144,1024]{1,0:T(8,128)(2,1)} custom-call(bf16[128,512]{1,0:T(8,128)(2,1)} %bitcast.22, bf16[128,512]{1,0:T(8,128)(2,1)} %bitcast.23, s32[1,128]{1,0:T(1,128)} %seg.1), custom_call_target="tpu_custom_call" | custom-call | tf_op jit(solution)/shard_map/pack/pallas_call | solution.py:270
  2.4 4.8 %collective-permute-start = (bf16[144,1024]{1,0:T(8,128)(2,1)}, bf16[144,1024]{1,0:T(8,128)(2,1)S(1)}, u32[]{:S(2)}, u32[]{:S(2)}) collective-permute-start(bf16[144,1024]{1,0:T(8,128)(2,1)} %pack.1), channel_id=1, source_target_pairs={{0,2},{1,3},{16,18},{17,19},{32,34},{33,35},{48,50},{49,51},{2,4},... | collective-permute-start | bytes 884744 | tf_op jit(solution)/shard_map/ppermute | solution.py:308
  7.3 0.7 collective-permute-start.1
  7.9 2.3 %pack_queries.1 = bf16[2,128,2176]{2,1,0:T(8,128)(2,1)} custom-call(bf16[128,2048]{1,0:T(8,128)(2,1)} %bitcast.20, bf16[128,2048]{1,0:T(8,128)(2,1)} %bitcast.21, bf16[16,128]{1,0:T(8,128)(2,1)} %bitcast.24), custom_call_target="tpu_custom_call" | custom-call | tf_op jit(solution)/shard_map/pack_queries/pallas_call | solution.py:270
  10.3 7.1 %all-to-all-start = ((bf16[2,128,2176]{2,1,0:T(8,128)(2,1)}), bf16[2,128,2176]{2,1,0:T(8,128)(2,1)S(1)}, u32[]{:S(2)}, u32[]{:S(2)}) async-start(bf16[2,128,2176]{2,1,0:T(8,128)(2,1)} %pack_queries.1), calls=%async_computation | async-start | bytes 2228224 | tf_op jit(solution)/shard_map/all_to_all | solution.py:280
  17.3 1.8 %all-to-all-done = bf16[2,128,2176]{2,1,0:T(8,128)(2,1)S(1)} async-done(((bf16[2,128,2176]{2,1,0:T(8,128)(2,1)}), bf16[2,128,2176]{2,1,0:T(8,128)(2,1)S(1)}, u32[]{:S(2)}, u32[]{:S(2)}) %all-to-all-start) | async-done | bytes 1114144 | tf_op jit(solution)/shard_map/all_to_all | solution.py:280
  19.1 0.7 collective-permute-start.3
  19.8 0.5 broadcast.7
  20.3 0.9 reduce.6
  21.3 1.0 reduce.7
  22.3 0.6 pad_maximum_fusion.parts
  23.0 2.2 %all-gather = bf16[288,1024]{1,0:T(8,128)(2,1)S(1)} all-gather(bf16[144,1024]{1,0:T(8,128)(2,1)S(1)} %copy-done.2), channel_id=2, replica_groups=mesh['task'=8,'yh'=4,'z'=8,'core'=2] {'core'}, dimensions={0}, use_global_device_ids=true | all-gather | bytes 884736 | tf_op jit(solution)/shard_map/all_gather | solution.py:320
  25.2 1.3 %collective-permute-start.5 = (bf16[144,1024]{1,0:T(8,128)(2,1)S(1)}, bf16[144,1024]{1,0:T(8,128)(2,1)S(1)}, u32[]{:S(2)}, u32[]{:S(2)}) collective-permute-start(bf16[144,1024]{1,0:T(8,128)(2,1)S(1)} %collective-permute-done.1), channel_id=1, source_target_pairs={{4,0},{5,1},{20,16},{21,17},{36,32},{37,33},{52,48},{53,49},{68,64... | collective-permute-start | bytes 884744 | tf_op jit(solution)/shard_map/ppermute | solution.py:308
  26.5 1.3 %collective-permute-start.2 = (bf16[144,1024]{1,0:T(8,128)(2,1)S(1)}, bf16[144,1024]{1,0:T(8,128)(2,1)S(1)}, u32[]{:S(2)}, u32[]{:S(2)}) collective-permute-start(bf16[144,1024]{1,0:T(8,128)(2,1)S(1)} %collective-permute-done.1), channel_id=1, source_target_pairs={{2,0},{3,1},{18,16},{19,17},{34,32},{35,33},{50,48},{51,49},{66,64... | collective-permute-start | bytes 884744 | tf_op jit(solution)/shard_map/ppermute | solution.py:308
  27.8 4.6 %collective-permute-start.4 = (bf16[144,1024]{1,0:T(8,128)(2,1)S(1)}, bf16[144,1024]{1,0:T(8,128)(2,1)S(1)}, u32[]{:S(2)}, u32[]{:S(2)}) collective-permute-start(bf16[144,1024]{1,0:T(8,128)(2,1)S(1)} %broadcast_select_fusion), channel_id=1, source_target_pairs={{0,2},{1,3},{16,18},{17,19},{32,34},{33,35},{48,50},{49,51},{2,4},... | collective-permute-start | bytes 884744 | tf_op jit(solution)/shard_map/ppermute | solution.py:308
  32.5 2.5 %all-gather.2 = bf16[288,1024]{1,0:T(8,128)(2,1)S(1)} all-gather(bf16[144,1024]{1,0:T(8,128)(2,1)S(1)} %broadcast_select_fusion), channel_id=4, replica_groups=mesh['task'=8,'yh'=4,'z'=8,'core'=2] {'core'}, dimensions={0}, use_global_device_ids=true | all-gather | bytes 884736 | tf_op jit(solution)/shard_map/all_gather | solution.py:331
  35.0 4.9 %collective-permute-done.5 = bf16[144,1024]{1,0:T(8,128)(2,1)S(1)} collective-permute-done((bf16[144,1024]{1,0:T(8,128)(2,1)S(1)}, bf16[144,1024]{1,0:T(8,128)(2,1)S(1)}, u32[]{:S(2)}, u32[]{:S(2)}) %collective-permute-start.5) | collective-permute-done | bytes 294944 | tf_op jit(solution)/shard_map/ppermute | solution.py:308
  39.9 0.0 copy-start.1
  39.9 2.9 %all-gather.3 = bf16[288,1024]{1,0:T(8,128)(2,1)S(1)} all-gather(bf16[144,1024]{1,0:T(8,128)(2,1)S(1)} %broadcast_select_fusion.1), channel_id=5, replica_groups=mesh['task'=8,'yh'=4,'z'=8,'core'=2] {'core'}, dimensions={0}, use_global_device_ids=true | all-gather | bytes 884736 | tf_op jit(solution)/shard_map/all_gather | solution.py:333
  42.9 1.0 collective-permute-done.2
  43.9 2.7 %all-gather.1 = bf16[288,1024]{1,0:T(8,128)(2,1)S(1)} all-gather(bf16[144,1024]{1,0:T(8,128)(2,1)S(1)} %broadcast_select_fusion.2), channel_id=3, replica_groups=mesh['task'=8,'yh'=4,'z'=8,'core'=2] {'core'}, dimensions={0}, use_global_device_ids=true | all-gather | bytes 884736 | tf_op jit(solution)/shard_map/all_gather | solution.py:334
  46.6 10.0 %attend.1 = f32[16,1280]{1,0:T(8,128)S(1)} custom-call(s32[1]{0:T(128)} %bitcast.core_ref, bf16[256,2176]{1,0:T(8,128)(2,1)S(1)} %bitcast.14, bf16[2,144,1024]{2,1,0:T(8,128)(2,1)S(1)} %bitcast.18, bf16[2,144,1024]{2,1,0:T(8,128)(2,1)S(1)} %bitcast.16, bf16[2,144,1024]{2,1,0:T(8,128)(2,1)S(1)} %bitcast.17, bf16[2,144,1024]{2,1,0:T(8,128)(2,1)S(1)} %bitcast.15, ...), custom_call_target="tpu_custom_call" | custom-call | flops 2000000000 | bytes 4000000 | tf_op jit(solution)/shard_map/attend/pallas_call | solution.py:208
  56.7 0.1 reshape.31
  56.8 24.1 %all_to_all.20.got = f32[32,1,640]{2,1,0:T(1,128)} all-to-all(f32[32,1,640]{2,1,0:T(1,128)S(1)} %reshape.31), channel_id=1, replica_groups=mesh['task'=8,'yh'=4,'z'=8,'core'=2] {'yh','z'}, dimensions={0} | all-to-all | bytes 163840 | tf_op jit(solution)/shard_map/all_to_all | solution.py:280
  80.9 1.7 %norm.1 = (f32[1,512]{1,0:T(1,128)}, f32[64,1,128]{2,1,0:T(1,128)}) custom-call(f32[32,1,640]{2,1,0:T(1,128)} %all_to_all.20.got), custom_call_target="tpu_custom_call" | custom-call | tf_op jit(solution)/shard_map/norm/pallas_call | solution.py:270
  82.6 5.8 %all-to-all-start.2 = ((f32[64,1,128]{2,1,0:T(1,128)}), f32[64,1,128]{2,1,0:T(1,128)S(1)}, u32[]{:S(2)}, u32[]{:S(2)}) async-start(f32[64,1,128]{2,1,0:T(1,128)} %get-tuple-element.29), calls=%async_computation.2 | async-start | bytes 65536 | tf_op jit(solution)/shard_map/all_to_all | solution.py:280
  89.0 11.1 %all-to-all-done.2.got = f32[64,1,128]{2,1,0:T(1,128)S(1)} async-done(((f32[64,1,128]{2,1,0:T(1,128)}), f32[64,1,128]{2,1,0:T(1,128)S(1)}, u32[]{:S(2)}, u32[]{:S(2)}) %all-to-all-start.2) | async-done | bytes 32800 | tf_op jit(solution)/shard_map/all_to_all | solution.py:280
  100.1 0.6 copy-done.5
  100.8 1.6 %update.1 = (f32[1,512]{1,0:T(1,128)}, f32[1,512]{1,0:T(1,128)}, f32[1,512]{1,0:T(1,128)}, f32[8,1,512]{2,1,0:T(1,128)}) custom-call(f32[1]{0:T(128)S(6)} %copy.15.damping, f32[64,1,128]{2,1,0:T(1,128)} %copy-done.5, f32[1,512]{1,0:T(1,128)} %get-tuple-element.30.h_all, f32[3,512]{1,0:T(4,128)} %pad_maximum_fusion.parts), custom_call_target="tpu_custom_call" | custom-call | tf_op jit(solution)/shard_map/update/pallas_call | solution.py:270
  102.3 9.1 %all_to_all.21 = f32[8,1,512]{2,1,0:T(1,128)S(1)} all-to-all(f32[8,1,512]{2,1,0:T(1,128)} %get-tuple-element.35), channel_id=1, replica_groups=mesh['task'=8,'yh'=4,'z'=8,'core'=2] {'task'}, dimensions={0} | all-to-all | bytes 32768 | tf_op jit(solution)/shard_map/all_to_all | solution.py:280
  111.5 0.6 broadcast_multiply_fusion
  (21 shorter events, 0.2 us)
Async XLA Ops:
  0.6 19.2 %copy-start = (f32[1,32768]{1,0:T(1,128)S(1)}, f32[1,32768]{1,0:T(1,128)}, u32[]{:S(2)}) copy-start(f32[1,32768]{1,0:T(1,128)} %param.18) | copy-start | bytes 393220
  2.4 16.7 %collective-permute-start = (bf16[144,1024]{1,0:T(8,128)(2,1)}, bf16[144,1024]{1,0:T(8,128)(2,1)S(1)}, u32[]{:S(2)}, u32[]{:S(2)}) collective-permute-start(bf16[144,1024]{1,0:T(8,128)(2,1)} %pack.1), channel_id=1, source_target_pairs={{0,2},{1,3},{16,18},{17,19},{32,34},{33,35},{48,50},{49,51},{2,4},... | collective-permute-start | bytes 884744 | tf_op jit(solution)/shard_map/ppermute | solution.py:308
  7.3 17.9 %collective-permute-start.1 = (bf16[144,1024]{1,0:T(8,128)(2,1)}, bf16[144,1024]{1,0:T(8,128)(2,1)S(1)}, u32[]{:S(2)}, u32[]{:S(2)}) collective-permute-start(bf16[144,1024]{1,0:T(8,128)(2,1)} %pack.1), channel_id=1, source_target_pairs={{14,18},{15,19},{30,34},{31,35},{46,50},{47,51},{12,16},{13,17},{2... | collective-permute-start | bytes 884744 | tf_op jit(solution)/shard_map/ppermute | solution.py:308
  10.3 7.1 %copy-start.3 = (f32[1,32768]{1,0:T(1,128)S(1)}, f32[1,32768]{1,0:T(1,128)}, u32[]{:S(2)}) copy-start(f32[1,32768]{1,0:T(1,128)} %param.20) | copy-start | bytes 393220
  10.3 7.1 %copy-start.4 = (f32[1,32768]{1,0:T(1,128)S(1)}, f32[1,32768]{1,0:T(1,128)}, u32[]{:S(2)}) copy-start(f32[1,32768]{1,0:T(1,128)} %param.19) | copy-start | bytes 393220
  10.3 8.8 %all-to-all-start = ((bf16[2,128,2176]{2,1,0:T(8,128)(2,1)}), bf16[2,128,2176]{2,1,0:T(8,128)(2,1)S(1)}, u32[]{:S(2)}, u32[]{:S(2)}) async-start(bf16[2,128,2176]{2,1,0:T(8,128)(2,1)} %pack_queries.1), calls=%async_computation | async-start | bytes 2228224 | tf_op jit(solution)/shard_map/all_to_all | solution.py:280
  17.3 5.6 %copy-start.2 = (bf16[144,1024]{1,0:T(8,128)(2,1)S(1)}, bf16[144,1024]{1,0:T(8,128)(2,1)}, u32[]{:S(2)}) copy-start(bf16[144,1024]{1,0:T(8,128)(2,1)} %pack.1) | copy-start | bytes 884740
  19.1 8.6 %collective-permute-start.3 = (bf16[144,1024]{1,0:T(8,128)(2,1)S(1)}, bf16[144,1024]{1,0:T(8,128)(2,1)S(1)}, u32[]{:S(2)}, u32[]{:S(2)}) collective-permute-start(bf16[144,1024]{1,0:T(8,128)(2,1)S(1)} %collective-permute-done), channel_id=1, source_target_pairs={{2,4},{3,5},{18,20},{19,21},{34,36},{35,37},{50,52},{51,53},{4,6},... | collective-permute-start | bytes 884744 | tf_op jit(solution)/shard_map/ppermute | solution.py:308
  25.2 14.7 %collective-permute-start.5 = (bf16[144,1024]{1,0:T(8,128)(2,1)S(1)}, bf16[144,1024]{1,0:T(8,128)(2,1)S(1)}, u32[]{:S(2)}, u32[]{:S(2)}) collective-permute-start(bf16[144,1024]{1,0:T(8,128)(2,1)S(1)} %collective-permute-done.1), channel_id=1, source_target_pairs={{4,0},{5,1},{20,16},{21,17},{36,32},{37,33},{52,48},{53,49},{68,64... | collective-permute-start | bytes 884744 | tf_op jit(solution)/shard_map/ppermute | solution.py:308
  26.5 17.4 %collective-permute-start.2 = (bf16[144,1024]{1,0:T(8,128)(2,1)S(1)}, bf16[144,1024]{1,0:T(8,128)(2,1)S(1)}, u32[]{:S(2)}, u32[]{:S(2)}) collective-permute-start(bf16[144,1024]{1,0:T(8,128)(2,1)S(1)} %collective-permute-done.1), channel_id=1, source_target_pairs={{2,0},{3,1},{18,16},{19,17},{34,32},{35,33},{50,48},{51,49},{66,64... | collective-permute-start | bytes 884744 | tf_op jit(solution)/shard_map/ppermute | solution.py:308
  27.8 16.0 %collective-permute-start.4 = (bf16[144,1024]{1,0:T(8,128)(2,1)S(1)}, bf16[144,1024]{1,0:T(8,128)(2,1)S(1)}, u32[]{:S(2)}, u32[]{:S(2)}) collective-permute-start(bf16[144,1024]{1,0:T(8,128)(2,1)S(1)} %broadcast_select_fusion), channel_id=1, source_target_pairs={{0,2},{1,3},{16,18},{17,19},{32,34},{33,35},{48,50},{49,51},{2,4},... | collective-permute-start | bytes 884744 | tf_op jit(solution)/shard_map/ppermute | solution.py:308
  39.9 6.7 %copy-start.1 = (bf16[1,16,2048]{2,1,0:T(8,128)(2,1)S(1)}, bf16[1,16,2048]{2,1,0:T(8,128)(2,1)}, u32[]{:S(2)}) copy-start(bf16[1,16,2048]{2,1,0:T(8,128)(2,1)} %param.13) | copy-start | bytes 196612
  82.6 17.6 %all-to-all-start.2 = ((f32[64,1,128]{2,1,0:T(1,128)}), f32[64,1,128]{2,1,0:T(1,128)S(1)}, u32[]{:S(2)}, u32[]{:S(2)}) async-start(f32[64,1,128]{2,1,0:T(1,128)} %get-tuple-element.29), calls=%async_computation.2 | async-start | bytes 65536 | tf_op jit(solution)/shard_map/all_to_all | solution.py:280
  100.1 0.6 copy-start.5

commit v9 on v8

--- a/solution.py
+++ b/solution.py
@@ -57,47 +57,61 @@
         out[core, :, 2 * HALF :] = a
 
 
-def attend_kernel(
-    core_ref, qg, far, c1, c2, c3, up, dmat, rmat, out, c0, sem, keys, keys_t, vals, qs, ts, at, qaug, s_ref, t_ref, u_ref, c_ref
-):
-    chunks = (c0, c1, c2, c3)
+def mine(ref, core):
+    parts = [ref[:, pl.ds(pl.multiple_of((g * 2 + core) * GFEAT, GFEAT), GFEAT)] for g in range(GROUPS)]
+    return jnp.concatenate(parts, axis=1)
+
+
+def place_keys(c, at_row, core, keys, keys_t, vals):
+    lane = lax.broadcasted_iota(jnp.int32, (BLOCK, BLOCK), 1).astype(F32)
+    hits = []
+    for half in range(2):
+        rows = slice(at_row + half * BLOCK, at_row + (half + 1) * BLOCK)
+        seg_row = c[half, BLOCK:, :BLOCK].astype(F32)[0:1]
+        hit = jnp.transpose(jnp.broadcast_to(seg_row, (BLOCK, BLOCK))) == lane
+        hits.append(hit)
+        for g in range(GROUPS):
+            col = pl.multiple_of((g * 2 + core) * HEAD_DIM, HEAD_DIM)
+            k = c[half, :BLOCK, pl.ds(col, HEAD_DIM)]
+            keys[g, rows, :HEAD_DIM] = k
+            keys[g, rows, HEAD_DIM:] = jnp.where(hit, 1.0, 0.0).astype(BF16)
+            keys_t[g, :, rows] = jnp.transpose(k.astype(F32)).astype(BF16)
+            vals[g, rows, :] = c[half, :BLOCK, pl.ds(2 * KHALF + col, HEAD_DIM)]
+    return hits
+
+
+def prepare_kernel(core_ref, qg, c1, c2, c3, up, dmat, qs, ts, at, qaug, keys, keys_t, vals):
     core = core_ref[0]
-    copy = pltpu.make_async_copy(far, c0, sem)
-    copy.start()
-
-    def mine(ref):
-        parts = [ref[:, pl.ds(pl.multiple_of((g * 2 + core) * GFEAT, GFEAT), GFEAT)] for g in range(GROUPS)]
-        return jnp.concatenate(parts, axis=1)
-
     a_pad = qg[:, 2 * HALF : 2 * HALF + 128]
     a = a_pad[:, :RANK]
-    qs[...] = (qg[:, :HALF].astype(F32) + dot(a, mine(up))).astype(BF16)
-    d, r = mine(dmat), mine(rmat)
+    qs[...] = (qg[:, :HALF].astype(F32) + dot(a, mine(up, core))).astype(BF16)
+    d = mine(dmat, core)
     d1 = d.astype(BF16)
     rest = d - d1.astype(F32)
     d2 = rest.astype(BF16)
     d3 = (rest - d2.astype(F32)).astype(BF16)
     ts[...] = (dot(a, d1) + dot(a, d2) + dot(a, d3)).astype(BF16)
     at[...] = jnp.transpose(a_pad.astype(F32))[:RANK].astype(BF16)
-    lane = lax.broadcasted_iota(jnp.int32, (BLOCK, BLOCK), 1).astype(F32)
-    for j in (3, 2, 1, 0):
-        c = chunks[j]
-        if j == 0:
-            copy.wait()
-        for half in range(2):
-            rows = slice((j * 2 + half) * BLOCK, (j * 2 + half + 1) * BLOCK)
-            seg_row = c[half, BLOCK:, :BLOCK].astype(F32)[0:1]
-            seg = jnp.transpose(jnp.broadcast_to(seg_row, (BLOCK, BLOCK)))
-            hit = seg == lane
-            for g in range(GROUPS):
-                col = pl.multiple_of((g * 2 + core) * HEAD_DIM, HEAD_DIM)
-                k = c[half, :BLOCK, pl.ds(col, HEAD_DIM)]
-                keys[g, rows, :HEAD_DIM] = k
-                keys[g, rows, HEAD_DIM:] = jnp.where(hit, 1.0, 0.0).astype(BF16)
-                keys_t[g, :, rows] = jnp.transpose(k.astype(F32)).astype(BF16)
-                vals[g, rows, :] = c[half, :BLOCK, pl.ds(2 * KHALF + col, HEAD_DIM)]
-            if j == 3:
-                qaug[half] = jnp.where(hit, 0.0, -1e30).astype(BF16)
+    for j, c in enumerate((c1, c2, c3)):
+        hits = place_keys(c, j * CHUNK, core, keys, keys_t, vals)
+    for half in range(2):
+        qaug[half] = jnp.where(hits[half], 0.0, -1e30).astype(BF16)
+
+
+def attend_kernel(
+    core_ref, qg, far, qs, ts, at, qaug, near, near_t, near_vals, dmat, rmat,
+    out, c0, sem, keys, keys_t, vals, s_ref, t_ref, u_ref, c_ref,
+):
+    core = core_ref[0]
+    copy = pltpu.make_async_copy(far, c0, sem)
+    copy.start()
+    d, r = mine(dmat, core), mine(rmat, core)
+    for g in range(GROUPS):
+        keys[g, CHUNK:, :] = near[g]
+        keys_t[g, :, CHUNK:] = near_t[g]
+        vals[g, CHUNK:, :] = near_vals[g]
+    copy.wait()
+    place_keys(c0, 0, core, keys, keys_t, vals)
     tri = jnp.where(lax.broadcasted_iota(jnp.int32, (BLOCK, BLOCK), 0) <= lax.broadcasted_iota(jnp.int32, (BLOCK, BLOCK), 1), 0.0, -1e30)
     cexp = HEAD_DIM**-0.5 * math.log2(math.e)
     steps = [(g, b, pair) for g in range(GROUPS) for b in range(2) for pair in range(2)]
@@ -203,32 +217,44 @@
         out[:, g * ROW + GFEAT : (g + 1) * ROW] = tail
 
 
-def attend(core, qg, chunks, up, dmat, rmat):
+def prepare(core, qg, chunks, up, dmat):
+    vm = pltpu.VMEM
+    shapes = [
+        (CHUNK, HALF), (CHUNK, HALF), (RANK, CHUNK), (2, BLOCK, BLOCK),
+        (GROUPS, SPAN * CHUNK, 2 * HEAD_DIM), (GROUPS, HEAD_DIM, SPAN * CHUNK), (GROUPS, SPAN * CHUNK, HEAD_DIM),
+    ]
+    return pl.pallas_call(
+        prepare_kernel,
+        out_shape=[jax.ShapeDtypeStruct(shape, BF16) for shape in shapes],
+        in_specs=[pl.BlockSpec(memory_space=pltpu.SMEM)] + [pl.BlockSpec(memory_space=vm)] * 6,
+        out_specs=[pl.BlockSpec(memory_space=vm)] * len(shapes),
+        compiler_params=pltpu.CompilerParams(vmem_limit_bytes=24 * 1024 * 1024),
+        name="prepare",
+    )(core, qg, *chunks, up, dmat)
+
+
+def attend(core, qg, far, ready, dmat, rmat):
     vm = pltpu.VMEM
     return pl.pallas_call(
         attend_kernel,
         out_shape=jax.ShapeDtypeStruct((RANK, GROUPS * ROW), F32),
-        in_specs=[pl.BlockSpec(memory_space=x) for x in (pltpu.SMEM, vm, pl.ANY, vm, vm, vm, vm, vm, vm)],
+        in_specs=[pl.BlockSpec(memory_space=x) for x in (pltpu.SMEM, vm, pl.ANY) + (vm,) * 9],
         out_specs=pl.BlockSpec(memory_space=vm),
         scratch_shapes=[
             vm((2, BLOCK + SEG_ROWS, 4 * KHALF), BF16),
             pltpu.SemaphoreType.DMA,
-            vm((GROUPS, 4 * CHUNK, 2 * HEAD_DIM), BF16),
-            vm((GROUPS, HEAD_DIM, 4 * CHUNK), BF16),
-            vm((GROUPS, 4 * CHUNK, HEAD_DIM), BF16),
-            vm((CHUNK, HALF), BF16),
-            vm((CHUNK, HALF), BF16),
-            vm((RANK, CHUNK), BF16),
-            vm((2, BLOCK, BLOCK), BF16),
+            vm((GROUPS, KEYS, 2 * HEAD_DIM), BF16),
+            vm((GROUPS, HEAD_DIM, KEYS), BF16),
+            vm((GROUPS, KEYS, HEAD_DIM), BF16),
             vm((3, KEYS, CHUNK), F32),
             vm((3, KEYS, CHUNK), F32),
             vm((3, KEYS, CHUNK), F32),
             vm((3, KEYS, CHUNK), BF16),
         ],
-        compiler_params=pltpu.CompilerParams(vmem_limit_bytes=48 * 1024 * 1024),
+        compiler_params=pltpu.CompilerParams(vmem_limit_bytes=40 * 1024 * 1024),
         cost_estimate=pl.CostEstimate(flops=2_000_000_000, bytes_accessed=4_000_000, transcendentals=2_000_000),
         name="attend",
-    )(core, qg, *chunks, up, dmat, rmat)
+    )(core, qg, far, *ready, dmat, rmat)
 
 
 def norm_kernel(got, h_out, out):
@@ -331,9 +357,11 @@
     second = lax.all_gather(second, "core")
     second, far, first = lax.optimization_barrier((second, far, first))
     first = lax.all_gather(jnp.where(z == 0, far, first), "core")
-    chunks = [lax.all_gather(jnp.where(z == 0, back, third), "core"), second, first, own]
-
-    terms = attend(core.reshape(1), qg, chunks, up, dmat, rmat)
+    ready = prepare(core.reshape(1), qg, (second, first, own), up, dmat)
+    back, third, *ready = lax.optimization_barrier((back, third, *ready))
+    late = lax.all_gather(jnp.where(z == 0, back, third), "core")
+
+    terms = attend(core.reshape(1), qg, late, ready, dmat, rmat)
 
     peers = n_yh * n_z
     h, scalars = in_vmem(

time: 113 us -> 112 us (level)
  transfers between devices with their start and end apart: 8 -> 8, of which waited for: 4 -> 4; matrix products, arithmetic and copies ran while one was open for 3% -> 3% of each run, Pallas kernels for 2% -> 3%
where the time goes in v9:
time: 112 us; the launch traced here: 111 us
  blocking collectives  43.6 us (39%)
  starting transfers between devices  26.3 us (23%)
  waiting for transfers between devices  18 us (16%)
  Pallas kernels  17.5 us (16%)
  other arithmetic  3.21 us (3%)
  between operations  1.47 us (1%)
  local copies, waits for them, and re-layouts  1.29 us (1%)
    all_to_all x2, blocking collectives, exchange(): return lax.all_to_all(x, axes, 0, 0, tiled=True)  33.4 us
    ppermute x6, starting transfers between devices, move(): return lax.ppermute(x, CTX, moves(n_yh, n_z, kinds))  13.5 us
    all_to_all x2, waiting for transfers between devices, exchange(): return lax.all_to_all(x, axes, 0, 0, tiled=True)  12.9 us
    all_to_all x2, starting transfers between devices, exchange(): return lax.all_to_all(x, axes, 0, 0, tiled=True)  12.8 us
    pallas_call x1, Pallas kernels, attend(): pl.pallas_call(attend_kernel, out_shape=jax.ShapeDtypeStruct((RANK, GROUP...  9.37 us
    pallas_call x4, Pallas kernels, in_vmem(): pl.pallas_call(kernel, out_shape=[jax.ShapeDtypeStruct(s, dtype) for s in...  7.34 us
    ppermute x6, waiting for transfers between devices, move(): return lax.ppermute(x, CTX, moves(n_yh, n_z, kinds))  5.11 us
    all_gather x1, blocking collectives, per_device(): first = lax.all_gather(jnp.where(z == 0, far, first), 'core')  2.8 us
  transfers between devices with their start and end apart: 8, of which 4 were waited for; matrix products, arithmetic and copies ran while one was open for 3% of the time, Pallas kernels for 3%

profile of v9, /device:TPU:1, one launch (start us, length us, event | category | flops | bytes accessed | tf_op | source)
XLA Modules:
  0.0 111.4 jit_solution(1703262465216387084)
XLA Ops:
  0.6 0.0 copy-start
  0.6 1.8 %pack.1 = bf16[144,1024]{1,0:T(8,128)(2,1)} custom-call(bf16[128,512]{1,0:T(8,128)(2,1)} %bitcast.23, bf16[128,512]{1,0:T(8,128)(2,1)} %bitcast.24, s32[1,128]{1,0:T(1,128)} %seg.1), custom_call_target="tpu_custom_call" | custom-call | tf_op jit(solution)/shard_map/pack/pallas_call | solution.py:296
  2.4 4.8 %collective-permute-start = (bf16[144,1024]{1,0:T(8,128)(2,1)}, bf16[144,1024]{1,0:T(8,128)(2,1)S(1)}, u32[]{:S(2)}, u32[]{:S(2)}) collective-permute-start(bf16[144,1024]{1,0:T(8,128)(2,1)} %pack.1), channel_id=1, source_target_pairs={{0,2},{1,3},{16,18},{17,19},{32,34},{33,35},{48,50},{49,51},{2,4},... | collective-permute-start | bytes 884744 | tf_op jit(solution)/shard_map/ppermute | solution.py:334
  7.2 0.7 collective-permute-start.1
  7.9 2.3 %pack_queries.1 = bf16[2,128,2176]{2,1,0:T(8,128)(2,1)} custom-call(bf16[128,2048]{1,0:T(8,128)(2,1)} %bitcast.21, bf16[128,2048]{1,0:T(8,128)(2,1)} %bitcast.22, bf16[16,128]{1,0:T(8,128)(2,1)} %bitcast.25), custom_call_target="tpu_custom_call" | custom-call | tf_op jit(solution)/shard_map/pack_queries/pallas_call | solution.py:296
  10.3 7.1 %all-to-all-start = ((bf16[2,128,2176]{2,1,0:T(8,128)(2,1)}), bf16[2,128,2176]{2,1,0:T(8,128)(2,1)S(1)}, u32[]{:S(2)}, u32[]{:S(2)}) async-start(bf16[2,128,2176]{2,1,0:T(8,128)(2,1)} %pack_queries.1), calls=%async_computation | async-start | bytes 2228224 | tf_op jit(solution)/shard_map/all_to_all | solution.py:306
  17.3 1.8 %all-to-all-done = bf16[2,128,2176]{2,1,0:T(8,128)(2,1)S(1)} async-done(((bf16[2,128,2176]{2,1,0:T(8,128)(2,1)}), bf16[2,128,2176]{2,1,0:T(8,128)(2,1)S(1)}, u32[]{:S(2)}, u32[]{:S(2)}) %all-to-all-start) | async-done | bytes 1114144 | tf_op jit(solution)/shard_map/all_to_all | solution.py:306
  19.1 0.7 collective-permute-start.3
  19.8 0.5 broadcast.7
  20.3 0.9 reduce.6
  21.3 1.0 reduce.7
  22.3 0.6 pad_maximum_fusion.parts
  22.9 2.2 %all-gather = bf16[288,1024]{1,0:T(8,128)(2,1)S(1)} all-gather(bf16[144,1024]{1,0:T(8,128)(2,1)S(1)} %copy-done.2), channel_id=2, replica_groups=mesh['task'=8,'yh'=4,'z'=8,'core'=2] {'core'}, dimensions={0}, use_global_device_ids=true | all-gather | bytes 884736 | tf_op jit(solution)/shard_map/all_gather | solution.py:346
  25.1 1.3 %collective-permute-start.5 = (bf16[144,1024]{1,0:T(8,128)(2,1)S(1)}, bf16[144,1024]{1,0:T(8,128)(2,1)S(1)}, u32[]{:S(2)}, u32[]{:S(2)}) collective-permute-start(bf16[144,1024]{1,0:T(8,128)(2,1)S(1)} %collective-permute-done.1), channel_id=1, source_target_pairs={{4,0},{5,1},{20,16},{21,17},{36,32},{37,33},{52,48},{53,49},{68,64... | collective-permute-start | bytes 884744 | tf_op jit(solution)/shard_map/ppermute | solution.py:334
  26.4 1.3 %collective-permute-start.2 = (bf16[144,1024]{1,0:T(8,128)(2,1)S(1)}, bf16[144,1024]{1,0:T(8,128)(2,1)S(1)}, u32[]{:S(2)}, u32[]{:S(2)}) collective-permute-start(bf16[144,1024]{1,0:T(8,128)(2,1)S(1)} %collective-permute-done.1), channel_id=1, source_target_pairs={{2,0},{3,1},{18,16},{19,17},{34,32},{35,33},{50,48},{51,49},{66,64... | collective-permute-start | bytes 884744 | tf_op jit(solution)/shard_map/ppermute | solution.py:334
  27.8 4.8 %collective-permute-start.4 = (bf16[144,1024]{1,0:T(8,128)(2,1)S(1)}, bf16[144,1024]{1,0:T(8,128)(2,1)S(1)}, u32[]{:S(2)}, u32[]{:S(2)}) collective-permute-start(bf16[144,1024]{1,0:T(8,128)(2,1)S(1)} %broadcast_select_fusion), channel_id=1, source_target_pairs={{0,2},{1,3},{16,18},{17,19},{32,34},{33,35},{48,50},{49,51},{2,4},... | collective-permute-start | bytes 884744 | tf_op jit(solution)/shard_map/ppermute | solution.py:334
  32.6 2.5 %all-gather.1 = bf16[288,1024]{1,0:T(8,128)(2,1)S(1)} all-gather(bf16[144,1024]{1,0:T(8,128)(2,1)S(1)} %broadcast_select_fusion), channel_id=3, replica_groups=mesh['task'=8,'yh'=4,'z'=8,'core'=2] {'core'}, dimensions={0}, use_global_device_ids=true | all-gather | bytes 884736 | tf_op jit(solution)/shard_map/all_gather | solution.py:357
  35.1 4.8 %collective-permute-done.5 = bf16[144,1024]{1,0:T(8,128)(2,1)S(1)} collective-permute-done((bf16[144,1024]{1,0:T(8,128)(2,1)S(1)}, bf16[144,1024]{1,0:T(8,128)(2,1)S(1)}, u32[]{:S(2)}, u32[]{:S(2)}) %collective-permute-start.5) | collective-permute-done | bytes 294944 | tf_op jit(solution)/shard_map/ppermute | solution.py:334
  39.9 2.8 %all-gather.2 = bf16[288,1024]{1,0:T(8,128)(2,1)S(1)} all-gather(bf16[144,1024]{1,0:T(8,128)(2,1)S(1)} %broadcast_select_fusion.2), channel_id=4, replica_groups=mesh['task'=8,'yh'=4,'z'=8,'core'=2] {'core'}, dimensions={0}, use_global_device_ids=true | all-gather | bytes 884736 | tf_op jit(solution)/shard_map/all_gather | solution.py:359
  42.7 0.8 prepare.1
  43.5 0.3 collective-permute-done.2
  43.8 2.7 %all-gather.3 = bf16[288,1024]{1,0:T(8,128)(2,1)S(1)} all-gather(bf16[144,1024]{1,0:T(8,128)(2,1)S(1)} %broadcast_select_fusion.1), channel_id=5, replica_groups=mesh['task'=8,'yh'=4,'z'=8,'core'=2] {'core'}, dimensions={0}, use_global_device_ids=true | all-gather | bytes 884736 | tf_op jit(solution)/shard_map/all_gather | solution.py:362
  46.6 9.4 %attend.1 = f32[16,1280]{1,0:T(8,128)S(1)} custom-call(s32[1]{0:T(128)} %bitcast.core_ref, bf16[256,2176]{1,0:T(8,128)(2,1)S(1)} %bitcast.15, bf16[2,144,1024]{2,1,0:T(8,128)(2,1)S(1)} %bitcast.19, bf16[256,1024]{1,0:T(8,128)(2,1)S(1)} %get-tuple-element.53.qs, bf16[256,1024]{1,0:T(8,128)(2,1)S(1)} %get-tuple-element.54.ts, ...), custom_call_target="tpu_custom_call" | custom-call | flops 2000000000 | bytes 4000000 | tf_op jit(solution)/shard_map/attend/pallas_call | solution.py:238
  56.0 0.1 reshape.32
  56.0 24.3 %all_to_all.20.got = f32[32,1,640]{2,1,0:T(1,128)} all-to-all(f32[32,1,640]{2,1,0:T(1,128)S(1)} %reshape.32), channel_id=1, replica_groups=mesh['task'=8,'yh'=4,'z'=8,'core'=2] {'yh','z'}, dimensions={0} | all-to-all | bytes 163840 | tf_op jit(solution)/shard_map/all_to_all | solution.py:306
  80.3 1.7 %norm.1 = (f32[1,512]{1,0:T(1,128)}, f32[64,1,128]{2,1,0:T(1,128)}) custom-call(f32[32,1,640]{2,1,0:T(1,128)} %all_to_all.20.got), custom_call_target="tpu_custom_call" | custom-call | tf_op jit(solution)/shard_map/norm/pallas_call | solution.py:296
  82.0 5.8 %all-to-all-start.2 = ((f32[64,1,128]{2,1,0:T(1,128)}), f32[64,1,128]{2,1,0:T(1,128)S(1)}, u32[]{:S(2)}, u32[]{:S(2)}) async-start(f32[64,1,128]{2,1,0:T(1,128)} %get-tuple-element.61), calls=%async_computation.2 | async-start | bytes 65536 | tf_op jit(solution)/shard_map/all_to_all | solution.py:306
  88.4 11.1 %all-to-all-done.2.got = f32[64,1,128]{2,1,0:T(1,128)S(1)} async-done(((f32[64,1,128]{2,1,0:T(1,128)}), f32[64,1,128]{2,1,0:T(1,128)S(1)}, u32[]{:S(2)}, u32[]{:S(2)}) %all-to-all-start.2) | async-done | bytes 32800 | tf_op jit(solution)/shard_map/all_to_all | solution.py:306
  99.6 0.6 copy-done.5
  100.2 1.6 %update.1 = (f32[1,512]{1,0:T(1,128)}, f32[1,512]{1,0:T(1,128)}, f32[1,512]{1,0:T(1,128)}, f32[8,1,512]{2,1,0:T(1,128)}) custom-call(f32[1]{0:T(128)S(6)} %copy.15.damping, f32[64,1,128]{2,1,0:T(1,128)} %copy-done.5, f32[1,512]{1,0:T(1,128)} %get-tuple-element.62.h_all, f32[3,512]{1,0:T(4,128)} %pad_maximum_fusion.parts), custom_call_target="tpu_custom_call" | custom-call | tf_op jit(solution)/shard_map/update/pallas_call | solution.py:296
  101.8 9.1 %all_to_all.21 = f32[8,1,512]{2,1,0:T(1,128)S(1)} all-to-all(f32[8,1,512]{2,1,0:T(1,128)} %get-tuple-element.67), channel_id=1, replica_groups=mesh['task'=8,'yh'=4,'z'=8,'core'=2] {'task'}, dimensions={0} | all-to-all | bytes 32768 | tf_op jit(solution)/shard_map/all_to_all | solution.py:306
  110.9 0.6 broadcast_multiply_fusion
  (22 shorter events, 0.2 us)
Async XLA Ops:
  0.6 19.2 %copy-start = (f32[1,32768]{1,0:T(1,128)S(1)}, f32[1,32768]{1,0:T(1,128)}, u32[]{:S(2)}) copy-start(f32[1,32768]{1,0:T(1,128)} %param.18) | copy-start | bytes 393220
  2.4 16.7 %collective-permute-start = (bf16[144,1024]{1,0:T(8,128)(2,1)}, bf16[144,1024]{1,0:T(8,128)(2,1)S(1)}, u32[]{:S(2)}, u32[]{:S(2)}) collective-permute-start(bf16[144,1024]{1,0:T(8,128)(2,1)} %pack.1), channel_id=1, source_target_pairs={{0,2},{1,3},{16,18},{17,19},{32,34},{33,35},{48,50},{49,51},{2,4},... | collective-permute-start | bytes 884744 | tf_op jit(solution)/shard_map/ppermute | solution.py:334
  7.2 17.9 %collective-permute-start.1 = (bf16[144,1024]{1,0:T(8,128)(2,1)}, bf16[144,1024]{1,0:T(8,128)(2,1)S(1)}, u32[]{:S(2)}, u32[]{:S(2)}) collective-permute-start(bf16[144,1024]{1,0:T(8,128)(2,1)} %pack.1), channel_id=1, source_target_pairs={{14,18},{15,19},{30,34},{31,35},{46,50},{47,51},{12,16},{13,17},{2... | collective-permute-start | bytes 884744 | tf_op jit(solution)/shard_map/ppermute | solution.py:334
  10.2 7.1 %copy-start.3 = (f32[1,32768]{1,0:T(1,128)S(1)}, f32[1,32768]{1,0:T(1,128)}, u32[]{:S(2)}) copy-start(f32[1,32768]{1,0:T(1,128)} %param.20) | copy-start | bytes 393220
  10.3 7.1 %copy-start.4 = (f32[1,32768]{1,0:T(1,128)S(1)}, f32[1,32768]{1,0:T(1,128)}, u32[]{:S(2)}) copy-start(f32[1,32768]{1,0:T(1,128)} %param.19) | copy-start | bytes 393220
  10.3 8.8 %all-to-all-start = ((bf16[2,128,2176]{2,1,0:T(8,128)(2,1)}), bf16[2,128,2176]{2,1,0:T(8,128)(2,1)S(1)}, u32[]{:S(2)}, u32[]{:S(2)}) async-start(bf16[2,128,2176]{2,1,0:T(8,128)(2,1)} %pack_queries.1), calls=%async_computation | async-start | bytes 2228224 | tf_op jit(solution)/shard_map/all_to_all | solution.py:306
  17.3 5.6 %copy-start.2 = (bf16[144,1024]{1,0:T(8,128)(2,1)S(1)}, bf16[144,1024]{1,0:T(8,128)(2,1)}, u32[]{:S(2)}) copy-start(bf16[144,1024]{1,0:T(8,128)(2,1)} %pack.1) | copy-start | bytes 884740
  19.1 8.6 %collective-permute-start.3 = (bf16[144,1024]{1,0:T(8,128)(2,1)S(1)}, bf16[144,1024]{1,0:T(8,128)(2,1)S(1)}, u32[]{:S(2)}, u32[]{:S(2)}) collective-permute-start(bf16[144,1024]{1,0:T(8,128)(2,1)S(1)} %collective-permute-done), channel_id=1, source_target_pairs={{2,4},{3,5},{18,20},{19,21},{34,36},{35,37},{50,52},{51,53},{4,6},... | collective-permute-start | bytes 884744 | tf_op jit(solution)/shard_map/ppermute | solution.py:334
  25.1 14.7 %collective-permute-start.5 = (bf16[144,1024]{1,0:T(8,128)(2,1)S(1)}, bf16[144,1024]{1,0:T(8,128)(2,1)S(1)}, u32[]{:S(2)}, u32[]{:S(2)}) collective-permute-start(bf16[144,1024]{1,0:T(8,128)(2,1)S(1)} %collective-permute-done.1), channel_id=1, source_target_pairs={{4,0},{5,1},{20,16},{21,17},{36,32},{37,33},{52,48},{53,49},{68,64... | collective-permute-start | bytes 884744 | tf_op jit(solution)/shard_map/ppermute | solution.py:334
  26.4 17.4 %collective-permute-start.2 = (bf16[144,1024]{1,0:T(8,128)(2,1)S(1)}, bf16[144,1024]{1,0:T(8,128)(2,1)S(1)}, u32[]{:S(2)}, u32[]{:S(2)}) collective-permute-start(bf16[144,1024]{1,0:T(8,128)(2,1)S(1)} %collective-permute-done.1), channel_id=1, source_target_pairs={{2,0},{3,1},{18,16},{19,17},{34,32},{35,33},{50,48},{51,49},{66,64... | collective-permute-start | bytes 884744 | tf_op jit(solution)/shard_map/ppermute | solution.py:334
  27.8 14.9 %copy-start.1 = (bf16[1,16,2048]{2,1,0:T(8,128)(2,1)S(1)}, bf16[1,16,2048]{2,1,0:T(8,128)(2,1)}, u32[]{:S(2)}) copy-start(bf16[1,16,2048]{2,1,0:T(8,128)(2,1)} %param.13) | copy-start | bytes 196612
  27.8 16.0 %collective-permute-start.4 = (bf16[144,1024]{1,0:T(8,128)(2,1)S(1)}, bf16[144,1024]{1,0:T(8,128)(2,1)S(1)}, u32[]{:S(2)}, u32[]{:S(2)}) collective-permute-start(bf16[144,1024]{1,0:T(8,128)(2,1)S(1)} %broadcast_select_fusion), channel_id=1, source_target_pairs={{0,2},{1,3},{16,18},{17,19},{32,34},{33,35},{48,50},{49,51},{2,4},... | collective-permute-start | bytes 884744 | tf_op jit(solution)/shard_map/ppermute | solution.py:334
  82.0 17.6 %all-to-all-start.2 = ((f32[64,1,128]{2,1,0:T(1,128)}), f32[64,1,128]{2,1,0:T(1,128)S(1)}, u32[]{:S(2)}, u32[]{:S(2)}) async-start(f32[64,1,128]{2,1,0:T(1,128)} %get-tuple-element.61), calls=%async_computation.2 | async-start | bytes 65536 | tf_op jit(solution)/shard_map/all_to_all | solution.py:306
  99.6 0.6 copy-start.5
